TPU v7x, 128 devices: a whole 4x4x4 slice. The times are simulated.
128 devices in a mesh: lat: 8 (over z, core), lon: 16 (over x, y).
Axes of the slice: x: 4, y: 4, z: 4, core: 2. Of those that a mesh axis runs over, the one named last changes fastest.
Arguments:
- obs_values: bfloat16 [524288, 128], P(('lat', 'lon')), may hold values from -6 to 6
- obs_dest: int32 [524288, 1], P(('lat', 'lon')), may hold values from 0 to 127; in each aligned block of 4096 rows (0 to 4095, 4096 to 8191, ...) at most 64 rows name the same one
- obs_cell: int32 [524288], P(('lat', 'lon')), may hold values from 0 to 8191
- obs_count: int32 [128], P(('lat', 'lon')), may hold values from 1 to 4096, 458752 in all
- conv_in: bfloat16 [3, 3, 128, 256], replicated, may hold values from -0.1875 to 0.1875
- conv_down: bfloat16 [3, 3, 256, 256], replicated, may hold values from -0.125 to 0.125
Outputs:
- encoded: bfloat16 [128, 2048, 256], P('lat', 'lon')
Inputs may be any that keep to these rules, and one draw needn't show every extreme that they name: `obs_dest`: within the rows of one device, no tile is named by more than 64 rows, and some device's rows name one tile exactly 64 times. `obs_count`: the counts sum to 458752 and the largest is 4096.
All inputs are finite; a program needn't handle non-finite values.
Results may differ from a plain program's by a relative error of at most 0.0052.
Values may be sent and summed in bfloat16 or wider, within the bound.
No kernel may reach another device: no remote copies, remote signals or barrier semaphores. Data moves between devices by JAX's collectives and lax.ppermute only.
A program may use at most 64 MiB of HBM per device.

v0:
```python
import math

import jax
import jax.numpy as jnp
from jax import lax
from jax.sharding import PartitionSpec as P

TH = 32
TW = 256


def extended_2(cells, sides, width, closed):
    for axis, dim in sides:
        count = lax.axis_size(axis)
        ends = count if closed else count - 1
        head = lax.slice_in_dim(cells, 0, width, axis=dim)
        tail = lax.slice_in_dim(cells, cells.shape[dim] - width, cells.shape[dim], axis=dim)
        cells = jnp.concatenate(
            [
                lax.ppermute(tail, axis, [(i, (i + 1) % count) for i in range(ends)]),
                cells,
                lax.ppermute(head, axis, [((i + 1) % count, i) for i in range(ends)]),
            ],
            axis=dim,
        )
    return cells


def shifted(value, axis, steps):
    count = lax.axis_size(axis)
    leading, last = (max(0, -steps), min(count, count - steps))
    return lax.ppermute(value, axis, [(source, source + steps) for source in range(leading, last)])


def passed_along(shard, axis, by):
    peers = lax.axis_size(axis)
    return lax.ppermute(shard, axis, [(i, (i + by) % peers) for i in range(peers)])


def convolve(field, weights, stride):
    return lax.conv_general_dilated(
        field[None],
        weights,
        (stride, stride),
        "VALID",
        dimension_numbers=("NHWC", "HWIO", "NHWC"),
        preferred_element_type=jnp.float32,
    )[0]


def body(obs_values, obs_dest, obs_cell, obs_count, conv_in, conv_down):
    lat_size = lax.axis_size("lat")
    lon_size = lax.axis_size("lon")
    devices = lat_size * lon_size
    obs_rows = obs_values.shape[0]
    channels = obs_values.shape[1]
    capacity = 2 * obs_rows // devices
    row_ids = jnp.arange(obs_rows, dtype=jnp.int32)
    is_valid = row_ids < obs_count[0]
    target = obs_dest[:, 0]
    target_hot = (
        (target[:, None] == jnp.arange(devices, dtype=jnp.int32)[None, :]) & is_valid[:, None]
    ).astype(jnp.int32)
    earlier = jnp.cumsum(target_hot, axis=0) - target_hot
    position = jnp.sum(earlier * target_hot, axis=1)
    live_counts = jnp.sum(target_hot, axis=0)
    slot_ids = jnp.where(is_valid, target * capacity + position, devices * capacity)
    send_values = (
        jnp.zeros((devices * capacity, channels), jnp.bfloat16)
        .at[slot_ids]
        .set(obs_values, mode="drop")
    )
    send_cells = jnp.zeros((devices * capacity,), jnp.int32).at[slot_ids].set(obs_cell, mode="drop")
    got_values, got_cells, got_counts = (
        lax.all_to_all(send_values, ("lat", "lon"), split_axis=0, concat_axis=0, tiled=True),
        lax.all_to_all(send_cells, ("lat", "lon"), split_axis=0, concat_axis=0, tiled=True),
        lax.all_to_all(live_counts, ("lat", "lon"), split_axis=0, concat_axis=0, tiled=True),
    )
    slot_in_source = jnp.arange(devices * capacity, dtype=jnp.int32) % capacity
    source_of_slot = jnp.arange(devices * capacity, dtype=jnp.int32) // capacity
    live_slot = slot_in_source < got_counts[source_of_slot]
    tile_cells = TH * TW
    got_cells = jnp.where(live_slot, got_cells, -1)
    slot_total = got_values.shape[0]
    block_size = math.gcd(slot_total, 1024)
    block_count = slot_total // block_size
    cell_iota = jnp.arange(tile_cells, dtype=jnp.int32)

    def accumulate(running, element):
        block_values, block_cells = element
        one_hot = (block_cells[:, None] == cell_iota[None, :]).astype(jnp.bfloat16)
        added = lax.dot_general(
            one_hot, block_values, (((0,), (0,)), ((), ())), preferred_element_type=jnp.float32
        )
        return (
            (running[0] + added, running[1] + jnp.sum(one_hot, axis=0, dtype=jnp.float32)),
            None,
        )

    start_state = (
        jnp.zeros((tile_cells, channels), jnp.float32),
        jnp.zeros((tile_cells,), jnp.float32),
    )
    (cell_sums, cell_counts), _ = lax.scan(
        accumulate,
        start_state,
        (
            got_values.reshape(block_count, block_size, channels),
            got_cells.reshape(block_count, block_size),
        ),
    )
    gridded = (
        (cell_sums / jnp.maximum(cell_counts, 1.0)[:, None])
        .astype(jnp.bfloat16)
        .reshape(TH, TW, channels)
    )
    extended = extended_2(gridded, (("lat", 0),), 1, False)
    extended = extended_2(extended, (("lon", 1),), 1, True)
    inner = jax.nn.gelu(convolve(extended, conv_in, 1)).astype(jnp.bfloat16)
    upper = shifted(inner[TH - 1 :], "lat", 1)
    hidden = jnp.concatenate([upper, inner], axis=0)
    western = passed_along(hidden[:, TW - 1 :], "lon", 1)
    hidden = jnp.concatenate([western, hidden], axis=1)
    return jax.nn.gelu(convolve(hidden, conv_down, 2)).astype(jnp.bfloat16)


def solution(mesh):
    placed = (
        P(("lat", "lon"), None),
        P(("lat", "lon"), None),
        P(("lat", "lon")),
        P(("lat", "lon")),
        P(),
        P(),
    )
    return jax.shard_map(
        body, mesh=mesh, in_specs=placed, out_specs=P("lat", "lon", None), check_vma=False
    )
```

profile of v0, /device:TPU:1, one launch (start us, length us, event | category | flops | bytes accessed | tf_op | source)
XLA Modules:
  0.0 351.4 jit_solution(1468316071173865489)
XLA Ops:
  0.8 0.8 copy.43
  1.6 1.1 fusion.43
  2.8 0.1 reduce-window.9
  2.8 0.2 broadcast_add_fusion
  3.1 1.2 copy.44
  4.3 2.2 convert_reduce_fusion.1
  6.5 0.7 copy.42
  7.2 11.5 %all-to-all-start = ((s32[128,1,1]{2,1,0:T(1,128)}), s32[128,1,1]{2,1,0:T(1,128)S(1)}, u32[]{:S(2)}, u32[]{:S(2)}) async-start(s32[128,1,1]{2,1,0:T(1,128)} %copy.42), calls=%async_computation | async-start | bytes 131072 | tf_op jit(solution)/shard_map/all_to_all | solution.py:77
  18.8 15.7 %scatter_custom_fusion = s32[8192]{0:T(1024)S(1)} fusion(s32[4096]{0:T(1024)S(1)} %bitcast.76, s32[4096]{0:T(1024)} %param.10, s32[]{:T(128)} %constant.35.clone.1), kind=kCustom, calls=%fused_computation.95 | custom fusion | bytes 33280 | tf_op jit(solution)/shard_map/scatter | solution.py:73
  34.5 0.7 all_to_all.25
  35.2 9.8 %all-to-all-start.1 = ((s32[128,64,1]{1,2,0:T(1,128)}), s32[128,64,1]{1,2,0:T(1,128)S(1)}, u32[]{:S(2)}, u32[]{:S(2)}) async-start(s32[128,64,1]{1,2,0:T(1,128)} %bitcast.10), calls=%async_computation.1 | async-start | bytes 131072 | tf_op jit(solution)/shard_map/all_to_all | solution.py:76
  45.0 12.8 %scatter_custom_fusion.1 = bf16[8192,128]{1,0:T(8,128)(2,1)} fusion(s32[4096]{0:T(1024)S(1)} %bitcast.77, bf16[4096,128]{1,0:T(8,128)(2,1)} %param.8, bf16[]{:T(256)} %constant.41.clone.1), kind=kCustom, calls=%fused_computation.67 | custom fusion | bytes 2097664 | tf_op jit(solution)/shard_map/scatter | solution.py:71
  57.8 9.8 %all-to-all-start.2 = ((bf16[128,64,128]{2,1,0:T(8,128)(2,1)}), bf16[128,64,128]{2,1,0:T(8,128)(2,1)S(1)}, u32[]{:S(2)}, u32[]{:S(2)}) async-start(bf16[128,64,128]{2,1,0:T(8,128)(2,1)} %bitcast.11), calls=%async_computation.2 | async-start | bytes 4194304 | tf_op jit(solution)/shard_map/all_to_all | solution.py:75
  67.6 2.4 reduce
  69.9 48.9 %gather_fusion = s32[8192]{0:T(1024)S(1)} fusion(s32[128]{0:T(128)S(1)} %reduce, s32[8192]{0:T(1024)S(1)} %broadcast_clamp_fusion), kind=kCustom, calls=%fused_computation | custom fusion | bytes 98304 | tf_op jit(solution)/shard_map/gather | solution.py:81
  118.8 0.5 broadcast.171
  119.4 0.7 reduce.4
  120.1 0.1 all_to_all.27
  120.2 170.4 %while.13 = (s32[]{:T(128)}, f32[8192,128]{1,0:T(8,128)}, f32[8192]{0:T(1024)S(1)}, s32[8,1024]{1,0:T(8,128)S(1)}, bf16[8,1024,128]{2,1,0:T(8,128)(2,1)S(1)}, /*index=5*/s32[]{:T(128)}, s32[]{:T(128)}) while((s32[]{:T(128)}, f32[8192,128]{1,0:T(8,128)}, f32[8192]{0:T(1024)S(1)}, s32[8,1024]{1,0:T(8,128)S(1)}, ...), condition=%wide.region_8.9_spmd.clone, body=%wide.region_6.8_spmd.clone.sunk | while | flops 2191532032 | bytes 8798312 | solution.py:104
  120.5 8.0 %convert_reduce_fusion.3 = f32[8192]{0:T(1024)S(1)} fusion(s32[1024]{0:T(1024)S(1)} %bitcast.73), kind=kLoop, calls=%fused_computation.7.clone.1 | loop fusion | flops 33546240 | bytes 36864 | tf_op jit(solution)/shard_map/while/body/eval_jaxpr/reduce_sum | solution.py:96
  128.5 10.8 %fusion.72 = f32[8192,128]{1,0:T(8,128)} fusion(s32[1024]{0:T(1024)S(1)} %bitcast.74, f32[8192,128]{1,0:T(8,128)} %get-tuple-element.115, pred[]{:T(512)S(6)} %compare.28, bf16[8,1024,128]{2,1,0:T(8,128)(2,1)S(1)} %get-tuple-element.125, s32[]{:T(128)S(6)} %copy.60), kind=kOutput, calls=%fused_computation.9.clone.1 | convolution fusion | flops 2157969408 | bytes 8654853 | tf_op jit(solution)/shard_map/while/body/eval_jaxpr/dot_general | solution.py:92
  139.3 8.0 %convert_reduce_fusion.3 = f32[8192]{0:T(1024)S(1)} fusion(s32[1024]{0:T(1024)S(1)} %bitcast.73), kind=kLoop, calls=%fused_computation.7.clone.1 | loop fusion | flops 33546240 | bytes 36864 | tf_op jit(solution)/shard_map/while/body/eval_jaxpr/reduce_sum | solution.py:96
  147.3 12.4 %fusion.72 = f32[8192,128]{1,0:T(8,128)} fusion(s32[1024]{0:T(1024)S(1)} %bitcast.74, f32[8192,128]{1,0:T(8,128)} %get-tuple-element.115, pred[]{:T(512)S(6)} %compare.28, bf16[8,1024,128]{2,1,0:T(8,128)(2,1)S(1)} %get-tuple-element.125, s32[]{:T(128)S(6)} %copy.60), kind=kOutput, calls=%fused_computation.9.clone.1 | convolution fusion | flops 2157969408 | bytes 8654853 | tf_op jit(solution)/shard_map/while/body/eval_jaxpr/dot_general | solution.py:92
  159.7 8.0 %convert_reduce_fusion.3 = f32[8192]{0:T(1024)S(1)} fusion(s32[1024]{0:T(1024)S(1)} %bitcast.73), kind=kLoop, calls=%fused_computation.7.clone.1 | loop fusion | flops 33546240 | bytes 36864 | tf_op jit(solution)/shard_map/while/body/eval_jaxpr/reduce_sum | solution.py:96
  167.7 12.4 %fusion.72 = f32[8192,128]{1,0:T(8,128)} fusion(s32[1024]{0:T(1024)S(1)} %bitcast.74, f32[8192,128]{1,0:T(8,128)} %get-tuple-element.115, pred[]{:T(512)S(6)} %compare.28, bf16[8,1024,128]{2,1,0:T(8,128)(2,1)S(1)} %get-tuple-element.125, s32[]{:T(128)S(6)} %copy.60), kind=kOutput, calls=%fused_computation.9.clone.1 | convolution fusion | flops 2157969408 | bytes 8654853 | tf_op jit(solution)/shard_map/while/body/eval_jaxpr/dot_general | solution.py:92
  180.0 8.0 %convert_reduce_fusion.3 = f32[8192]{0:T(1024)S(1)} fusion(s32[1024]{0:T(1024)S(1)} %bitcast.73), kind=kLoop, calls=%fused_computation.7.clone.1 | loop fusion | flops 33546240 | bytes 36864 | tf_op jit(solution)/shard_map/while/body/eval_jaxpr/reduce_sum | solution.py:96
  188.0 12.4 %fusion.72 = f32[8192,128]{1,0:T(8,128)} fusion(s32[1024]{0:T(1024)S(1)} %bitcast.74, f32[8192,128]{1,0:T(8,128)} %get-tuple-element.115, pred[]{:T(512)S(6)} %compare.28, bf16[8,1024,128]{2,1,0:T(8,128)(2,1)S(1)} %get-tuple-element.125, s32[]{:T(128)S(6)} %copy.60), kind=kOutput, calls=%fused_computation.9.clone.1 | convolution fusion | flops 2157969408 | bytes 8654853 | tf_op jit(solution)/shard_map/while/body/eval_jaxpr/dot_general | solution.py:92
  200.4 8.0 %convert_reduce_fusion.3 = f32[8192]{0:T(1024)S(1)} fusion(s32[1024]{0:T(1024)S(1)} %bitcast.73), kind=kLoop, calls=%fused_computation.7.clone.1 | loop fusion | flops 33546240 | bytes 36864 | tf_op jit(solution)/shard_map/while/body/eval_jaxpr/reduce_sum | solution.py:96
  208.4 12.4 %fusion.72 = f32[8192,128]{1,0:T(8,128)} fusion(s32[1024]{0:T(1024)S(1)} %bitcast.74, f32[8192,128]{1,0:T(8,128)} %get-tuple-element.115, pred[]{:T(512)S(6)} %compare.28, bf16[8,1024,128]{2,1,0:T(8,128)(2,1)S(1)} %get-tuple-element.125, s32[]{:T(128)S(6)} %copy.60), kind=kOutput, calls=%fused_computation.9.clone.1 | convolution fusion | flops 2157969408 | bytes 8654853 | tf_op jit(solution)/shard_map/while/body/eval_jaxpr/dot_general | solution.py:92
  220.8 8.0 %convert_reduce_fusion.3 = f32[8192]{0:T(1024)S(1)} fusion(s32[1024]{0:T(1024)S(1)} %bitcast.73), kind=kLoop, calls=%fused_computation.7.clone.1 | loop fusion | flops 33546240 | bytes 36864 | tf_op jit(solution)/shard_map/while/body/eval_jaxpr/reduce_sum | solution.py:96
  228.8 12.4 %fusion.72 = f32[8192,128]{1,0:T(8,128)} fusion(s32[1024]{0:T(1024)S(1)} %bitcast.74, f32[8192,128]{1,0:T(8,128)} %get-tuple-element.115, pred[]{:T(512)S(6)} %compare.28, bf16[8,1024,128]{2,1,0:T(8,128)(2,1)S(1)} %get-tuple-element.125, s32[]{:T(128)S(6)} %copy.60), kind=kOutput, calls=%fused_computation.9.clone.1 | convolution fusion | flops 2157969408 | bytes 8654853 | tf_op jit(solution)/shard_map/while/body/eval_jaxpr/dot_general | solution.py:92
  241.1 8.0 %convert_reduce_fusion.3 = f32[8192]{0:T(1024)S(1)} fusion(s32[1024]{0:T(1024)S(1)} %bitcast.73), kind=kLoop, calls=%fused_computation.7.clone.1 | loop fusion | flops 33546240 | bytes 36864 | tf_op jit(solution)/shard_map/while/body/eval_jaxpr/reduce_sum | solution.py:96
  249.1 12.4 %fusion.72 = f32[8192,128]{1,0:T(8,128)} fusion(s32[1024]{0:T(1024)S(1)} %bitcast.74, f32[8192,128]{1,0:T(8,128)} %get-tuple-element.115, pred[]{:T(512)S(6)} %compare.28, bf16[8,1024,128]{2,1,0:T(8,128)(2,1)S(1)} %get-tuple-element.125, s32[]{:T(128)S(6)} %copy.60), kind=kOutput, calls=%fused_computation.9.clone.1 | convolution fusion | flops 2157969408 | bytes 8654853 | tf_op jit(solution)/shard_map/while/body/eval_jaxpr/dot_general | solution.py:92
  261.5 8.0 %convert_reduce_fusion.3 = f32[8192]{0:T(1024)S(1)} fusion(s32[1024]{0:T(1024)S(1)} %bitcast.73), kind=kLoop, calls=%fused_computation.7.clone.1 | loop fusion | flops 33546240 | bytes 36864 | tf_op jit(solution)/shard_map/while/body/eval_jaxpr/reduce_sum | solution.py:96
  269.5 12.4 %fusion.72 = f32[8192,128]{1,0:T(8,128)} fusion(s32[1024]{0:T(1024)S(1)} %bitcast.74, f32[8192,128]{1,0:T(8,128)} %get-tuple-element.115, pred[]{:T(512)S(6)} %compare.28, bf16[8,1024,128]{2,1,0:T(8,128)(2,1)S(1)} %get-tuple-element.125, s32[]{:T(128)S(6)} %copy.60), kind=kOutput, calls=%fused_computation.9.clone.1 | convolution fusion | flops 2157969408 | bytes 8654853 | tf_op jit(solution)/shard_map/while/body/eval_jaxpr/dot_general | solution.py:92
  290.6 2.9 divide_convert_fusion
  293.5 3.7 %collective-permute-start = (bf16[1,256,128]{2,1,0:T(8,128)(2,1)S(1)}, bf16[1,256,128]{2,1,0:T(8,128)(2,1)S(1)}, u32[]{:S(2)}, u32[]{:S(2)}) collective-permute-start(bf16[1,256,128]{2,1,0:T(8,128)(2,1)S(1)} %get-tuple-element.74), channel_id=1, source_target_pairs={{0,16},{16,32},{32,48},{48,64},{64,80},{80,96},{96,112},{1,17},{17... | collective-permute-start | bytes 196616 | tf_op jit(solution)/shard_map/ppermute | solution.py:20
  297.2 1.9 collective-permute-start.1
  299.1 3.6 %collective-permute-done.1 = bf16[1,256,128]{2,1,0:T(8,128)(2,1)S(1)} collective-permute-done((bf16[1,256,128]{2,1,0:T(8,128)(2,1)S(1)}, bf16[1,256,128]{2,1,0:T(8,128)(2,1)S(1)}, u32[]{:S(2)}, u32[]{:S(2)}) %collective-permute-start.1) | collective-permute-done | bytes 65568 | tf_op jit(solution)/shard_map/ppermute | solution.py:22
  302.8 1.3 collective-permute-start.2
  304.1 3.6 %collective-permute-start.3 = (bf16[34,1,128]{2,1,0:T(2,128)(2,1)S(1)}, bf16[34,1,128]{2,1,0:T(2,128)(2,1)S(1)}, u32[]{:S(2)}, u32[]{:S(2)}) collective-permute-start(bf16[34,1,128]{2,1,0:T(2,128)(2,1)S(1)} %get-tuple-element.73), channel_id=1, source_target_pairs={{1,0},{2,1},{3,2},{4,3},{5,4},{6,5},{7,6},{8,7},{9,8},{10,9},{11,1... | collective-permute-start | bytes 26120 | tf_op jit(solution)/shard_map/ppermute | solution.py:22
  307.7 1.1 collective-permute-done.2
  308.8 1.9 maximum_bitcast_fusion.1
  310.7 0.2 pad
  310.9 0.0 copy-start.3
  310.9 1.9 reshape.103
  312.9 2.2 copy.47
  315.1 6.2 %broadcast_select_fusion = f32[32,8,33,256]{3,1,2,0:T(8,128)S(1)} fusion(pred[8,33]{0,1:T(8,128)(4,1)S(1)} %copy-done.3, bf16[3,3,128,256]{3,2,1,0:T(8,128)(2,1)S(1)} %copy-done.2, bf16[34,1,7,2,128]{4,2,3,0,1:T(8,128)(2,1)S(1)} %slice.50, bf16[34,1,8,33,128]{4,2,3,0,1:T(8,128)(2,1)S(1)} %copy.47), kind=kOutput, calls=%fused_computation.36 | convolution fusion | flops 4992307200 | bytes 11660552 | tf_op jit(solution)/shard_map/conv_general_dilated | solution.py:41
  321.3 2.8 copy.48
  324.1 2.9 fusion.17
  327.0 0.3 slice.52
  327.2 3.0 collective-permute-start.4
  330.3 3.3 collective-permute-done.4
  333.6 0.1 collective-permute-start.5
  333.7 6.2 %collective-permute-done.5 = bf16[33,1,256]{2,0,1:T(8,128)(2,1)S(1)} collective-permute-done((bf16[33,1,256]{2,0,1:T(8,128)(2,1)S(1)}, bf16[33,1,256]{2,0,1:T(8,128)(2,1)S(1)}, u32[]{:S(2)}, u32[]{:S(2)}) %collective-permute-start.5) | collective-permute-done | bytes 16928 | tf_op jit(solution)/shard_map/ppermute | solution.py:37
  339.9 3.1 maximum_bitcast_fusion
  343.0 0.5 pad.2
  343.5 0.0 copy-start.4
  343.5 1.8 copy.51
  345.3 0.1 slice.53
  345.4 3.0 fusion.48
  348.4 0.7 copy.52
  349.1 0.7 fusion.42
  349.8 1.3 copy.53
  (45 shorter events, 0.4 us)
Async XLA Ops:
  0.0 345.4 %copy-start = (bf16[3,3,256,256]{3,2,1,0:T(8,128)(2,1)S(1)}, bf16[3,3,256,256]{3,2,1,0:T(8,128)(2,1)}, u32[]{:S(2)}) copy-start(bf16[3,3,256,256]{3,2,1,0:T(8,128)(2,1)} %param.13) | copy-start | bytes 3538948
  2.8 1.5 copy-start.1
  7.2 28.0 %all-to-all-start = ((s32[128,1,1]{2,1,0:T(1,128)}), s32[128,1,1]{2,1,0:T(1,128)S(1)}, u32[]{:S(2)}, u32[]{:S(2)}) async-start(s32[128,1,1]{2,1,0:T(1,128)} %copy.42), calls=%async_computation | async-start | bytes 131072 | tf_op jit(solution)/shard_map/all_to_all | solution.py:77
  35.2 22.5 %all-to-all-start.1 = ((s32[128,64,1]{1,2,0:T(1,128)}), s32[128,64,1]{1,2,0:T(1,128)S(1)}, u32[]{:S(2)}, u32[]{:S(2)}) async-start(s32[128,64,1]{1,2,0:T(1,128)} %bitcast.10), calls=%async_computation.1 | async-start | bytes 131072 | tf_op jit(solution)/shard_map/all_to_all | solution.py:76
  57.8 62.5 %all-to-all-start.2 = ((bf16[128,64,128]{2,1,0:T(8,128)(2,1)}), bf16[128,64,128]{2,1,0:T(8,128)(2,1)S(1)}, u32[]{:S(2)}, u32[]{:S(2)}) async-start(bf16[128,64,128]{2,1,0:T(8,128)(2,1)} %bitcast.11), calls=%async_computation.2 | async-start | bytes 4194304 | tf_op jit(solution)/shard_map/all_to_all | solution.py:75
  293.5 5.6 %collective-permute-start = (bf16[1,256,128]{2,1,0:T(8,128)(2,1)S(1)}, bf16[1,256,128]{2,1,0:T(8,128)(2,1)S(1)}, u32[]{:S(2)}, u32[]{:S(2)}) collective-permute-start(bf16[1,256,128]{2,1,0:T(8,128)(2,1)S(1)} %get-tuple-element.74), channel_id=1, source_target_pairs={{0,16},{16,32},{32,48},{48,64},{64,80},{80,96},{96,112},{1,17},{17... | collective-permute-start | bytes 196616 | tf_op jit(solution)/shard_map/ppermute | solution.py:20
  297.2 5.6 %collective-permute-start.1 = (bf16[1,256,128]{2,1,0:T(8,128)(2,1)S(1)}, bf16[1,256,128]{2,1,0:T(8,128)(2,1)S(1)}, u32[]{:S(2)}, u32[]{:S(2)}) collective-permute-start(bf16[1,256,128]{2,1,0:T(8,128)(2,1)S(1)} %get-tuple-element.75), channel_id=1, source_target_pairs={{16,0},{32,16},{48,32},{64,48},{80,64},{96,80},{112,96},{17,1},{33... | collective-permute-start | bytes 196616 | tf_op jit(solution)/shard_map/ppermute | solution.py:22
  302.8 6.0 %collective-permute-start.2 = (bf16[34,1,128]{2,1,0:T(2,128)(2,1)S(1)}, bf16[34,1,128]{2,1,0:T(2,128)(2,1)S(1)}, u32[]{:S(2)}, u32[]{:S(2)}) collective-permute-start(bf16[34,1,128]{2,1,0:T(2,128)(2,1)S(1)} %get-tuple-element.72), channel_id=1, source_target_pairs={{0,1},{1,2},{2,3},{3,4},{4,5},{5,6},{6,7},{7,8},{8,9},{9,10},{10,1... | collective-permute-start | bytes 26120 | tf_op jit(solution)/shard_map/ppermute | solution.py:20
  304.1 4.7 %collective-permute-start.3 = (bf16[34,1,128]{2,1,0:T(2,128)(2,1)S(1)}, bf16[34,1,128]{2,1,0:T(2,128)(2,1)S(1)}, u32[]{:S(2)}, u32[]{:S(2)}) collective-permute-start(bf16[34,1,128]{2,1,0:T(2,128)(2,1)S(1)} %get-tuple-element.73), channel_id=1, source_target_pairs={{1,0},{2,1},{3,2},{4,3},{5,4},{6,5},{7,6},{8,7},{9,8},{10,9},{11,1... | collective-permute-start | bytes 26120 | tf_op jit(solution)/shard_map/ppermute | solution.py:22
  310.9 4.2 %copy-start.3 = (pred[8,33]{0,1:T(8,128)(4,1)S(1)}, pred[8,33]{0,1:T(8,128)(4,1)}, u32[]{:S(2)}) copy-start(pred[8,33]{0,1:T(8,128)(4,1)} %constant.86) | copy-start | bytes 796
  312.9 2.2 copy-start.2
  327.2 6.3 %collective-permute-start.4 = (bf16[1,256,256]{2,0,1:T(2,128)(2,1)S(1)}, bf16[1,256,256]{2,0,1:T(2,128)(2,1)S(1)}, u32[]{:S(2)}, u32[]{:S(2)}) collective-permute-start(bf16[1,256,256]{2,0,1:T(2,128)(2,1)S(1)} %slice.52), channel_id=1, source_target_pairs={{0,16},{16,32},{32,48},{48,64},{64,80},{80,96},{96,112},{1,17},{17... | collective-permute-start | bytes 393224 | tf_op jit(solution)/shard_map/ppermute | solution.py:32
  333.6 6.3 %collective-permute-start.5 = (bf16[33,1,256]{2,0,1:T(8,128)(2,1)S(1)}, bf16[33,1,256]{2,0,1:T(8,128)(2,1)S(1)}, u32[]{:S(2)}, u32[]{:S(2)}) collective-permute-start(bf16[33,1,256]{2,0,1:T(8,128)(2,1)S(1)} %pad_maximum_fusion), channel_id=1, source_target_pairs={{0,1},{1,2},{2,3},{3,4},{4,5},{5,6},{6,7},{7,8},{8,9},{9,10},{10,1... | collective-permute-start | bytes 50696 | tf_op jit(solution)/shard_map/ppermute | solution.py:37
  343.5 1.9 copy-start.4
where the time goes:
time: 356 us; the launch traced here: 351 us
  matrix products  106 us (30%)
  local copies, waits for them, and re-layouts  93.3 us (26%)
  other arithmetic  82.3 us (23%)
  starting transfers between devices  44.6 us (13%)
  waiting for transfers between devices  14.2 us (4%)
  loops' own time  9.18 us (3%)
    dot_general x8, matrix products, accumulate(): lax.dot_general(one_hot, block_values, (((0,), (0,)), ((), ())), preferre...  97.3 us
    reduce_sum x8, other arithmetic, accumulate(): jnp.sum(one_hot, axis=0, dtype=jnp.float32)  63.8 us
    gather x2, local copies, waits for them, and re-layouts, body(): live_slot = slot_in_source < got_counts[source_of_slot]  48.9 us
    scatter x1, local copies, waits for them, and re-layouts, body(): jnp.zeros((devices * capacity,), jnp.int32).at[slot_ids]  15.7 us
    scatter x1, local copies, waits for them, and re-layouts, body(): send_values = jnp.zeros((devices * capacity, channels), jnp.bfloat16).at[...  12.8 us
    all_to_all x1, starting transfers between devices, body(): lax.all_to_all(live_counts, ('lat', 'lon'), split_axis=0, concat_axis=0,...  11.5 us
    all_to_all x1, starting transfers between devices, body(): lax.all_to_all(send_cells, ('lat', 'lon'), split_axis=0, concat_axis=0, t...  9.76 us
    all_to_all x1, starting transfers between devices, body(): lax.all_to_all(send_values, ('lat', 'lon'), split_axis=0, concat_axis=0,...  9.76 us
  transfers between devices with their start and end apart: 9, of which 4 were waited for; matrix products, arithmetic and copies ran while one was open for 23% of the time, Pallas kernels for 0%

commit v1 on v0

v1 whole, which is shorter than its diff:
```python
import functools

import jax
import jax.numpy as jnp
from jax import lax
from jax.experimental import pallas as pl
from jax.experimental.pallas import tpu as pltpu
from jax.sharding import PartitionSpec as P

TH = 32
TW = 256
CH = 128
HID = 256
DEV = 128
CAP = 64
ROWS = 4096
BLK = 72
SEND = DEV * BLK
TRASH = 256
GROUP = 32
COLS = 48
F32 = jnp.float32
BF16 = jnp.bfloat16


def gelu(x):
    inner = x * (0.7978845608028654 + 0.035677408136300125 * (x * x))
    return (0.5 * x) * (1.0 + jnp.tanh(inner))


def pack_kernel(count_ref, dest_ref, cell_ref, val_ref, out_ref, x32, o32, slot_v, slot_s, sem):
    count = count_ref[0]
    lane = lax.broadcasted_iota(jnp.int32, (1, 256), 1)
    dest_ids = lax.broadcasted_iota(jnp.int32, (DEV, 256), 0)
    pos_ids = lax.broadcasted_iota(jnp.int32, (CAP, 256), 0)
    upper = (
        lax.broadcasted_iota(jnp.int32, (256, 256), 0)
        < lax.broadcasted_iota(jnp.int32, (256, 256), 1)
    ).astype(F32).astype(BF16)
    carry = jnp.zeros((DEV, 1), F32)
    cells = jnp.zeros((DEV, 2 * CAP), F32)
    for a in range(ROWS // 256):
        dest = jnp.concatenate([dest_ref[2 * a : 2 * a + 1], dest_ref[2 * a + 1 : 2 * a + 2]], axis=1)
        cell = jnp.concatenate([cell_ref[2 * a : 2 * a + 1], cell_ref[2 * a + 1 : 2 * a + 2]], axis=1)
        live = (lane + 256 * a) < count
        dest_or = jnp.where(live, dest, DEV)
        hot = (dest_ids == dest_or).astype(F32)
        hot16 = hot.astype(BF16)
        before = jnp.dot(hot16, upper, preferred_element_type=F32) + carry
        carry = carry + jnp.sum(hot, axis=1, keepdims=True)
        pos = jnp.sum(hot * before, axis=0, keepdims=True).astype(jnp.int32)
        slot = jnp.where(live, dest * BLK + pos, SEND)
        slot_v[2 * a : 2 * a + 1] = slot[:, :128]
        slot_v[2 * a + 1 : 2 * a + 2] = slot[:, 128:]
        high = (cell // TW + 1).astype(F32)
        low = ((cell % 16) * 16 + (cell % TW) // 16).astype(F32)
        pos_hot = pos_ids == pos
        coded = jnp.concatenate(
            [jnp.where(pos_hot, high, 0.0), jnp.where(pos_hot, low, 0.0)], axis=0
        ).astype(BF16)
        cells = cells + lax.dot_general(
            hot16, coded, (((1,), (1,)), ((), ())), preferred_element_type=F32
        )
    to_scalar = pltpu.make_async_copy(slot_v, slot_s, sem)
    to_scalar.start()

    def widen(i, c):
        rows = pl.ds(pl.multiple_of(i * 128, 128), 128)
        x32[rows, :] = val_ref[rows, :].astype(F32)
        return c

    lax.fori_loop(0, ROWS // 128, widen, 0)
    to_scalar.wait()

    def move(i, c):
        for k in range(32):
            slot = slot_s[i // 4, (i % 4) * 32 + k]
            o32[pl.ds(slot, 1), :] = x32[pl.ds(i * 32 + k, 1), :]
        return c

    lax.fori_loop(0, ROWS // 32, move, 0)
    for d in range(DEV):
        o32[d * BLK + CAP : d * BLK + CAP + 1, :] = cells[d : d + 1, :]

    def narrow(i, c):
        rows = pl.ds(pl.multiple_of(i * 128, 128), 128)
        out_ref[rows, :] = o32[rows, :].astype(BF16)
        return c

    lax.fori_loop(0, SEND // 128, narrow, 0)


def pack(obs_values, obs_dest, obs_cell, obs_count):
    return pl.pallas_call(
        pack_kernel,
        out_shape=jax.ShapeDtypeStruct((SEND, CH), BF16),
        in_specs=[pl.BlockSpec(memory_space=pltpu.SMEM)] + [pl.BlockSpec(memory_space=pltpu.VMEM)] * 3,
        out_specs=pl.BlockSpec(memory_space=pltpu.VMEM),
        scratch_shapes=[
            pltpu.VMEM((ROWS, CH), F32),
            pltpu.VMEM((SEND + 8, CH), F32),
            pltpu.VMEM((32, 128), jnp.int32),
            pltpu.SMEM((32, 128), jnp.int32),
            pltpu.SemaphoreType.DMA,
        ],
        compiler_params=pltpu.CompilerParams(vmem_limit_bytes=40 * 1024 * 1024),
        name="pack",
    )(obs_count, obs_dest.reshape(32, 128), obs_cell.reshape(32, 128), obs_values)


def grid_kernel(
    got_ref, out_ref, top_ref, bottom_ref, edge_ref, x32, acc, table_v, table_s, rowpair, colpair, edge32, sem
):
    def widen(i, c):
        rows = pl.ds(pl.multiple_of(i * 128, 128), 128)
        x32[rows, :] = got_ref[rows, :].astype(F32)
        return c

    lax.fori_loop(0, SEND // 128, widen, 0)
    cells = jnp.concatenate([x32[s * BLK + CAP : s * BLK + CAP + 1, :] for s in range(DEV)], axis=0)
    swapped = pltpu.roll(cells, CAP, axis=1)
    lane = lax.broadcasted_iota(jnp.int32, (DEV, 128), 1)
    first = lane < CAP
    index = jnp.where(
        cells == 0.0, lane, cells.astype(jnp.int32) * TW + swapped.astype(jnp.int32)
    )
    index = jnp.where(first, index, -1)
    repeated = jnp.zeros((DEV, 128), jnp.bool_)
    for d in range(1, GROUP):
        same = (index == pltpu.roll(index, d, axis=1)) & (lane % GROUP >= d)
        repeated = repeated | same
    repeated = jnp.where(first & repeated, 1.0, 0.0).astype(BF16)
    groups = (
        lax.broadcasted_iota(jnp.int32, (128, 128), 0) // GROUP
        == (lax.broadcasted_iota(jnp.int32, (128, 128), 1) - CAP)
    ).astype(F32).astype(BF16)
    flags = jnp.dot(repeated, groups, preferred_element_type=F32).astype(jnp.int32)
    table_v[...] = jnp.where(first, index, flags)
    to_scalar = pltpu.make_async_copy(table_v, table_s, sem)
    to_scalar.start()

    half = DEV // 2
    firsth = lax.broadcasted_iota(jnp.int32, (half, 128), 1) < CAP
    rowpair[...] = jnp.where(firsth, cells[:half], swapped[half:])
    colpair[...] = jnp.where(firsth, swapped[:half], cells[half:])
    col_ids = lax.broadcasted_iota(jnp.int32, (TW, 128), 0).astype(F32)
    row_ids = (lax.broadcasted_iota(jnp.int32, (128, 128), 0) + 1).astype(F32)

    def tally(i, total):
        col_hot = (col_ids == colpair[pl.ds(i, 1), :]).astype(F32).astype(BF16)
        row_hot = (row_ids == rowpair[pl.ds(i, 1), :]).astype(F32).astype(BF16)
        return total + lax.dot_general(
            col_hot, row_hot, (((1,), (1,)), ((), ())), preferred_element_type=F32
        )

    tallies = lax.fori_loop(0, half, tally, jnp.zeros((TW, 128), F32))
    inverse = 1.0 / jnp.maximum(tallies, 1.0)

    def clear(i, c):
        acc[pl.ds(pl.multiple_of(i * 128, 128), 128), :] = jnp.zeros((128, CH), F32)
        return c

    lax.fori_loop(0, (TRASH + TH * TW) // 128, clear, 0)
    to_scalar.wait()

    def source(s, c):
        for g in range(CAP // GROUP):
            clash = table_s[s, CAP + g]

            @pl.when(clash == 0)
            def _():
                index = [table_s[s, g * GROUP + k] for k in range(GROUP)]
                sums = [
                    acc[pl.ds(index[k], 1), :] + x32[pl.ds(s * BLK + g * GROUP + k, 1), :]
                    for k in range(GROUP)
                ]
                for k in range(GROUP):
                    acc[pl.ds(index[k], 1), :] = sums[k]

            @pl.when(clash != 0)
            def _():
                for k in range(GROUP):
                    at = pl.ds(table_s[s, g * GROUP + k], 1)
                    acc[at, :] = acc[at, :] + x32[pl.ds(s * BLK + g * GROUP + k, 1), :]

        return c

    lax.fori_loop(0, DEV, source, 0)
    for i in range(TH):
        scale = jnp.broadcast_to(inverse[:, i : i + 1], (TW, CH))
        mean = acc[TRASH + i * TW : TRASH + (i + 1) * TW, :] * scale
        out_ref[i * TW : (i + 1) * TW, :] = mean.astype(BF16)
        if i == 0:
            top_ref[...] = mean.astype(BF16)
        if i >= TH - 2:
            bottom_ref[(i - TH + 2) * TW : (i - TH + 3) * TW, :] = mean.astype(BF16)
        edge32[0, i : i + 1, :] = mean[0:1]
        edge32[1, i : i + 1, :] = mean[239:240]
        edge32[2, i : i + 1, :] = mean[255:256]
    edge_ref[...] = edge32[...].astype(BF16)


def to_grid(got):
    shapes = [(TH * TW, CH), (TW, CH), (2 * TW, CH), (3, TH, CH)]
    return pl.pallas_call(
        grid_kernel,
        out_shape=[jax.ShapeDtypeStruct(s, BF16) for s in shapes],
        in_specs=[pl.BlockSpec(memory_space=pltpu.VMEM)],
        out_specs=[pl.BlockSpec(memory_space=pltpu.VMEM)] * 4,
        scratch_shapes=[
            pltpu.VMEM((SEND, CH), F32),
            pltpu.VMEM((TRASH + TH * TW, CH), F32),
            pltpu.VMEM((DEV, 128), jnp.int32),
            pltpu.SMEM((DEV, 128), jnp.int32),
            pltpu.VMEM((DEV // 2, 128), F32),
            pltpu.VMEM((DEV // 2, 128), F32),
            pltpu.VMEM((3, TH, CH), F32),
            pltpu.SemaphoreType.DMA,
        ],
        compiler_params=pltpu.CompilerParams(vmem_limit_bytes=40 * 1024 * 1024),
        name="to_grid",
    )(got)


def conv_kernel(
    band_ref, cell_ref, north_ref, south_ref, own_ref, west_ref, east_ref, w1_ref, w2_ref, out_ref,
    field, even, odd, wcol, ecol, hcol,
):
    field[0:2, 1:17] = north_ref[...].reshape(2, 16, 16, CH)
    field[2 + TH, 1:17] = south_ref[...].reshape(16, 16, CH)

    def place(i, c):
        rows = pl.ds(pl.multiple_of(i * TW, TW), TW)
        field[2 + i, 1:17] = cell_ref[rows, :].reshape(16, 16, CH)
        return c

    lax.fori_loop(0, TH, place, 0)
    wcol[...] = west_ref[1].astype(F32)
    ecol[...] = east_ref[...].astype(F32)
    sub = lax.broadcasted_iota(jnp.int32, (16, CH), 0)

    def wrap(r, c):
        before = pltpu.roll(field[r, 16].astype(F32), 1, axis=0)
        field[r, 0] = jnp.where(sub == 0, wcol[pl.ds(r, 1), :], before).astype(BF16)
        after = pltpu.roll(field[r, 1].astype(F32), 15, axis=0)
        field[r, 17] = jnp.where(sub == 15, ecol[pl.ds(r, 1), :], after).astype(BF16)
        return c

    lax.fori_loop(0, TH + 3, wrap, 0)

    taps = [west_ref[0].astype(F32), west_ref[1].astype(F32), own_ref[...].astype(F32)]
    lhs = jnp.concatenate([taps[b][a : a + 40] for a in range(3) for b in range(3)], axis=1)
    hcol[...] = gelu(jnp.dot(lhs.astype(BF16), w1_ref[...], preferred_element_type=F32))
    sub2 = lax.broadcasted_iota(jnp.int32, (16, HID), 0)

    def first(step, c):
        lhs = jnp.concatenate(
            [
                jnp.concatenate(
                    [
                        field[3 * step + r + a, b : b + 16].reshape(TW, CH)
                        for a in range(3)
                        for b in range(3)
                    ],
                    axis=1,
                )
                for r in range(3)
            ],
            axis=0,
        )
        y = gelu(jnp.dot(lhs, w1_ref[...], preferred_element_type=F32))
        y16 = y.astype(BF16).reshape(3, 8, 2, 16, HID)
        for r in range(3):
            hr = 3 * step + r
            odd[hr] = y16[r, :, 0]
            even[hr, 1:9] = y16[r, :, 1]
            before = pltpu.roll(y[r * TW + 240 : r * TW + 256], 1, axis=0)
            even[hr, 0] = jnp.where(sub2 == 0, hcol[pl.ds(hr, 1), :], before).astype(BF16)
        return c

    lax.fori_loop(0, 11, first, 0)

    @pl.when(band_ref[0] == 0)
    def _():
        even[0] = jnp.zeros((9, 16, HID), BF16)
        odd[0] = jnp.zeros((8, 16, HID), BF16)

    out_row = lax.broadcasted_iota(jnp.int32, (128, 128), 0)
    out_col = lax.broadcasted_iota(jnp.int32, (128, 128), 1)
    order = ((out_row % 8) * 16 + out_row // 8 == out_col).astype(F32).astype(BF16)

    def second(step, c):
        lhs = jnp.concatenate(
            [
                jnp.concatenate(
                    [
                        x.reshape(128, HID)
                        for a in range(3)
                        for x in (
                            even[4 * step + 2 * r + a, 0:8],
                            odd[4 * step + 2 * r + a],
                            even[4 * step + 2 * r + a, 1:9],
                        )
                    ],
                    axis=1,
                )
                for r in range(2)
            ],
            axis=0,
        )
        y = gelu(jnp.dot(lhs, w2_ref[...], preferred_element_type=F32)).astype(BF16)
        for r in range(2):
            out_ref[2 * step + r] = jnp.dot(
                order, y[r * 128 : (r + 1) * 128], preferred_element_type=F32
            ).astype(BF16)
        return c

    lax.fori_loop(0, TH // 4, second, 0)


def convolve(band, cells, north, south, own, west, east, w1, w2):
    return pl.pallas_call(
        conv_kernel,
        out_shape=jax.ShapeDtypeStruct((TH // 2, TW // 2, HID), BF16),
        in_specs=[pl.BlockSpec(memory_space=pltpu.SMEM)] + [pl.BlockSpec(memory_space=pltpu.VMEM)] * 8,
        out_specs=pl.BlockSpec(memory_space=pltpu.VMEM),
        scratch_shapes=[
            pltpu.VMEM((TH + 3, 18, 16, CH), BF16),
            pltpu.VMEM((TH + 1, 9, 16, HID), BF16),
            pltpu.VMEM((TH + 1, 8, 16, HID), BF16),
            pltpu.VMEM((COLS, CH), F32),
            pltpu.VMEM((COLS, CH), F32),
            pltpu.VMEM((40, HID), F32),
        ],
        compiler_params=pltpu.CompilerParams(vmem_limit_bytes=48 * 1024 * 1024),
        name="convolve",
    )(band, cells, north, south, own, west, east, w1, w2)


def body(obs_values, obs_dest, obs_cell, obs_count, conv_in, conv_down):
    lat = lax.axis_size("lat")
    lon = lax.axis_size("lon")
    send = pack(obs_values, obs_dest, obs_cell, obs_count)
    got = lax.all_to_all(
        send.reshape(DEV, BLK, CH), ("lat", "lon"), split_axis=0, concat_axis=0, tiled=True
    )
    cells, top, bottom, edge = to_grid(got.reshape(SEND, CH))
    north = lax.ppermute(bottom, "lat", [(i, i + 1) for i in range(lat - 1)])
    south = lax.ppermute(top, "lat", [(i + 1, i) for i in range(lat - 1)])
    north3 = north.reshape(2, TW, CH)
    full = jnp.stack(
        [
            jnp.concatenate(
                [north3[:, at], edge[e], south[at : at + 1], jnp.zeros((COLS - TH - 3, CH), BF16)]
            )
            for e, at in enumerate((0, 239, 255))
        ]
    )
    own = full[0]
    west = lax.ppermute(full[1:], "lon", [(i, (i + 1) % lon) for i in range(lon)])
    east = lax.ppermute(own, "lon", [((i + 1) % lon, i) for i in range(lon)])
    band = lax.axis_index("lat").astype(jnp.int32).reshape(1)
    return convolve(
        band, cells, north, south, own, west, east,
        conv_in.reshape(9 * CH, HID), conv_down.reshape(9 * HID, HID),
    )


def solution(mesh):
    placed = (
        P(("lat", "lon"), None),
        P(("lat", "lon"), None),
        P(("lat", "lon")),
        P(("lat", "lon")),
        P(),
        P(),
    )
    return jax.shard_map(
        body, mesh=mesh, in_specs=placed, out_specs=P("lat", "lon", None), check_vma=False
    )
```

time: 356 us -> 131 us (0.37); the launches traced: 351 us -> 131 us
  matrix products: 106 us -> 0 us
  local copies, waits for them, and re-layouts: 93.3 us -> 8.17 us
  other arithmetic: 82.3 us -> 0.09 us
  Pallas kernels: 0 us -> 63.2 us
  starting transfers between devices: 44.6 us -> 21.1 us
  waiting for transfers between devices: 14.2 us -> 37.3 us
  loops' own time: 9.18 us -> 0 us
    dot_general x8 -> x0, matrix products: 97.3 us -> none  [accumulate(): lax.dot_general(one_hot, block_values, (((0,), (0,)), ((), ())), preferre...]
    reduce_sum x9 -> x0, other arithmetic: 66 us -> none  [the longest x8 63.8 us: accumulate(): jnp.sum(one_hot, axis=0, dtype=jnp.float32)]
    pallas_call x0 -> x3, Pallas kernels: none -> 63.2 us  [the longest x1 35.4 us: to_grid(): pl.pallas_call(grid_kernel, out_shape=[jax.ShapeDtypeStruct(s, BF16) for...]
    gather x2 -> x0, local copies, waits for them, and re-layouts: 48.9 us -> none  [body(): live_slot = slot_in_source < got_counts[source_of_slot]]
    all_to_all x3 -> x1, waiting for transfers between devices: 0.01 us -> 32.5 us  [body(): lax.all_to_all(send.reshape(DEV, BLK, CH), ('lat', 'lon'), split_axis=0,...]
    scatter x2 -> x0, local copies, waits for them, and re-layouts: 28.5 us -> none  [the longest x1 15.7 us: body(): jnp.zeros((devices * capacity,), jnp.int32).at[slot_ids]]
    all_to_all x3 -> x1, starting transfers between devices: 31 us -> 11.5 us  [body(): lax.all_to_all(send.reshape(DEV, BLK, CH), ('lat', 'lon'), split_axis=0,...]
    conv_general_dilated x7 -> x0, local copies, waits for them, and re-layouts: 9.5 us -> none  [convolve(): lax.conv_general_dilated(field[None], weights, (stride, stride), 'VALID',...]
  transfers between devices with their start and end apart: 9 -> 5, of which waited for: 4 -> 4; matrix products, arithmetic and copies ran while one was open for 23% -> 0% of each run, Pallas kernels for 0% -> 0%
where the time goes in v1:
time: 131 us
  Pallas kernels  63.2 us (48%)
  waiting for transfers between devices  37.3 us (28%)
  starting transfers between devices  21.1 us (16%)
  local copies, waits for them, and re-layouts  8.17 us (6%)
    pallas_call x1, Pallas kernels, to_grid(): pl.pallas_call(grid_kernel, out_shape=[jax.ShapeDtypeStruct(s, BF16) for...  35.4 us
    all_to_all x1, waiting for transfers between devices, body(): lax.all_to_all(send.reshape(DEV, BLK, CH), ('lat', 'lon'), split_axis=0,...  32.5 us
    pallas_call x1, Pallas kernels, convolve(): pl.pallas_call(conv_kernel, out_shape=jax.ShapeDtypeStruct((TH // 2, TW /...  15.3 us
    pallas_call x1, Pallas kernels, pack(): pl.pallas_call(pack_kernel, out_shape=jax.ShapeDtypeStruct((SEND, CH), BF...  12.4 us
    all_to_all x1, starting transfers between devices, body(): lax.all_to_all(send.reshape(DEV, BLK, CH), ('lat', 'lon'), split_axis=0,...  11.5 us
    unnamed x17, local copies, waits for them, and re-layouts  8.07 us
    ppermute x1, waiting for transfers between devices, body(): south = lax.ppermute(top, 'lat', [(i + 1, i) for i in range(lat - 1)])  3.64 us
    ppermute x1, starting transfers between devices, body(): east = lax.ppermute(own, 'lon', [((i + 1) % lon, i) for i in range(lon)])  3.48 us
  transfers between devices with their start and end apart: 5, of which 4 were waited for; matrix products, arithmetic and copies ran while one was open for 0% of the time, Pallas kernels for 0%

profile of v1, /device:TPU:1, one launch (start us, length us, event | category | flops | bytes accessed | tf_op | source)
XLA Modules:
  0.0 130.7 jit_solution(18014731872319755077)
XLA Ops:
  0.7 0.0 copy-start.4
  0.7 1.2 copy-done.4
  1.9 0.0 copy-start.6
  1.9 0.7 copy-done.6
  2.6 0.0 copy-start.7
  2.6 0.7 copy-done.7
  3.3 12.4 %pack.1 = bf16[9216,128]{1,0:T(8,128)(2,1)S(1)} custom-call(s32[1]{0:T(128)S(6)} %copy.17.count_ref, s32[32,128]{1,0:T(8,128)S(1)} %bitcast.30, s32[32,128]{1,0:T(8,128)S(1)} %bitcast.31, bf16[4096,128]{1,0:T(8,128)(2,1)S(1)} %copy-done.4), custom_call_target="tpu_custom_call" | custom-call | tf_op jit(solution)/shard_map/pack/pallas_call | solution.py:94
  15.7 0.0 copy-start
  15.7 1.4 %copy-done = bf16[9216,128]{1,0:T(8,128)(2,1)} copy-done((bf16[9216,128]{1,0:T(8,128)(2,1)}, bf16[9216,128]{1,0:T(8,128)(2,1)S(1)}, u32[]{:S(2)}) %copy-start) | copy-done | bytes 2359320
  17.1 11.5 %all-to-all-start = ((bf16[128,72,128]{2,1,0:T(8,128)(2,1)}), bf16[128,72,128]{2,1,0:T(8,128)(2,1)S(1)}, u32[]{:S(2)}, u32[]{:S(2)}) async-start(bf16[128,72,128]{2,1,0:T(8,128)(2,1)} %bitcast.26), calls=%async_computation | async-start | bytes 4718592 | tf_op jit(solution)/shard_map/all_to_all | solution.py:344
  28.6 0.0 copy-start.3
  28.7 0.1 pad.13.clone
  28.7 32.5 %all-to-all-done = bf16[128,72,128]{2,1,0:T(8,128)(2,1)S(1)} async-done(((bf16[128,72,128]{2,1,0:T(8,128)(2,1)}), bf16[128,72,128]{2,1,0:T(8,128)(2,1)S(1)}, u32[]{:S(2)}, u32[]{:S(2)}) %all-to-all-start) | async-done | bytes 2359328 | tf_op jit(solution)/shard_map/all_to_all | solution.py:344
  61.2 35.4 %to_grid.1 = (bf16[8192,128]{1,0:T(8,128)(2,1)S(1)}, bf16[256,128]{1,0:T(8,128)(2,1)S(1)}, bf16[512,128]{1,0:T(8,128)(2,1)S(1)}, bf16[3,32,128]{2,1,0:T(8,128)(2,1)S(1)}) custom-call(bf16[9216,128]{1,0:T(8,128)(2,1)S(1)} %bitcast.25), custom_call_target="tpu_custom_call" | custom-call | tf_op jit(solution)/shard_map/to_grid/pallas_call | solution.py:205
  96.7 0.0 copy-start.1
  96.7 1.3 %copy-done.1 = bf16[8192,128]{1,0:T(8,128)(2,1)} copy-done((bf16[8192,128]{1,0:T(8,128)(2,1)}, bf16[8192,128]{1,0:T(8,128)(2,1)S(1)}, u32[]{:S(2)}) %copy-start.1) | copy-done | bytes 2097176
  98.0 2.9 %collective-permute-start = (bf16[512,128]{1,0:T(8,128)(2,1)S(1)}, bf16[512,128]{1,0:T(8,128)(2,1)S(1)}, u32[]{:S(2)}, u32[]{:S(2)}) collective-permute-start(bf16[512,128]{1,0:T(8,128)(2,1)S(1)} %get-tuple-element.10), channel_id=1, source_target_pairs={{0,16},{16,32},{32,48},{48,64},{64,80},{80,96},{96,112},{1,17},{17... | collective-permute-start | bytes 393224 | tf_op jit(solution)/shard_map/ppermute | solution.py:348
  100.9 1.9 %collective-permute-start.1 = (bf16[256,128]{1,0:T(8,128)(2,1)S(1)}, bf16[256,128]{1,0:T(8,128)(2,1)S(1)}, u32[]{:S(2)}, u32[]{:S(2)}) collective-permute-start(bf16[256,128]{1,0:T(8,128)(2,1)S(1)} %get-tuple-element.11), channel_id=1, source_target_pairs={{16,0},{32,16},{48,32},{64,48},{80,64},{96,80},{112,96},{17,1},{33... | collective-permute-start | bytes 196616 | tf_op jit(solution)/shard_map/ppermute | solution.py:349
  102.8 3.6 %collective-permute-done.1.south_ref = bf16[256,128]{1,0:T(8,128)(2,1)S(1)} collective-permute-done((bf16[256,128]{1,0:T(8,128)(2,1)S(1)}, bf16[256,128]{1,0:T(8,128)(2,1)S(1)}, u32[]{:S(2)}, u32[]{:S(2)}) %collective-permute-start.1) | collective-permute-done | bytes 65568 | tf_op jit(solution)/shard_map/ppermute | solution.py:349
  106.5 0.0 collective-permute-done.north_ref
  106.5 0.1 maximum_bitcast_fusion
  106.6 1.4 %collective-permute-start.2 = (bf16[2,48,128]{2,1,0:T(8,128)(2,1)S(1)}, bf16[2,48,128]{2,1,0:T(8,128)(2,1)S(1)}, u32[]{:S(2)}, u32[]{:S(2)}) collective-permute-start(bf16[2,48,128]{2,1,0:T(8,128)(2,1)S(1)} %pad_maximum_fusion), channel_id=1, source_target_pairs={{0,1},{1,2},{2,3},{3,4},{4,5},{5,6},{6,7},{7,8},{8,9},{9,10},{10,1... | collective-permute-start | bytes 73736 | tf_op jit(solution)/shard_map/ppermute | solution.py:360
  108.0 3.5 %collective-permute-start.3 = (bf16[48,128]{1,0:T(8,128)(2,1)S(1)}, bf16[48,128]{1,0:T(8,128)(2,1)S(1)}, u32[]{:S(2)}, u32[]{:S(2)}) collective-permute-start(bf16[48,128]{1,0:T(8,128)(2,1)S(1)} %get-tuple-element.24.own_ref), channel_id=1, source_target_pairs={{1,0},{2,1},{3,2},{4,3},{5,4},{6,5},{7,6},{8,7},{9,8},{10,9},{11,1... | collective-permute-start | bytes 36872 | tf_op jit(solution)/shard_map/ppermute | solution.py:361
  111.5 0.8 collective-permute-done.3.east_ref
  112.3 0.4 collective-permute-done.2.west_ref
  112.7 0.0 copy-done.3
  112.7 0.0 copy-start.2
  112.7 1.6 %copy-done.2 = bf16[8192,128]{1,0:T(8,128)(2,1)S(1)} copy-done((bf16[8192,128]{1,0:T(8,128)(2,1)S(1)}, bf16[8192,128]{1,0:T(8,128)(2,1)}, u32[]{:S(2)}) %copy-start.2) | copy-done | bytes 2097176
  114.3 0.0 copy-start.5
  114.3 1.1 copy-done.5
  115.3 15.3 %convolve.1 = bf16[16,128,256]{2,1,0:T(8,128)(2,1)} custom-call(s32[1]{0:T(128)} %bitcast.band_ref, bf16[8192,128]{1,0:T(8,128)(2,1)S(1)} %copy-done.2, bf16[512,128]{1,0:T(8,128)(2,1)S(1)} %collective-permute-done.north_ref, bf16[256,128]{1,0:T(8,128)(2,1)S(1)} %collective-permute-done.1.south_ref, bf16[48,128]{1,0:T(8,128)(2,1)S(1)} %get-tuple-element.24.own_ref, ...), custom_call_target="tpu_custom_call" | custom-call | tf_op jit(solution)/shard_map/convolve/pallas_call | solution.py:322
  (7 shorter events, 0.0 us)
Async XLA Ops:
  0.7 1.2 copy-start.4
  1.9 0.7 copy-start.6
  2.6 0.7 copy-start.7
  15.7 1.4 %copy-start = (bf16[9216,128]{1,0:T(8,128)(2,1)}, bf16[9216,128]{1,0:T(8,128)(2,1)S(1)}, u32[]{:S(2)}) copy-start(bf16[9216,128]{1,0:T(8,128)(2,1)S(1)} %pack.1) | copy-start | bytes 7077892
  17.1 44.1 %all-to-all-start = ((bf16[128,72,128]{2,1,0:T(8,128)(2,1)}), bf16[128,72,128]{2,1,0:T(8,128)(2,1)S(1)}, u32[]{:S(2)}, u32[]{:S(2)}) async-start(bf16[128,72,128]{2,1,0:T(8,128)(2,1)} %bitcast.26), calls=%async_computation | async-start | bytes 4718592 | tf_op jit(solution)/shard_map/all_to_all | solution.py:344
  28.6 84.0 %copy-start.3 = (bf16[3,3,256,256]{3,2,1,0:T(8,128)(2,1)S(1)}, bf16[3,3,256,256]{3,2,1,0:T(8,128)(2,1)}, u32[]{:S(2)}) copy-start(bf16[3,3,256,256]{3,2,1,0:T(8,128)(2,1)} %param.11) | copy-start | bytes 3538948
  96.7 1.3 %copy-start.1 = (bf16[8192,128]{1,0:T(8,128)(2,1)}, bf16[8192,128]{1,0:T(8,128)(2,1)S(1)}, u32[]{:S(2)}) copy-start(bf16[8192,128]{1,0:T(8,128)(2,1)S(1)} %get-tuple-element.9.cell_ref) | copy-start | bytes 6291460
  98.0 8.5 %collective-permute-start = (bf16[512,128]{1,0:T(8,128)(2,1)S(1)}, bf16[512,128]{1,0:T(8,128)(2,1)S(1)}, u32[]{:S(2)}, u32[]{:S(2)}) collective-permute-start(bf16[512,128]{1,0:T(8,128)(2,1)S(1)} %get-tuple-element.10), channel_id=1, source_target_pairs={{0,16},{16,32},{32,48},{48,64},{64,80},{80,96},{96,112},{1,17},{17... | collective-permute-start | bytes 393224 | tf_op jit(solution)/shard_map/ppermute | solution.py:348
  100.9 5.6 %collective-permute-start.1 = (bf16[256,128]{1,0:T(8,128)(2,1)S(1)}, bf16[256,128]{1,0:T(8,128)(2,1)S(1)}, u32[]{:S(2)}, u32[]{:S(2)}) collective-permute-start(bf16[256,128]{1,0:T(8,128)(2,1)S(1)} %get-tuple-element.11), channel_id=1, source_target_pairs={{16,0},{32,16},{48,32},{64,48},{80,64},{96,80},{112,96},{17,1},{33... | collective-permute-start | bytes 196616 | tf_op jit(solution)/shard_map/ppermute | solution.py:349
  106.6 6.1 %collective-permute-start.2 = (bf16[2,48,128]{2,1,0:T(8,128)(2,1)S(1)}, bf16[2,48,128]{2,1,0:T(8,128)(2,1)S(1)}, u32[]{:S(2)}, u32[]{:S(2)}) collective-permute-start(bf16[2,48,128]{2,1,0:T(8,128)(2,1)S(1)} %pad_maximum_fusion), channel_id=1, source_target_pairs={{0,1},{1,2},{2,3},{3,4},{4,5},{5,6},{6,7},{7,8},{8,9},{9,10},{10,1... | collective-permute-start | bytes 73736 | tf_op jit(solution)/shard_map/ppermute | solution.py:360
  108.0 4.3 %collective-permute-start.3 = (bf16[48,128]{1,0:T(8,128)(2,1)S(1)}, bf16[48,128]{1,0:T(8,128)(2,1)S(1)}, u32[]{:S(2)}, u32[]{:S(2)}) collective-permute-start(bf16[48,128]{1,0:T(8,128)(2,1)S(1)} %get-tuple-element.24.own_ref), channel_id=1, source_target_pairs={{1,0},{2,1},{3,2},{4,3},{5,4},{6,5},{7,6},{8,7},{9,8},{10,9},{11,1... | collective-permute-start | bytes 36872 | tf_op jit(solution)/shard_map/ppermute | solution.py:361
  112.7 1.6 %copy-start.2 = (bf16[8192,128]{1,0:T(8,128)(2,1)S(1)}, bf16[8192,128]{1,0:T(8,128)(2,1)}, u32[]{:S(2)}) copy-start(bf16[8192,128]{1,0:T(8,128)(2,1)} %copy-done.1) | copy-start | bytes 6291460
  114.3 1.1 copy-start.5

commit v2 on v1

--- a/solution.py
+++ b/solution.py
@@ -17,7 +17,8 @@
 BLK = 72
 SEND = DEV * BLK
 TRASH = 256
-GROUP = 32
+GROUP = 8
+PART = 32
 COLS = 48
 F32 = jnp.float32
 BF16 = jnp.bfloat16
@@ -28,7 +29,16 @@
     return (0.5 * x) * (1.0 + jnp.tanh(inner))
 
 
-def pack_kernel(count_ref, dest_ref, cell_ref, val_ref, out_ref, x32, o32, slot_v, slot_s, sem):
+def pack_kernel(
+    count_ref, dest_hbm, cell_hbm, val_hbm, out_hbm,
+    dest_ref, cell_ref, val_ref, o16, x32, o32, slot_v, slot_s, sem, sem_in, sem_out,
+):
+    fetches = [
+        pltpu.make_async_copy(src, dst, sem_in.at[i])
+        for i, (src, dst) in enumerate(((dest_hbm, dest_ref), (cell_hbm, cell_ref), (val_hbm, val_ref)))
+    ]
+    for fetch in fetches:
+        fetch.start()
     count = count_ref[0]
     lane = lax.broadcasted_iota(jnp.int32, (1, 256), 1)
     dest_ids = lax.broadcasted_iota(jnp.int32, (DEV, 256), 0)
@@ -37,6 +47,8 @@
         lax.broadcasted_iota(jnp.int32, (256, 256), 0)
         < lax.broadcasted_iota(jnp.int32, (256, 256), 1)
     ).astype(F32).astype(BF16)
+    fetches[0].wait()
+    fetches[1].wait()
     carry = jnp.zeros((DEV, 1), F32)
     cells = jnp.zeros((DEV, 2 * CAP), F32)
     for a in range(ROWS // 256):
@@ -63,6 +75,7 @@
         )
     to_scalar = pltpu.make_async_copy(slot_v, slot_s, sem)
     to_scalar.start()
+    fetches[2].wait()
 
     def widen(i, c):
         rows = pl.ds(pl.multiple_of(i * 128, 128), 128)
@@ -73,43 +86,58 @@
     to_scalar.wait()
 
     def move(i, c):
-        for k in range(32):
-            slot = slot_s[i // 4, (i % 4) * 32 + k]
-            o32[pl.ds(slot, 1), :] = x32[pl.ds(i * 32 + k, 1), :]
-        return c
-
-    lax.fori_loop(0, ROWS // 32, move, 0)
+        base = pl.multiple_of(i * 128, 128)
+        for k in range(128):
+            o32[pl.ds(slot_s[i, k], 1), :] = x32[pl.ds(base + k, 1), :]
+        return c
+
+    lax.fori_loop(0, ROWS // 128, move, 0)
     for d in range(DEV):
         o32[d * BLK + CAP : d * BLK + CAP + 1, :] = cells[d : d + 1, :]
 
     def narrow(i, c):
         rows = pl.ds(pl.multiple_of(i * 128, 128), 128)
-        out_ref[rows, :] = o32[rows, :].astype(BF16)
-        return c
-
-    lax.fori_loop(0, SEND // 128, narrow, 0)
+        o16[rows, :] = o32[rows, :].astype(BF16)
+        return c
+
+    parts = 4
+    stores = []
+    for p in range(parts):
+        lax.fori_loop(p * SEND // 128 // parts, (p + 1) * SEND // 128 // parts, narrow, 0)
+        rows = pl.ds(p * SEND // parts, SEND // parts)
+        store = pltpu.make_async_copy(o16.at[rows], out_hbm.at[rows], sem_out.at[p])
+        store.start()
+        stores.append(store)
+    for store in stores:
+        store.wait()
 
 
 def pack(obs_values, obs_dest, obs_cell, obs_count):
     return pl.pallas_call(
         pack_kernel,
         out_shape=jax.ShapeDtypeStruct((SEND, CH), BF16),
-        in_specs=[pl.BlockSpec(memory_space=pltpu.SMEM)] + [pl.BlockSpec(memory_space=pltpu.VMEM)] * 3,
-        out_specs=pl.BlockSpec(memory_space=pltpu.VMEM),
+        in_specs=[pl.BlockSpec(memory_space=pltpu.SMEM)] + [pl.BlockSpec(memory_space=pl.ANY)] * 3,
+        out_specs=pl.BlockSpec(memory_space=pl.ANY),
         scratch_shapes=[
+            pltpu.VMEM((32, 128), jnp.int32),
+            pltpu.VMEM((32, 128), jnp.int32),
+            pltpu.VMEM((ROWS, CH), BF16),
+            pltpu.VMEM((SEND, CH), BF16),
             pltpu.VMEM((ROWS, CH), F32),
             pltpu.VMEM((SEND + 8, CH), F32),
             pltpu.VMEM((32, 128), jnp.int32),
             pltpu.SMEM((32, 128), jnp.int32),
             pltpu.SemaphoreType.DMA,
+            pltpu.SemaphoreType.DMA((3,)),
+            pltpu.SemaphoreType.DMA((4,)),
         ],
-        compiler_params=pltpu.CompilerParams(vmem_limit_bytes=40 * 1024 * 1024),
+        compiler_params=pltpu.CompilerParams(vmem_limit_bytes=60 * 1024 * 1024),
         name="pack",
     )(obs_count, obs_dest.reshape(32, 128), obs_cell.reshape(32, 128), obs_values)
 
 
 def grid_kernel(
-    got_ref, out_ref, top_ref, bottom_ref, edge_ref, x32, acc, table_v, table_s, rowpair, colpair, edge32, sem
+    got_ref, out_ref, top_ref, bottom_ref, edge_ref, x32, acc, acc2, table_v, table_s, rowpair, colpair, edge32, sem
 ):
     def widen(i, c):
         rows = pl.ds(pl.multiple_of(i * 128, 128), 128)
@@ -131,10 +159,11 @@
         repeated = repeated | same
     repeated = jnp.where(first & repeated, 1.0, 0.0).astype(BF16)
     groups = (
-        lax.broadcasted_iota(jnp.int32, (128, 128), 0) // GROUP
+        lax.broadcasted_iota(jnp.int32, (128, 128), 0) // PART
         == (lax.broadcasted_iota(jnp.int32, (128, 128), 1) - CAP)
     ).astype(F32).astype(BF16)
-    flags = jnp.dot(repeated, groups, preferred_element_type=F32).astype(jnp.int32)
+    flags = jnp.dot(repeated, groups, preferred_element_type=F32)
+    flags = (flags + pltpu.roll(flags, DEV // 2, axis=0)).astype(jnp.int32)
     table_v[...] = jnp.where(first, index, flags)
     to_scalar = pltpu.make_async_copy(table_v, table_s, sem)
     to_scalar.start()
@@ -143,52 +172,65 @@
     firsth = lax.broadcasted_iota(jnp.int32, (half, 128), 1) < CAP
     rowpair[...] = jnp.where(firsth, cells[:half], swapped[half:])
     colpair[...] = jnp.where(firsth, swapped[:half], cells[half:])
+    batch = 8
     col_ids = lax.broadcasted_iota(jnp.int32, (TW, 128), 0).astype(F32)
     row_ids = (lax.broadcasted_iota(jnp.int32, (128, 128), 0) + 1).astype(F32)
 
     def tally(i, total):
-        col_hot = (col_ids == colpair[pl.ds(i, 1), :]).astype(F32).astype(BF16)
-        row_hot = (row_ids == rowpair[pl.ds(i, 1), :]).astype(F32).astype(BF16)
+        at = [pl.ds(i * batch + k, 1) for k in range(batch)]
+        col_hot = jnp.concatenate(
+            [(col_ids == colpair[r, :]).astype(F32).astype(BF16) for r in at], axis=1
+        )
+        row_hot = jnp.concatenate(
+            [(row_ids == rowpair[r, :]).astype(F32).astype(BF16) for r in at], axis=1
+        )
         return total + lax.dot_general(
             col_hot, row_hot, (((1,), (1,)), ((), ())), preferred_element_type=F32
         )
 
-    tallies = lax.fori_loop(0, half, tally, jnp.zeros((TW, 128), F32))
+    tallies = lax.fori_loop(0, half // batch, tally, jnp.zeros((TW, 128), F32))
     inverse = 1.0 / jnp.maximum(tallies, 1.0)
 
     def clear(i, c):
         acc[pl.ds(pl.multiple_of(i * 128, 128), 128), :] = jnp.zeros((128, CH), F32)
+        acc2[pl.ds(pl.multiple_of(i * 128, 128), 128), :] = jnp.zeros((128, CH), F32)
         return c
 
     lax.fori_loop(0, (TRASH + TH * TW) // 128, clear, 0)
     to_scalar.wait()
 
     def source(s, c):
-        for g in range(CAP // GROUP):
-            clash = table_s[s, CAP + g]
+        pairs = ((acc, s), (acc2, s + half))
+        for p in range(CAP // PART):
+            clash = table_s[s, CAP + p]
 
             @pl.when(clash == 0)
             def _():
-                index = [table_s[s, g * GROUP + k] for k in range(GROUP)]
-                sums = [
-                    acc[pl.ds(index[k], 1), :] + x32[pl.ds(s * BLK + g * GROUP + k, 1), :]
-                    for k in range(GROUP)
-                ]
-                for k in range(GROUP):
-                    acc[pl.ds(index[k], 1), :] = sums[k]
+                for g in range(p * PART // GROUP, (p + 1) * PART // GROUP):
+                    slots = range(g * GROUP, (g + 1) * GROUP)
+                    index = [[pl.ds(table_s[t, k], 1) for k in slots] for _, t in pairs]
+                    sums = [
+                        [a[at, :] + x32[pl.ds(t * BLK + k, 1), :] for at, k in zip(ix, slots)]
+                        for (a, t), ix in zip(pairs, index)
+                    ]
+                    for (a, _), ix, new in zip(pairs, index, sums):
+                        for at, value in zip(ix, new):
+                            a[at, :] = value
 
             @pl.when(clash != 0)
             def _():
-                for k in range(GROUP):
-                    at = pl.ds(table_s[s, g * GROUP + k], 1)
-                    acc[at, :] = acc[at, :] + x32[pl.ds(s * BLK + g * GROUP + k, 1), :]
-
-        return c
-
-    lax.fori_loop(0, DEV, source, 0)
+                for k in range(p * PART, (p + 1) * PART):
+                    for a, t in pairs:
+                        at = pl.ds(table_s[t, k], 1)
+                        a[at, :] = a[at, :] + x32[pl.ds(t * BLK + k, 1), :]
+
+        return c
+
+    lax.fori_loop(0, half, source, 0)
     for i in range(TH):
         scale = jnp.broadcast_to(inverse[:, i : i + 1], (TW, CH))
-        mean = acc[TRASH + i * TW : TRASH + (i + 1) * TW, :] * scale
+        rows = slice(TRASH + i * TW, TRASH + (i + 1) * TW)
+        mean = (acc[rows, :] + acc2[rows, :]) * scale
         out_ref[i * TW : (i + 1) * TW, :] = mean.astype(BF16)
         if i == 0:
             top_ref[...] = mean.astype(BF16)
@@ -210,6 +252,7 @@
         scratch_shapes=[
             pltpu.VMEM((SEND, CH), F32),
             pltpu.VMEM((TRASH + TH * TW, CH), F32),
+            pltpu.VMEM((TRASH + TH * TW, CH), F32),
             pltpu.VMEM((DEV, 128), jnp.int32),
             pltpu.SMEM((DEV, 128), jnp.int32),
             pltpu.VMEM((DEV // 2, 128), F32),
@@ -217,7 +260,7 @@
             pltpu.VMEM((3, TH, CH), F32),
             pltpu.SemaphoreType.DMA,
         ],
-        compiler_params=pltpu.CompilerParams(vmem_limit_bytes=40 * 1024 * 1024),
+        compiler_params=pltpu.CompilerParams(vmem_limit_bytes=24 * 1024 * 1024),
         name="to_grid",
     )(got)
 
@@ -332,7 +375,7 @@
             pltpu.VMEM((COLS, CH), F32),
             pltpu.VMEM((40, HID), F32),
         ],
-        compiler_params=pltpu.CompilerParams(vmem_limit_bytes=48 * 1024 * 1024),
+        compiler_params=pltpu.CompilerParams(vmem_limit_bytes=24 * 1024 * 1024),
         name="convolve",
     )(band, cells, north, south, own, west, east, w1, w2)
 

time: 131 us -> 104 us (0.79)
  Pallas kernels: 63.2 us -> 39.5 us
  local copies, waits for them, and re-layouts: 8.17 us -> 4.09 us
    pallas_call x1, Pallas kernels: 35.4 us -> 16.5 us  [to_grid(): pl.pallas_call(grid_kernel, out_shape=[jax.ShapeDtypeStruct(s, BF16) for...]
    pallas_call x1, Pallas kernels: 12.4 us -> 7.72 us  [pack(): pl.pallas_call(pack_kernel, out_shape=jax.ShapeDtypeStruct((SEND, CH), BF...]
    unnamed x17 -> x9, local copies, waits for them, and re-layouts: 8.07 us -> 3.99 us
where the time goes in v2:
time: 104 us; the launch traced here: 103 us
  Pallas kernels  39.5 us (38%)
  waiting for transfers between devices  37.3 us (36%)
  starting transfers between devices  21.3 us (20%)
  local copies, waits for them, and re-layouts  4.09 us (4%)
    all_to_all x1, waiting for transfers between devices, body(): lax.all_to_all(send.reshape(DEV, BLK, CH), ('lat', 'lon'), split_axis=0,...  32.5 us
    pallas_call x1, Pallas kernels, to_grid(): pl.pallas_call(grid_kernel, out_shape=[jax.ShapeDtypeStruct(s, BF16) for...  16.5 us
    pallas_call x1, Pallas kernels, convolve(): pl.pallas_call(conv_kernel, out_shape=jax.ShapeDtypeStruct((TH // 2, TW /...  15.3 us
    all_to_all x1, starting transfers between devices, body(): lax.all_to_all(send.reshape(DEV, BLK, CH), ('lat', 'lon'), split_axis=0,...  11.5 us
    pallas_call x1, Pallas kernels, pack(): pl.pallas_call(pack_kernel, out_shape=jax.ShapeDtypeStruct((SEND, CH), BF...  7.72 us
    ppermute x1, starting transfers between devices, body(): east = lax.ppermute(own, 'lon', [((i + 1) % lon, i) for i in range(lon)])  4.1 us
    unnamed x9, local copies, waits for them, and re-layouts  3.99 us
    ppermute x1, waiting for transfers between devices, body(): south = lax.ppermute(top, 'lat', [(i + 1, i) for i in range(lat - 1)])  3.64 us
  transfers between devices with their start and end apart: 5, of which 4 were waited for; matrix products, arithmetic and copies ran while one was open for 0% of the time, Pallas kernels for 0%

profile of v2, /device:TPU:1, one launch (start us, length us, event | category | flops | bytes accessed | tf_op | source)
XLA Modules:
  0.0 103.1 jit_solution(12905518801124913949)
XLA Ops:
  0.7 7.7 %pack.1 = bf16[9216,128]{1,0:T(8,128)(2,1)} custom-call(s32[1]{0:T(128)S(6)} %copy.17.count_ref, s32[32,128]{1,0:T(8,128)} %bitcast.30, s32[32,128]{1,0:T(8,128)} %bitcast.31, bf16[4096,128]{1,0:T(8,128)(2,1)} %val_hbm.1), custom_call_target="tpu_custom_call" | custom-call | tf_op jit(solution)/shard_map/pack/pallas_call | solution.py:116
  8.4 11.5 %all-to-all-start = ((bf16[128,72,128]{2,1,0:T(8,128)(2,1)}), bf16[128,72,128]{2,1,0:T(8,128)(2,1)S(1)}, u32[]{:S(2)}, u32[]{:S(2)}) async-start(bf16[128,72,128]{2,1,0:T(8,128)(2,1)} %bitcast.29), calls=%async_computation | async-start | bytes 4718592 | tf_op jit(solution)/shard_map/all_to_all | solution.py:387
  19.9 0.0 copy-start.2
  19.9 0.1 pad.13.clone
  20.0 32.5 %all-to-all-done = bf16[128,72,128]{2,1,0:T(8,128)(2,1)S(1)} async-done(((bf16[128,72,128]{2,1,0:T(8,128)(2,1)}), bf16[128,72,128]{2,1,0:T(8,128)(2,1)S(1)}, u32[]{:S(2)}, u32[]{:S(2)}) %all-to-all-start) | async-done | bytes 2359328 | tf_op jit(solution)/shard_map/all_to_all | solution.py:387
  52.5 16.5 %to_grid.1 = (bf16[8192,128]{1,0:T(8,128)(2,1)S(1)}, bf16[256,128]{1,0:T(8,128)(2,1)S(1)}, bf16[512,128]{1,0:T(8,128)(2,1)S(1)}, bf16[3,32,128]{2,1,0:T(8,128)(2,1)S(1)}) custom-call(bf16[9216,128]{1,0:T(8,128)(2,1)S(1)} %bitcast.25), custom_call_target="tpu_custom_call" | custom-call | tf_op jit(solution)/shard_map/to_grid/pallas_call | solution.py:247
  68.9 0.0 copy-start
  68.9 1.3 %copy-done = bf16[8192,128]{1,0:T(8,128)(2,1)} copy-done((bf16[8192,128]{1,0:T(8,128)(2,1)}, bf16[8192,128]{1,0:T(8,128)(2,1)S(1)}, u32[]{:S(2)}) %copy-start) | copy-done | bytes 2097176
  70.3 3.1 %collective-permute-start = (bf16[512,128]{1,0:T(8,128)(2,1)S(1)}, bf16[512,128]{1,0:T(8,128)(2,1)S(1)}, u32[]{:S(2)}, u32[]{:S(2)}) collective-permute-start(bf16[512,128]{1,0:T(8,128)(2,1)S(1)} %get-tuple-element.10), channel_id=1, source_target_pairs={{0,16},{16,32},{32,48},{48,64},{64,80},{80,96},{96,112},{1,17},{17... | collective-permute-start | bytes 393224 | tf_op jit(solution)/shard_map/ppermute | solution.py:391
  73.3 1.9 %collective-permute-start.1 = (bf16[256,128]{1,0:T(8,128)(2,1)S(1)}, bf16[256,128]{1,0:T(8,128)(2,1)S(1)}, u32[]{:S(2)}, u32[]{:S(2)}) collective-permute-start(bf16[256,128]{1,0:T(8,128)(2,1)S(1)} %get-tuple-element.11), channel_id=1, source_target_pairs={{16,0},{32,16},{48,32},{64,48},{80,64},{96,80},{112,96},{17,1},{33... | collective-permute-start | bytes 196616 | tf_op jit(solution)/shard_map/ppermute | solution.py:392
  75.3 3.6 %collective-permute-done.1.south_ref = bf16[256,128]{1,0:T(8,128)(2,1)S(1)} collective-permute-done((bf16[256,128]{1,0:T(8,128)(2,1)S(1)}, bf16[256,128]{1,0:T(8,128)(2,1)S(1)}, u32[]{:S(2)}, u32[]{:S(2)}) %collective-permute-start.1) | collective-permute-done | bytes 65568 | tf_op jit(solution)/shard_map/ppermute | solution.py:392
  78.9 0.0 collective-permute-done.north_ref
  79.0 0.1 maximum_bitcast_fusion
  79.1 0.8 collective-permute-start.2
  79.8 4.1 %collective-permute-start.3 = (bf16[48,128]{1,0:T(8,128)(2,1)S(1)}, bf16[48,128]{1,0:T(8,128)(2,1)S(1)}, u32[]{:S(2)}, u32[]{:S(2)}) collective-permute-start(bf16[48,128]{1,0:T(8,128)(2,1)S(1)} %get-tuple-element.24.own_ref), channel_id=1, source_target_pairs={{1,0},{2,1},{3,2},{4,3},{5,4},{6,5},{7,6},{8,7},{9,8},{10,9},{11,1... | collective-permute-start | bytes 36872 | tf_op jit(solution)/shard_map/ppermute | solution.py:404
  83.9 0.8 collective-permute-done.3.east_ref
  84.7 0.4 collective-permute-done.2.west_ref
  85.1 0.0 copy-done.2
  85.1 0.0 copy-start.1
  85.1 1.6 %copy-done.1 = bf16[8192,128]{1,0:T(8,128)(2,1)S(1)} copy-done((bf16[8192,128]{1,0:T(8,128)(2,1)S(1)}, bf16[8192,128]{1,0:T(8,128)(2,1)}, u32[]{:S(2)}) %copy-start.1) | copy-done | bytes 2097176
  86.7 0.0 copy-start.3
  86.7 1.1 %copy-done.3 = bf16[3,3,128,256]{3,2,1,0:T(8,128)(2,1)S(1)} copy-done((bf16[3,3,128,256]{3,2,1,0:T(8,128)(2,1)S(1)}, bf16[3,3,128,256]{3,2,1,0:T(8,128)(2,1)}, u32[]{:S(2)}) %copy-start.3) | copy-done | bytes 589848
  87.8 15.3 %convolve.1 = bf16[16,128,256]{2,1,0:T(8,128)(2,1)} custom-call(s32[1]{0:T(128)} %bitcast.band_ref, bf16[8192,128]{1,0:T(8,128)(2,1)S(1)} %copy-done.1, bf16[512,128]{1,0:T(8,128)(2,1)S(1)} %collective-permute-done.north_ref, bf16[256,128]{1,0:T(8,128)(2,1)S(1)} %collective-permute-done.1.south_ref, bf16[48,128]{1,0:T(8,128)(2,1)S(1)} %get-tuple-element.24.own_ref, ...), custom_call_target="tpu_custom_call" | custom-call | tf_op jit(solution)/shard_map/convolve/pallas_call | solution.py:365
  (7 shorter events, 0.0 us)
Async XLA Ops:
  8.4 44.1 %all-to-all-start = ((bf16[128,72,128]{2,1,0:T(8,128)(2,1)}), bf16[128,72,128]{2,1,0:T(8,128)(2,1)S(1)}, u32[]{:S(2)}, u32[]{:S(2)}) async-start(bf16[128,72,128]{2,1,0:T(8,128)(2,1)} %bitcast.29), calls=%async_computation | async-start | bytes 4718592 | tf_op jit(solution)/shard_map/all_to_all | solution.py:387
  19.9 65.2 %copy-start.2 = (bf16[3,3,256,256]{3,2,1,0:T(8,128)(2,1)S(1)}, bf16[3,3,256,256]{3,2,1,0:T(8,128)(2,1)}, u32[]{:S(2)}) copy-start(bf16[3,3,256,256]{3,2,1,0:T(8,128)(2,1)} %param.11) | copy-start | bytes 3538948
  68.9 1.3 %copy-start = (bf16[8192,128]{1,0:T(8,128)(2,1)}, bf16[8192,128]{1,0:T(8,128)(2,1)S(1)}, u32[]{:S(2)}) copy-start(bf16[8192,128]{1,0:T(8,128)(2,1)S(1)} %get-tuple-element.9.cell_ref) | copy-start | bytes 6291460
  70.3 8.7 %collective-permute-start = (bf16[512,128]{1,0:T(8,128)(2,1)S(1)}, bf16[512,128]{1,0:T(8,128)(2,1)S(1)}, u32[]{:S(2)}, u32[]{:S(2)}) collective-permute-start(bf16[512,128]{1,0:T(8,128)(2,1)S(1)} %get-tuple-element.10), channel_id=1, source_target_pairs={{0,16},{16,32},{32,48},{48,64},{64,80},{80,96},{96,112},{1,17},{17... | collective-permute-start | bytes 393224 | tf_op jit(solution)/shard_map/ppermute | solution.py:391
  73.3 5.6 %collective-permute-start.1 = (bf16[256,128]{1,0:T(8,128)(2,1)S(1)}, bf16[256,128]{1,0:T(8,128)(2,1)S(1)}, u32[]{:S(2)}, u32[]{:S(2)}) collective-permute-start(bf16[256,128]{1,0:T(8,128)(2,1)S(1)} %get-tuple-element.11), channel_id=1, source_target_pairs={{16,0},{32,16},{48,32},{64,48},{80,64},{96,80},{112,96},{17,1},{33... | collective-permute-start | bytes 196616 | tf_op jit(solution)/shard_map/ppermute | solution.py:392
  79.1 6.1 %collective-permute-start.2 = (bf16[2,48,128]{2,1,0:T(8,128)(2,1)S(1)}, bf16[2,48,128]{2,1,0:T(8,128)(2,1)S(1)}, u32[]{:S(2)}, u32[]{:S(2)}) collective-permute-start(bf16[2,48,128]{2,1,0:T(8,128)(2,1)S(1)} %pad_maximum_fusion), channel_id=1, source_target_pairs={{0,1},{1,2},{2,3},{3,4},{4,5},{5,6},{6,7},{7,8},{8,9},{9,10},{10,1... | collective-permute-start | bytes 73736 | tf_op jit(solution)/shard_map/ppermute | solution.py:403
  79.8 4.9 %collective-permute-start.3 = (bf16[48,128]{1,0:T(8,128)(2,1)S(1)}, bf16[48,128]{1,0:T(8,128)(2,1)S(1)}, u32[]{:S(2)}, u32[]{:S(2)}) collective-permute-start(bf16[48,128]{1,0:T(8,128)(2,1)S(1)} %get-tuple-element.24.own_ref), channel_id=1, source_target_pairs={{1,0},{2,1},{3,2},{4,3},{5,4},{6,5},{7,6},{8,7},{9,8},{10,9},{11,1... | collective-permute-start | bytes 36872 | tf_op jit(solution)/shard_map/ppermute | solution.py:404
  85.1 1.6 %copy-start.1 = (bf16[8192,128]{1,0:T(8,128)(2,1)S(1)}, bf16[8192,128]{1,0:T(8,128)(2,1)}, u32[]{:S(2)}) copy-start(bf16[8192,128]{1,0:T(8,128)(2,1)} %copy-done) | copy-start | bytes 6291460
  86.7 1.1 %copy-start.3 = (bf16[3,3,128,256]{3,2,1,0:T(8,128)(2,1)S(1)}, bf16[3,3,128,256]{3,2,1,0:T(8,128)(2,1)}, u32[]{:S(2)}) copy-start(bf16[3,3,128,256]{3,2,1,0:T(8,128)(2,1)} %param.10) | copy-start | bytes 1769476

commit v3 on v2

--- a/solution.py
+++ b/solution.py
@@ -14,11 +14,13 @@
 DEV = 128
 CAP = 64
 ROWS = 4096
-BLK = 72
+BLK = 66
 SEND = DEV * BLK
 TRASH = 256
 GROUP = 8
 PART = 32
+FIRST = 11
+SECOND = 8
 COLS = 48
 F32 = jnp.float32
 BF16 = jnp.bfloat16
@@ -51,6 +53,7 @@
     fetches[1].wait()
     carry = jnp.zeros((DEV, 1), F32)
     cells = jnp.zeros((DEV, 2 * CAP), F32)
+    slots = []
     for a in range(ROWS // 256):
         dest = jnp.concatenate([dest_ref[2 * a : 2 * a + 1], dest_ref[2 * a + 1 : 2 * a + 2]], axis=1)
         cell = jnp.concatenate([cell_ref[2 * a : 2 * a + 1], cell_ref[2 * a + 1 : 2 * a + 2]], axis=1)
@@ -62,8 +65,7 @@
         carry = carry + jnp.sum(hot, axis=1, keepdims=True)
         pos = jnp.sum(hot * before, axis=0, keepdims=True).astype(jnp.int32)
         slot = jnp.where(live, dest * BLK + pos, SEND)
-        slot_v[2 * a : 2 * a + 1] = slot[:, :128]
-        slot_v[2 * a + 1 : 2 * a + 2] = slot[:, 128:]
+        slots += [slot[:, :128], slot[:, 128:]]
         high = (cell // TW + 1).astype(F32)
         low = ((cell % 16) * 16 + (cell % TW) // 16).astype(F32)
         pos_hot = pos_ids == pos
@@ -73,6 +75,8 @@
         cells = cells + lax.dot_general(
             hot16, coded, (((1,), (1,)), ((), ())), preferred_element_type=F32
         )
+    slots = jnp.concatenate(slots + [jnp.zeros((96, 128), jnp.int32)], axis=0)
+    slot_v[...] = slots.T
     to_scalar = pltpu.make_async_copy(slot_v, slot_s, sem)
     to_scalar.start()
     fetches[2].wait()
@@ -88,7 +92,7 @@
     def move(i, c):
         base = pl.multiple_of(i * 128, 128)
         for k in range(128):
-            o32[pl.ds(slot_s[i, k], 1), :] = x32[pl.ds(base + k, 1), :]
+            o32[pl.ds(slot_s.at[k][i], 1), :] = x32[pl.ds(base + k, 1), :]
         return c
 
     lax.fori_loop(0, ROWS // 128, move, 0)
@@ -100,7 +104,7 @@
         o16[rows, :] = o32[rows, :].astype(BF16)
         return c
 
-    parts = 4
+    parts = 3
     stores = []
     for p in range(parts):
         lax.fori_loop(p * SEND // 128 // parts, (p + 1) * SEND // 128 // parts, narrow, 0)
@@ -125,11 +129,11 @@
             pltpu.VMEM((SEND, CH), BF16),
             pltpu.VMEM((ROWS, CH), F32),
             pltpu.VMEM((SEND + 8, CH), F32),
-            pltpu.VMEM((32, 128), jnp.int32),
-            pltpu.SMEM((32, 128), jnp.int32),
+            pltpu.VMEM((128, 128), jnp.int32),
+            pltpu.SMEM((128, 128), jnp.int32),
             pltpu.SemaphoreType.DMA,
             pltpu.SemaphoreType.DMA((3,)),
-            pltpu.SemaphoreType.DMA((4,)),
+            pltpu.SemaphoreType.DMA((3,)),
         ],
         compiler_params=pltpu.CompilerParams(vmem_limit_bytes=60 * 1024 * 1024),
         name="pack",
@@ -137,14 +141,24 @@
 
 
 def grid_kernel(
-    got_ref, out_ref, top_ref, bottom_ref, edge_ref, x32, acc, acc2, table_v, table_s, rowpair, colpair, edge32, sem
+    got_ref, out_hbm, top_ref, bottom_ref, edge_ref,
+    out_ref, x32, acc, acc2, table_v, table_s, rowpair, colpair, edge32, sem, sem_out,
 ):
+    parts = 4
+
+    def clear(i, c):
+        acc[pl.ds(pl.multiple_of(i * 128, 128), 128), :] = jnp.zeros((128, CH), F32)
+        acc2[pl.ds(pl.multiple_of(i * 128, 128), 128), :] = jnp.zeros((128, CH), F32)
+        return c
+
+    lax.fori_loop(0, (TRASH + TH * TW) // 128, clear, 0)
+
     def widen(i, c):
-        rows = pl.ds(pl.multiple_of(i * 128, 128), 128)
+        rows = pl.ds(pl.multiple_of(i * 192, 192), 192)
         x32[rows, :] = got_ref[rows, :].astype(F32)
         return c
 
-    lax.fori_loop(0, SEND // 128, widen, 0)
+    lax.fori_loop(0, SEND // 192, widen, 0)
     cells = jnp.concatenate([x32[s * BLK + CAP : s * BLK + CAP + 1, :] for s in range(DEV)], axis=0)
     swapped = pltpu.roll(cells, CAP, axis=1)
     lane = lax.broadcasted_iota(jnp.int32, (DEV, 128), 1)
@@ -164,7 +178,7 @@
     ).astype(F32).astype(BF16)
     flags = jnp.dot(repeated, groups, preferred_element_type=F32)
     flags = (flags + pltpu.roll(flags, DEV // 2, axis=0)).astype(jnp.int32)
-    table_v[...] = jnp.where(first, index, flags)
+    table_v[...] = jnp.where(first, index, flags).T
     to_scalar = pltpu.make_async_copy(table_v, table_s, sem)
     to_scalar.start()
 
@@ -191,24 +205,18 @@
     tallies = lax.fori_loop(0, half // batch, tally, jnp.zeros((TW, 128), F32))
     inverse = 1.0 / jnp.maximum(tallies, 1.0)
 
-    def clear(i, c):
-        acc[pl.ds(pl.multiple_of(i * 128, 128), 128), :] = jnp.zeros((128, CH), F32)
-        acc2[pl.ds(pl.multiple_of(i * 128, 128), 128), :] = jnp.zeros((128, CH), F32)
-        return c
-
-    lax.fori_loop(0, (TRASH + TH * TW) // 128, clear, 0)
     to_scalar.wait()
 
     def source(s, c):
         pairs = ((acc, s), (acc2, s + half))
         for p in range(CAP // PART):
-            clash = table_s[s, CAP + p]
+            clash = table_s.at[CAP + p][s]
 
             @pl.when(clash == 0)
             def _():
                 for g in range(p * PART // GROUP, (p + 1) * PART // GROUP):
                     slots = range(g * GROUP, (g + 1) * GROUP)
-                    index = [[pl.ds(table_s[t, k], 1) for k in slots] for _, t in pairs]
+                    index = [[pl.ds(table_s.at[k][t], 1) for k in slots] for _, t in pairs]
                     sums = [
                         [a[at, :] + x32[pl.ds(t * BLK + k, 1), :] for at, k in zip(ix, slots)]
                         for (a, t), ix in zip(pairs, index)
@@ -221,12 +229,13 @@
             def _():
                 for k in range(p * PART, (p + 1) * PART):
                     for a, t in pairs:
-                        at = pl.ds(table_s[t, k], 1)
+                        at = pl.ds(table_s.at[k][t], 1)
                         a[at, :] = a[at, :] + x32[pl.ds(t * BLK + k, 1), :]
 
         return c
 
     lax.fori_loop(0, half, source, 0)
+    stores = []
     for i in range(TH):
         scale = jnp.broadcast_to(inverse[:, i : i + 1], (TW, CH))
         rows = slice(TRASH + i * TW, TRASH + (i + 1) * TW)
@@ -239,7 +248,15 @@
         edge32[0, i : i + 1, :] = mean[0:1]
         edge32[1, i : i + 1, :] = mean[239:240]
         edge32[2, i : i + 1, :] = mean[255:256]
+        if (i + 1) % (TH // parts) == 0:
+            p = i // (TH // parts)
+            rows = pl.ds(p * (TH // parts) * TW, (TH // parts) * TW)
+            store = pltpu.make_async_copy(out_ref.at[rows], out_hbm.at[rows], sem_out.at[p])
+            store.start()
+            stores.append(store)
     edge_ref[...] = edge32[...].astype(BF16)
+    for store in stores:
+        store.wait()
 
 
 def to_grid(got):
@@ -248,8 +265,9 @@
         grid_kernel,
         out_shape=[jax.ShapeDtypeStruct(s, BF16) for s in shapes],
         in_specs=[pl.BlockSpec(memory_space=pltpu.VMEM)],
-        out_specs=[pl.BlockSpec(memory_space=pltpu.VMEM)] * 4,
+        out_specs=[pl.BlockSpec(memory_space=pl.ANY)] + [pl.BlockSpec(memory_space=pltpu.VMEM)] * 3,
         scratch_shapes=[
+            pltpu.VMEM((TH * TW, CH), BF16),
             pltpu.VMEM((SEND, CH), F32),
             pltpu.VMEM((TRASH + TH * TW, CH), F32),
             pltpu.VMEM((TRASH + TH * TW, CH), F32),
@@ -259,25 +277,32 @@
             pltpu.VMEM((DEV // 2, 128), F32),
             pltpu.VMEM((3, TH, CH), F32),
             pltpu.SemaphoreType.DMA,
+            pltpu.SemaphoreType.DMA((4,)),
         ],
-        compiler_params=pltpu.CompilerParams(vmem_limit_bytes=24 * 1024 * 1024),
+        compiler_params=pltpu.CompilerParams(vmem_limit_bytes=60 * 1024 * 1024),
         name="to_grid",
     )(got)
 
 
 def conv_kernel(
-    band_ref, cell_ref, north_ref, south_ref, own_ref, west_ref, east_ref, w1_ref, w2_ref, out_ref,
-    field, even, odd, wcol, ecol, hcol,
+    band_ref, cell_hbm, north_hbm, south_hbm, own_hbm, west_hbm, east_hbm, w1_hbm, w2_hbm, out_ref,
+    field, even, odd, own_ref, west_ref, east_ref, wcol, ecol, hcol, w1_ref, w2_ref, o32, sem,
 ):
-    field[0:2, 1:17] = north_ref[...].reshape(2, 16, 16, CH)
-    field[2 + TH, 1:17] = south_ref[...].reshape(16, 16, CH)
-
-    def place(i, c):
-        rows = pl.ds(pl.multiple_of(i * TW, TW), TW)
-        field[2 + i, 1:17] = cell_ref[rows, :].reshape(16, 16, CH)
-        return c
-
-    lax.fori_loop(0, TH, place, 0)
+    pairs = (
+        (west_hbm, west_ref),
+        (east_hbm, east_ref),
+        (own_hbm, own_ref),
+        (north_hbm, field.at[pl.ds(0, 2), pl.ds(1, 16)]),
+        (south_hbm, field.at[2 + TH, pl.ds(1, 16)]),
+        (cell_hbm, field.at[pl.ds(2, TH), pl.ds(1, 16)]),
+        (w1_hbm, w1_ref),
+        (w2_hbm, w2_ref),
+    )
+    fetches = [pltpu.make_async_copy(src, dst, sem.at[i]) for i, (src, dst) in enumerate(pairs)]
+    for fetch in fetches:
+        fetch.start()
+    for fetch in fetches[:6]:
+        fetch.wait()
     wcol[...] = west_ref[1].astype(F32)
     ecol[...] = east_ref[...].astype(F32)
     sub = lax.broadcasted_iota(jnp.int32, (16, CH), 0)
@@ -289,7 +314,8 @@
         field[r, 17] = jnp.where(sub == 15, ecol[pl.ds(r, 1), :], after).astype(BF16)
         return c
 
-    lax.fori_loop(0, TH + 3, wrap, 0)
+    lax.fori_loop(0, TH + 3, wrap, 0, unroll=5)
+    fetches[6].wait()
 
     taps = [west_ref[0].astype(F32), west_ref[1].astype(F32), own_ref[...].astype(F32)]
     lhs = jnp.concatenate([taps[b][a : a + 40] for a in range(3) for b in range(3)], axis=1)
@@ -299,38 +325,30 @@
     def first(step, c):
         lhs = jnp.concatenate(
             [
-                jnp.concatenate(
-                    [
-                        field[3 * step + r + a, b : b + 16].reshape(TW, CH)
-                        for a in range(3)
-                        for b in range(3)
-                    ],
-                    axis=1,
-                )
-                for r in range(3)
+                field[pl.ds(FIRST * step + a, FIRST), b : b + 16].reshape(FIRST * TW, CH)
+                for a in range(3)
+                for b in range(3)
             ],
-            axis=0,
+            axis=1,
         )
         y = gelu(jnp.dot(lhs, w1_ref[...], preferred_element_type=F32))
-        y16 = y.astype(BF16).reshape(3, 8, 2, 16, HID)
-        for r in range(3):
-            hr = 3 * step + r
+        y16 = y.astype(BF16).reshape(FIRST, 8, 2, 16, HID)
+        for r in range(FIRST):
+            hr = FIRST * step + r
             odd[hr] = y16[r, :, 0]
             even[hr, 1:9] = y16[r, :, 1]
             before = pltpu.roll(y[r * TW + 240 : r * TW + 256], 1, axis=0)
             even[hr, 0] = jnp.where(sub2 == 0, hcol[pl.ds(hr, 1), :], before).astype(BF16)
         return c
 
-    lax.fori_loop(0, 11, first, 0)
+    lax.fori_loop(0, (TH + 1) // FIRST, first, 0)
 
     @pl.when(band_ref[0] == 0)
     def _():
         even[0] = jnp.zeros((9, 16, HID), BF16)
         odd[0] = jnp.zeros((8, 16, HID), BF16)
 
-    out_row = lax.broadcasted_iota(jnp.int32, (128, 128), 0)
-    out_col = lax.broadcasted_iota(jnp.int32, (128, 128), 1)
-    order = ((out_row % 8) * 16 + out_row // 8 == out_col).astype(F32).astype(BF16)
+    fetches[7].wait()
 
     def second(step, c):
         lhs = jnp.concatenate(
@@ -340,44 +358,57 @@
                         x.reshape(128, HID)
                         for a in range(3)
                         for x in (
-                            even[4 * step + 2 * r + a, 0:8],
-                            odd[4 * step + 2 * r + a],
-                            even[4 * step + 2 * r + a, 1:9],
+                            even[2 * (SECOND * step + r) + a, 0:8],
+                            odd[2 * (SECOND * step + r) + a],
+                            even[2 * (SECOND * step + r) + a, 1:9],
                         )
                     ],
                     axis=1,
                 )
-                for r in range(2)
+                for r in range(SECOND)
             ],
             axis=0,
         )
-        y = gelu(jnp.dot(lhs, w2_ref[...], preferred_element_type=F32)).astype(BF16)
-        for r in range(2):
-            out_ref[2 * step + r] = jnp.dot(
-                order, y[r * 128 : (r + 1) * 128], preferred_element_type=F32
-            ).astype(BF16)
-        return c
-
-    lax.fori_loop(0, TH // 4, second, 0)
+        y = gelu(jnp.dot(lhs, w2_ref[...], preferred_element_type=F32))
+        for r in range(SECOND):
+            for h in range(2):
+                for t in range(8):
+                    o32[r, h, pl.ds(t, 16, stride=8), :] = y[
+                        r * 128 + t * 16 : r * 128 + (t + 1) * 16, h * 128 : (h + 1) * 128
+                    ]
+            out_ref[SECOND * step + r] = jnp.concatenate([o32[r, 0], o32[r, 1]], axis=1).astype(BF16)
+        return c
+
+    lax.fori_loop(0, TH // 2 // SECOND, second, 0)
 
 
 def convolve(band, cells, north, south, own, west, east, w1, w2):
     return pl.pallas_call(
         conv_kernel,
         out_shape=jax.ShapeDtypeStruct((TH // 2, TW // 2, HID), BF16),
-        in_specs=[pl.BlockSpec(memory_space=pltpu.SMEM)] + [pl.BlockSpec(memory_space=pltpu.VMEM)] * 8,
+        in_specs=[pl.BlockSpec(memory_space=pltpu.SMEM)] + [pl.BlockSpec(memory_space=pl.ANY)] * 8,
         out_specs=pl.BlockSpec(memory_space=pltpu.VMEM),
         scratch_shapes=[
             pltpu.VMEM((TH + 3, 18, 16, CH), BF16),
             pltpu.VMEM((TH + 1, 9, 16, HID), BF16),
             pltpu.VMEM((TH + 1, 8, 16, HID), BF16),
+            pltpu.VMEM((COLS, CH), BF16),
+            pltpu.VMEM((2, COLS, CH), BF16),
+            pltpu.VMEM((COLS, CH), BF16),
             pltpu.VMEM((COLS, CH), F32),
             pltpu.VMEM((COLS, CH), F32),
             pltpu.VMEM((40, HID), F32),
+            pltpu.VMEM((9 * CH, HID), BF16),
+            pltpu.VMEM((9 * HID, HID), BF16),
+            pltpu.VMEM((SECOND, 2, TW // 2, 128), F32),
+            pltpu.SemaphoreType.DMA((8,)),
         ],
-        compiler_params=pltpu.CompilerParams(vmem_limit_bytes=24 * 1024 * 1024),
+        compiler_params=pltpu.CompilerParams(vmem_limit_bytes=56 * 1024 * 1024),
         name="convolve",
-    )(band, cells, north, south, own, west, east, w1, w2)
+    )(
+        band, cells.reshape(TH, 16, 16, CH), north.reshape(2, 16, 16, CH), south.reshape(16, 16, CH),
+        own, west, east, w1, w2,
+    )
 
 
 def body(obs_values, obs_dest, obs_cell, obs_count, conv_in, conv_down):
@@ -385,7 +416,7 @@
     lon = lax.axis_size("lon")
     send = pack(obs_values, obs_dest, obs_cell, obs_count)
     got = lax.all_to_all(
-        send.reshape(DEV, BLK, CH), ("lat", "lon"), split_axis=0, concat_axis=0, tiled=True
+        send.reshape(DEV, BLK // 2, 2, CH), ("lat", "lon"), split_axis=0, concat_axis=0, tiled=True
     )
     cells, top, bottom, edge = to_grid(got.reshape(SEND, CH))
     north = lax.ppermute(bottom, "lat", [(i, i + 1) for i in range(lat - 1)])

time: 104 us -> 97.9 us (0.941)
  waiting for transfers between devices: 37.3 us -> 34.7 us
  Pallas kernels: 39.5 us -> 37.6 us
  local copies, waits for them, and re-layouts: 4.09 us -> 2.78 us
    all_to_all x1, waiting for transfers between devices: 32.5 us -> 30.4 us  [body(): lax.all_to_all(send.reshape(DEV, BLK // 2, 2, CH), ('lat', 'lon'), split_...]
    unnamed x9 -> x13, local copies, waits for them, and re-layouts: 3.99 us -> 1.95 us
    pallas_call x1, Pallas kernels: 15.3 us -> 13.3 us  [convolve(): pl.pallas_call(conv_kernel, out_shape=jax.ShapeDtypeStruct((TH // 2, TW /...]
  transfers between devices with their start and end apart: 5 -> 5, of which waited for: 4 -> 4; matrix products, arithmetic and copies ran while one was open for 0% -> 1% of each run, Pallas kernels for 0% -> 0%
where the time goes in v3:
time: 97.9 us; the launch traced here: 97.5 us
  Pallas kernels  37.6 us (38%)
  waiting for transfers between devices  34.7 us (35%)
  starting transfers between devices  21.6 us (22%)
  local copies, waits for them, and re-layouts  2.78 us (3%)
    all_to_all x1, waiting for transfers between devices, body(): lax.all_to_all(send.reshape(DEV, BLK // 2, 2, CH), ('lat', 'lon'), split_...  30.4 us
    pallas_call x1, Pallas kernels, to_grid(): pl.pallas_call(grid_kernel, out_shape=[jax.ShapeDtypeStruct(s, BF16) for...  16.7 us
    pallas_call x1, Pallas kernels, convolve(): pl.pallas_call(conv_kernel, out_shape=jax.ShapeDtypeStruct((TH // 2, TW /...  13.3 us
    all_to_all x1, starting transfers between devices, body(): lax.all_to_all(send.reshape(DEV, BLK // 2, 2, CH), ('lat', 'lon'), split_...  11.5 us
    pallas_call x1, Pallas kernels, pack(): pl.pallas_call(pack_kernel, out_shape=jax.ShapeDtypeStruct((SEND, CH), BF...  7.57 us
    ppermute x1, starting transfers between devices, body(): east = lax.ppermute(own, 'lon', [((i + 1) % lon, i) for i in range(lon)])  4.15 us
    ppermute x1, starting transfers between devices, body(): north = lax.ppermute(bottom, 'lat', [(i, i + 1) for i in range(lat - 1)])  3.35 us
    ppermute x1, waiting for transfers between devices, body(): south = lax.ppermute(top, 'lat', [(i + 1, i) for i in range(lat - 1)])  3.13 us
  transfers between devices with their start and end apart: 5, of which 4 were waited for; matrix products, arithmetic and copies ran while one was open for 1% of the time, Pallas kernels for 0%

profile of v3, /device:TPU:1, one launch (start us, length us, event | category | flops | bytes accessed | tf_op | source)
XLA Modules:
  0.0 97.5 jit_solution(17923244992242078437)
XLA Ops:
  0.7 7.6 %pack.1 = bf16[8448,128]{1,0:T(8,128)(2,1)} custom-call(s32[1]{0:T(128)S(6)} %copy.17.count_ref, s32[32,128]{1,0:T(8,128)} %bitcast.36, s32[32,128]{1,0:T(8,128)} %bitcast.37, bf16[4096,128]{1,0:T(8,128)(2,1)} %val_hbm.1), custom_call_target="tpu_custom_call" | custom-call | tf_op jit(solution)/shard_map/pack/pallas_call | solution.py:120
  8.2 11.5 %all-to-all-start = ((bf16[128,33,2,128]{3,2,1,0:T(2,128)(2,1)}), bf16[128,33,2,128]{3,2,1,0:T(2,128)(2,1)S(1)}, u32[]{:S(2)}, u32[]{:S(2)}) async-start(bf16[128,33,2,128]{3,2,1,0:T(2,128)(2,1)} %bitcast.29), calls=%async_computation | async-start | bytes 4325376 | tf_op jit(solution)/shard_map/all_to_all | solution.py:418
  19.7 0.1 pad.13.clone
  19.8 30.4 %all-to-all-done = bf16[128,33,2,128]{3,2,1,0:T(2,128)(2,1)S(1)} async-done(((bf16[128,33,2,128]{3,2,1,0:T(2,128)(2,1)}), bf16[128,33,2,128]{3,2,1,0:T(2,128)(2,1)S(1)}, u32[]{:S(2)}, u32[]{:S(2)}) %all-to-all-start) | async-done | bytes 2162720 | tf_op jit(solution)/shard_map/all_to_all | solution.py:418
  50.2 0.0 copy-start
  50.2 1.4 %copy-done = bf16[128,33,2,128]{3,2,1,0:T(2,128)(2,1)} copy-done((bf16[128,33,2,128]{3,2,1,0:T(2,128)(2,1)}, bf16[128,33,2,128]{3,2,1,0:T(2,128)(2,1)S(1)}, u32[]{:S(2)}) %copy-start) | copy-done | bytes 2162712
  51.6 16.7 %to_grid.1 = (bf16[8192,128]{1,0:T(8,128)(2,1)}, bf16[256,128]{1,0:T(8,128)(2,1)}, bf16[512,128]{1,0:T(8,128)(2,1)}, bf16[3,32,128]{2,1,0:T(8,128)(2,1)}) custom-call(bf16[8448,128]{1,0:T(8,128)(2,1)} %bitcast.28), custom_call_target="tpu_custom_call" | custom-call | tf_op jit(solution)/shard_map/to_grid/pallas_call | solution.py:264
  68.2 3.3 %collective-permute-start = (bf16[512,128]{1,0:T(8,128)(2,1)}, bf16[512,128]{1,0:T(8,128)(2,1)S(1)}, u32[]{:S(2)}, u32[]{:S(2)}) collective-permute-start(bf16[512,128]{1,0:T(8,128)(2,1)} %get-tuple-element.10), channel_id=1, source_target_pairs={{0,16},{16,32},{32,48},{48,64},{64,80},{80,96},{96,112},{1,17},{17... | collective-permute-start | bytes 393224 | tf_op jit(solution)/shard_map/ppermute | solution.py:422
  71.6 1.9 %collective-permute-start.1 = (bf16[256,128]{1,0:T(8,128)(2,1)}, bf16[256,128]{1,0:T(8,128)(2,1)S(1)}, u32[]{:S(2)}, u32[]{:S(2)}) collective-permute-start(bf16[256,128]{1,0:T(8,128)(2,1)} %get-tuple-element.11), channel_id=1, source_target_pairs={{16,0},{32,16},{48,32},{64,48},{80,64},{96,80},{112,96},{17,1},{33... | collective-permute-start | bytes 196616 | tf_op jit(solution)/shard_map/ppermute | solution.py:423
  73.5 0.7 slice_bitcast_fusion.1
  74.2 3.1 %collective-permute-done.1 = bf16[256,128]{1,0:T(8,128)(2,1)S(1)} collective-permute-done((bf16[256,128]{1,0:T(8,128)(2,1)}, bf16[256,128]{1,0:T(8,128)(2,1)S(1)}, u32[]{:S(2)}, u32[]{:S(2)}) %collective-permute-start.1) | collective-permute-done | bytes 65568 | tf_op jit(solution)/shard_map/ppermute | solution.py:423
  77.4 0.0 copy-start.2
  77.4 0.0 collective-permute-done
  77.4 0.0 copy-start.1
  77.4 0.1 maximum_bitcast_fusion
  77.5 0.0 copy-start.3
  77.5 0.7 collective-permute-start.2
  78.2 4.1 %collective-permute-start.3 = (bf16[48,128]{1,0:T(8,128)(2,1)S(1)}, bf16[48,128]{1,0:T(8,128)(2,1)S(1)}, u32[]{:S(2)}, u32[]{:S(2)}) collective-permute-start(bf16[48,128]{1,0:T(8,128)(2,1)S(1)} %get-tuple-element.24.own_hbm), channel_id=1, source_target_pairs={{1,0},{2,1},{3,2},{4,3},{5,4},{6,5},{7,6},{8,7},{9,8},{10,9},{11,1... | collective-permute-start | bytes 36872 | tf_op jit(solution)/shard_map/ppermute | solution.py:435
  82.4 0.8 collective-permute-done.3.east_hbm
  83.2 0.0 copy-start.5
  83.2 0.4 collective-permute-done.2.west_hbm
  83.6 0.0 copy-start.4
  83.6 0.0 copy-done.2
  83.6 0.0 copy-done.1
  83.6 0.0 copy-done.3
  83.6 0.2 copy-done.5
  83.8 0.4 copy-done.4
  84.2 13.3 %convolve.1 = bf16[16,128,256]{2,1,0:T(8,128)(2,1)} custom-call(s32[1]{0:T(128)} %bitcast.band_ref, bf16[32,16,16,128]{3,2,1,0:T(8,128)(2,1)} %bitcast.30, bf16[2,16,16,128]{3,2,1,0:T(8,128)(2,1)} %bitcast.34, bf16[16,16,128]{2,1,0:T(8,128)(2,1)} %bitcast.35, bf16[48,128]{1,0:T(8,128)(2,1)} %copy-done.3, bf16[2,48,128]{2,1,0:T(8,128)(2,1)} %copy-done.4, ...), custom_call_target="tpu_custom_call" | custom-call | tf_op jit(solution)/shard_map/convolve/pallas_call | solution.py:386
  (6 shorter events, 0.0 us)
Async XLA Ops:
  8.2 42.0 %all-to-all-start = ((bf16[128,33,2,128]{3,2,1,0:T(2,128)(2,1)}), bf16[128,33,2,128]{3,2,1,0:T(2,128)(2,1)S(1)}, u32[]{:S(2)}, u32[]{:S(2)}) async-start(bf16[128,33,2,128]{3,2,1,0:T(2,128)(2,1)} %bitcast.29), calls=%async_computation | async-start | bytes 4325376 | tf_op jit(solution)/shard_map/all_to_all | solution.py:418
  50.2 1.4 %copy-start = (bf16[128,33,2,128]{3,2,1,0:T(2,128)(2,1)}, bf16[128,33,2,128]{3,2,1,0:T(2,128)(2,1)S(1)}, u32[]{:S(2)}) copy-start(bf16[128,33,2,128]{3,2,1,0:T(2,128)(2,1)S(1)} %all-to-all-done) | copy-start | bytes 6488068
  68.2 9.2 %collective-permute-start = (bf16[512,128]{1,0:T(8,128)(2,1)}, bf16[512,128]{1,0:T(8,128)(2,1)S(1)}, u32[]{:S(2)}, u32[]{:S(2)}) collective-permute-start(bf16[512,128]{1,0:T(8,128)(2,1)} %get-tuple-element.10), channel_id=1, source_target_pairs={{0,16},{16,32},{32,48},{48,64},{64,80},{80,96},{96,112},{1,17},{17... | collective-permute-start | bytes 393224 | tf_op jit(solution)/shard_map/ppermute | solution.py:422
  71.6 5.8 %collective-permute-start.1 = (bf16[256,128]{1,0:T(8,128)(2,1)}, bf16[256,128]{1,0:T(8,128)(2,1)S(1)}, u32[]{:S(2)}, u32[]{:S(2)}) collective-permute-start(bf16[256,128]{1,0:T(8,128)(2,1)} %get-tuple-element.11), channel_id=1, source_target_pairs={{16,0},{32,16},{48,32},{64,48},{80,64},{96,80},{112,96},{17,1},{33... | collective-permute-start | bytes 196616 | tf_op jit(solution)/shard_map/ppermute | solution.py:423
  77.4 6.2 %copy-start.2 = (bf16[256,128]{1,0:T(8,128)(2,1)}, bf16[256,128]{1,0:T(8,128)(2,1)S(1)}, u32[]{:S(2)}) copy-start(bf16[256,128]{1,0:T(8,128)(2,1)S(1)} %collective-permute-done.1) | copy-start | bytes 196612
  77.4 6.2 %copy-start.1 = (bf16[512,128]{1,0:T(8,128)(2,1)}, bf16[512,128]{1,0:T(8,128)(2,1)S(1)}, u32[]{:S(2)}) copy-start(bf16[512,128]{1,0:T(8,128)(2,1)S(1)} %collective-permute-done) | copy-start | bytes 393220
  77.5 6.1 %copy-start.3 = (bf16[48,128]{1,0:T(8,128)(2,1)}, bf16[48,128]{1,0:T(8,128)(2,1)S(1)}, u32[]{:S(2)}) copy-start(bf16[48,128]{1,0:T(8,128)(2,1)S(1)} %get-tuple-element.24.own_hbm) | copy-start | bytes 36868
  77.5 6.1 %collective-permute-start.2 = (bf16[2,48,128]{2,1,0:T(8,128)(2,1)S(1)}, bf16[2,48,128]{2,1,0:T(8,128)(2,1)S(1)}, u32[]{:S(2)}, u32[]{:S(2)}) collective-permute-start(bf16[2,48,128]{2,1,0:T(8,128)(2,1)S(1)} %pad_maximum_fusion), channel_id=1, source_target_pairs={{0,1},{1,2},{2,3},{3,4},{4,5},{5,6},{6,7},{7,8},{8,9},{9,10},{10,1... | collective-permute-start | bytes 73736 | tf_op jit(solution)/shard_map/ppermute | solution.py:434
  78.2 5.0 %collective-permute-start.3 = (bf16[48,128]{1,0:T(8,128)(2,1)S(1)}, bf16[48,128]{1,0:T(8,128)(2,1)S(1)}, u32[]{:S(2)}, u32[]{:S(2)}) collective-permute-start(bf16[48,128]{1,0:T(8,128)(2,1)S(1)} %get-tuple-element.24.own_hbm), channel_id=1, source_target_pairs={{1,0},{2,1},{3,2},{4,3},{5,4},{6,5},{7,6},{8,7},{9,8},{10,9},{11,1... | collective-permute-start | bytes 36872 | tf_op jit(solution)/shard_map/ppermute | solution.py:435
  83.2 0.6 copy-start.5
  83.6 0.6 copy-start.4

commit v4 on v3

--- a/solution.py
+++ b/solution.py
@@ -141,10 +141,16 @@
 
 
 def grid_kernel(
-    got_ref, out_hbm, top_ref, bottom_ref, edge_ref,
-    out_ref, x32, acc, acc2, table_v, table_s, rowpair, colpair, edge32, sem, sem_out,
+    got_hbm, out_hbm, top_ref, bottom_ref, edge_ref,
+    got_ref, out_ref, x32, acc, acc2, table_v, table_s, rowpair, colpair, edge32, sem, sem_in, sem_out,
 ):
     parts = 4
+    fetches = []
+    for p in range(parts):
+        rows = pl.ds(p * SEND // parts, SEND // parts)
+        fetch = pltpu.make_async_copy(got_hbm.at[rows], got_ref.at[rows], sem_in.at[p])
+        fetch.start()
+        fetches.append(fetch)
 
     def clear(i, c):
         acc[pl.ds(pl.multiple_of(i * 128, 128), 128), :] = jnp.zeros((128, CH), F32)
@@ -158,7 +164,9 @@
         x32[rows, :] = got_ref[rows, :].astype(F32)
         return c
 
-    lax.fori_loop(0, SEND // 192, widen, 0)
+    for p in range(parts):
+        fetches[p].wait()
+        lax.fori_loop(p * SEND // 192 // parts, (p + 1) * SEND // 192 // parts, widen, 0)
     cells = jnp.concatenate([x32[s * BLK + CAP : s * BLK + CAP + 1, :] for s in range(DEV)], axis=0)
     swapped = pltpu.roll(cells, CAP, axis=1)
     lane = lax.broadcasted_iota(jnp.int32, (DEV, 128), 1)
@@ -264,9 +272,10 @@
     return pl.pallas_call(
         grid_kernel,
         out_shape=[jax.ShapeDtypeStruct(s, BF16) for s in shapes],
-        in_specs=[pl.BlockSpec(memory_space=pltpu.VMEM)],
+        in_specs=[pl.BlockSpec(memory_space=pl.ANY)],
         out_specs=[pl.BlockSpec(memory_space=pl.ANY)] + [pl.BlockSpec(memory_space=pltpu.VMEM)] * 3,
         scratch_shapes=[
+            pltpu.VMEM((SEND, CH), BF16),
             pltpu.VMEM((TH * TW, CH), BF16),
             pltpu.VMEM((SEND, CH), F32),
             pltpu.VMEM((TRASH + TH * TW, CH), F32),
@@ -278,8 +287,9 @@
             pltpu.VMEM((3, TH, CH), F32),
             pltpu.SemaphoreType.DMA,
             pltpu.SemaphoreType.DMA((4,)),
+            pltpu.SemaphoreType.DMA((4,)),
         ],
-        compiler_params=pltpu.CompilerParams(vmem_limit_bytes=60 * 1024 * 1024),
+        compiler_params=pltpu.CompilerParams(vmem_limit_bytes=52 * 1024 * 1024),
         name="to_grid",
     )(got)
 
@@ -403,7 +413,7 @@
             pltpu.VMEM((SECOND, 2, TW // 2, 128), F32),
             pltpu.SemaphoreType.DMA((8,)),
         ],
-        compiler_params=pltpu.CompilerParams(vmem_limit_bytes=56 * 1024 * 1024),
+        compiler_params=pltpu.CompilerParams(vmem_limit_bytes=52 * 1024 * 1024),
         name="convolve",
     )(
         band, cells.reshape(TH, 16, 16, CH), north.reshape(2, 16, 16, CH), south.reshape(16, 16, CH),

time: 97.9 us -> 94.1 us (0.961)
  local copies, waits for them, and re-layouts: 2.78 us -> 0.12 us
  Pallas kernels: 37.6 us -> 35.8 us
    unnamed x13 -> x5, local copies, waits for them, and re-layouts: 1.95 us -> 0.02 us
    pallas_call x1, Pallas kernels: 16.7 us -> 14.9 us  [to_grid(): pl.pallas_call(grid_kernel, out_shape=[jax.ShapeDtypeStruct(s, BF16) for...]
  transfers between devices with their start and end apart: 5 -> 5, of which waited for: 4 -> 4; matrix products, arithmetic and copies ran while one was open for 1% -> 0% of each run, Pallas kernels for 0% -> 0%
where the time goes in v4:
time: 94.1 us; the launch traced here: 93.7 us
  Pallas kernels  35.8 us (38%)
  waiting for transfers between devices  34.9 us (37%)
  starting transfers between devices  22 us (23%)
    all_to_all x1, waiting for transfers between devices, body(): lax.all_to_all(send.reshape(DEV, BLK // 2, 2, CH), ('lat', 'lon'), split_...  30.1 us
    pallas_call x1, Pallas kernels, to_grid(): pl.pallas_call(grid_kernel, out_shape=[jax.ShapeDtypeStruct(s, BF16) for...  14.9 us
    pallas_call x1, Pallas kernels, convolve(): pl.pallas_call(conv_kernel, out_shape=jax.ShapeDtypeStruct((TH // 2, TW /...  13.4 us
    all_to_all x1, starting transfers between devices, body(): lax.all_to_all(send.reshape(DEV, BLK // 2, 2, CH), ('lat', 'lon'), split_...  11.9 us
    pallas_call x1, Pallas kernels, pack(): pl.pallas_call(pack_kernel, out_shape=jax.ShapeDtypeStruct((SEND, CH), BF...  7.54 us
    ppermute x1, starting transfers between devices, body(): east = lax.ppermute(own, 'lon', [((i + 1) % lon, i) for i in range(lon)])  4.11 us
    ppermute x1, waiting for transfers between devices, body(): south = lax.ppermute(top, 'lat', [(i + 1, i) for i in range(lat - 1)])  3.64 us
    ppermute x1, starting transfers between devices, body(): north = lax.ppermute(bottom, 'lat', [(i, i + 1) for i in range(lat - 1)])  3.35 us
  transfers between devices with their start and end apart: 5, of which 4 were waited for; matrix products, arithmetic and copies ran while one was open for 0% of the time, Pallas kernels for 0%

profile of v4, /device:TPU:1, one launch (start us, length us, event | category | flops | bytes accessed | tf_op | source)
XLA Modules:
  0.0 93.7 jit_solution(11741386751726409154)
XLA Ops:
  0.7 7.5 %pack.1 = bf16[8448,128]{1,0:T(8,128)(2,1)} custom-call(s32[1]{0:T(128)S(6)} %copy.17.count_ref, s32[32,128]{1,0:T(8,128)} %bitcast.35, s32[32,128]{1,0:T(8,128)} %bitcast.36, bf16[4096,128]{1,0:T(8,128)(2,1)} %val_hbm.1), custom_call_target="tpu_custom_call" | custom-call | tf_op jit(solution)/shard_map/pack/pallas_call | solution.py:120
  8.2 11.9 %all-to-all-start = ((bf16[128,33,2,128]{3,2,1,0:T(2,128)(2,1)}), bf16[128,33,2,128]{3,2,1,0:T(2,128)(2,1)}, u32[]{:S(2)}, u32[]{:S(2)}) async-start(bf16[128,33,2,128]{3,2,1,0:T(2,128)(2,1)} %bitcast.33), calls=%async_computation | async-start | bytes 4325376 | tf_op jit(solution)/shard_map/all_to_all | solution.py:428
  20.1 0.0 copy-start
  20.1 0.0 copy-start.1
  20.1 0.1 pad.13.clone
  20.2 30.1 %all-to-all-done = bf16[128,33,2,128]{3,2,1,0:T(2,128)(2,1)} async-done(((bf16[128,33,2,128]{3,2,1,0:T(2,128)(2,1)}), bf16[128,33,2,128]{3,2,1,0:T(2,128)(2,1)}, u32[]{:S(2)}, u32[]{:S(2)}) %all-to-all-start) | async-done | bytes 2162720 | tf_op jit(solution)/shard_map/all_to_all | solution.py:428
  50.3 14.9 %to_grid.1 = (bf16[8192,128]{1,0:T(8,128)(2,1)}, bf16[256,128]{1,0:T(8,128)(2,1)S(1)}, bf16[512,128]{1,0:T(8,128)(2,1)S(1)}, bf16[3,32,128]{2,1,0:T(8,128)(2,1)S(1)}) custom-call(bf16[8448,128]{1,0:T(8,128)(2,1)} %bitcast.4.got_hbm), custom_call_target="tpu_custom_call" | custom-call | tf_op jit(solution)/shard_map/to_grid/pallas_call | solution.py:272
  65.2 3.3 %collective-permute-start = (bf16[512,128]{1,0:T(8,128)(2,1)S(1)}, bf16[512,128]{1,0:T(8,128)(2,1)S(1)}, u32[]{:S(2)}, u32[]{:S(2)}) collective-permute-start(bf16[512,128]{1,0:T(8,128)(2,1)S(1)} %get-tuple-element.10), channel_id=1, source_target_pairs={{0,16},{16,32},{32,48},{48,64},{64,80},{80,96},{96,112},{1,17},{17... | collective-permute-start | bytes 393224 | tf_op jit(solution)/shard_map/ppermute | solution.py:432
  68.6 1.9 %collective-permute-start.1 = (bf16[256,128]{1,0:T(8,128)(2,1)S(1)}, bf16[256,128]{1,0:T(8,128)(2,1)S(1)}, u32[]{:S(2)}, u32[]{:S(2)}) collective-permute-start(bf16[256,128]{1,0:T(8,128)(2,1)S(1)} %get-tuple-element.11), channel_id=1, source_target_pairs={{16,0},{32,16},{48,32},{64,48},{80,64},{96,80},{112,96},{17,1},{33... | collective-permute-start | bytes 196616 | tf_op jit(solution)/shard_map/ppermute | solution.py:433
  70.5 3.6 %collective-permute-done.1 = bf16[256,128]{1,0:T(8,128)(2,1)S(1)} collective-permute-done((bf16[256,128]{1,0:T(8,128)(2,1)S(1)}, bf16[256,128]{1,0:T(8,128)(2,1)S(1)}, u32[]{:S(2)}, u32[]{:S(2)}) %collective-permute-start.1) | collective-permute-done | bytes 65568 | tf_op jit(solution)/shard_map/ppermute | solution.py:433
  74.2 0.0 collective-permute-done
  74.2 0.1 maximum_bitcast_fusion
  74.3 0.7 collective-permute-start.2
  75.0 4.1 %collective-permute-start.3 = (bf16[48,128]{1,0:T(8,128)(2,1)S(1)}, bf16[48,128]{1,0:T(8,128)(2,1)S(1)}, u32[]{:S(2)}, u32[]{:S(2)}) collective-permute-start(bf16[48,128]{1,0:T(8,128)(2,1)S(1)} %get-tuple-element.24.own_hbm), channel_id=1, source_target_pairs={{1,0},{2,1},{3,2},{4,3},{5,4},{6,5},{7,6},{8,7},{9,8},{10,9},{11,1... | collective-permute-start | bytes 36872 | tf_op jit(solution)/shard_map/ppermute | solution.py:445
  79.1 0.8 collective-permute-done.3.east_hbm
  80.0 0.4 collective-permute-done.2.west_hbm
  80.4 0.0 copy-done
  80.4 0.0 copy-done.1
  80.4 13.4 %convolve.1 = bf16[16,128,256]{2,1,0:T(8,128)(2,1)} custom-call(s32[1]{0:T(128)} %bitcast.band_ref, bf16[32,16,16,128]{3,2,1,0:T(8,128)(2,1)} %bitcast.34, bf16[2,16,16,128]{3,2,1,0:T(8,128)(2,1)S(1)} %bitcast.31, bf16[16,16,128]{2,1,0:T(8,128)(2,1)S(1)} %bitcast.32, bf16[48,128]{1,0:T(8,128)(2,1)S(1)} %get-tuple-element.24.own_hbm, ...), custom_call_target="tpu_custom_call" | custom-call | tf_op jit(solution)/shard_map/convolve/pallas_call | solution.py:396
  (7 shorter events, 0.0 us)
Async XLA Ops:
  8.2 42.1 %all-to-all-start = ((bf16[128,33,2,128]{3,2,1,0:T(2,128)(2,1)}), bf16[128,33,2,128]{3,2,1,0:T(2,128)(2,1)}, u32[]{:S(2)}, u32[]{:S(2)}) async-start(bf16[128,33,2,128]{3,2,1,0:T(2,128)(2,1)} %bitcast.33), calls=%async_computation | async-start | bytes 4325376 | tf_op jit(solution)/shard_map/all_to_all | solution.py:428
  20.1 60.2 %copy-start = (bf16[3,3,256,256]{3,2,1,0:T(8,128)(2,1)S(1)}, bf16[3,3,256,256]{3,2,1,0:T(8,128)(2,1)}, u32[]{:S(2)}) copy-start(bf16[3,3,256,256]{3,2,1,0:T(8,128)(2,1)} %param.11) | copy-start | bytes 3538948
  20.1 60.2 %copy-start.1 = (bf16[3,3,128,256]{3,2,1,0:T(8,128)(2,1)S(1)}, bf16[3,3,128,256]{3,2,1,0:T(8,128)(2,1)}, u32[]{:S(2)}) copy-start(bf16[3,3,128,256]{3,2,1,0:T(8,128)(2,1)} %param.10) | copy-start | bytes 1769476
  65.2 8.9 %collective-permute-start = (bf16[512,128]{1,0:T(8,128)(2,1)S(1)}, bf16[512,128]{1,0:T(8,128)(2,1)S(1)}, u32[]{:S(2)}, u32[]{:S(2)}) collective-permute-start(bf16[512,128]{1,0:T(8,128)(2,1)S(1)} %get-tuple-element.10), channel_id=1, source_target_pairs={{0,16},{16,32},{32,48},{48,64},{64,80},{80,96},{96,112},{1,17},{17... | collective-permute-start | bytes 393224 | tf_op jit(solution)/shard_map/ppermute | solution.py:432
  68.6 5.6 %collective-permute-start.1 = (bf16[256,128]{1,0:T(8,128)(2,1)S(1)}, bf16[256,128]{1,0:T(8,128)(2,1)S(1)}, u32[]{:S(2)}, u32[]{:S(2)}) collective-permute-start(bf16[256,128]{1,0:T(8,128)(2,1)S(1)} %get-tuple-element.11), channel_id=1, source_target_pairs={{16,0},{32,16},{48,32},{64,48},{80,64},{96,80},{112,96},{17,1},{33... | collective-permute-start | bytes 196616 | tf_op jit(solution)/shard_map/ppermute | solution.py:433
  74.3 6.1 %collective-permute-start.2 = (bf16[2,48,128]{2,1,0:T(8,128)(2,1)S(1)}, bf16[2,48,128]{2,1,0:T(8,128)(2,1)S(1)}, u32[]{:S(2)}, u32[]{:S(2)}) collective-permute-start(bf16[2,48,128]{2,1,0:T(8,128)(2,1)S(1)} %pad_maximum_fusion), channel_id=1, source_target_pairs={{0,1},{1,2},{2,3},{3,4},{4,5},{5,6},{6,7},{7,8},{8,9},{9,10},{10,1... | collective-permute-start | bytes 73736 | tf_op jit(solution)/shard_map/ppermute | solution.py:444
  75.0 4.9 %collective-permute-start.3 = (bf16[48,128]{1,0:T(8,128)(2,1)S(1)}, bf16[48,128]{1,0:T(8,128)(2,1)S(1)}, u32[]{:S(2)}, u32[]{:S(2)}) collective-permute-start(bf16[48,128]{1,0:T(8,128)(2,1)S(1)} %get-tuple-element.24.own_hbm), channel_id=1, source_target_pairs={{1,0},{2,1},{3,2},{4,3},{5,4},{6,5},{7,6},{8,7},{9,8},{10,9},{11,1... | collective-permute-start | bytes 36872 | tf_op jit(solution)/shard_map/ppermute | solution.py:445

commit v5 on v4

--- a/solution.py
+++ b/solution.py
@@ -18,7 +18,7 @@
 SEND = DEV * BLK
 TRASH = 256
 GROUP = 8
-PART = 32
+PART = 64
 FIRST = 11
 SECOND = 8
 COLS = 48
@@ -75,8 +75,7 @@
         cells = cells + lax.dot_general(
             hot16, coded, (((1,), (1,)), ((), ())), preferred_element_type=F32
         )
-    slots = jnp.concatenate(slots + [jnp.zeros((96, 128), jnp.int32)], axis=0)
-    slot_v[...] = slots.T
+    slot_v[...] = jnp.concatenate(slots, axis=0)
     to_scalar = pltpu.make_async_copy(slot_v, slot_s, sem)
     to_scalar.start()
     fetches[2].wait()
@@ -90,12 +89,11 @@
     to_scalar.wait()
 
     def move(i, c):
-        base = pl.multiple_of(i * 128, 128)
-        for k in range(128):
-            o32[pl.ds(slot_s.at[k][i], 1), :] = x32[pl.ds(base + k, 1), :]
-        return c
-
-    lax.fori_loop(0, ROWS // 128, move, 0)
+        for k in range(ROWS // 128):
+            o32[pl.ds(slot_s.at[k][i], 1), :] = x32[pl.ds(k * 128 + i, 1), :]
+        return c
+
+    lax.fori_loop(0, 128, move, 0)
     for d in range(DEV):
         o32[d * BLK + CAP : d * BLK + CAP + 1, :] = cells[d : d + 1, :]
 
@@ -129,8 +127,8 @@
             pltpu.VMEM((SEND, CH), BF16),
             pltpu.VMEM((ROWS, CH), F32),
             pltpu.VMEM((SEND + 8, CH), F32),
-            pltpu.VMEM((128, 128), jnp.int32),
-            pltpu.SMEM((128, 128), jnp.int32),
+            pltpu.VMEM((32, 128), jnp.int32),
+            pltpu.SMEM((32, 128), jnp.int32),
             pltpu.SemaphoreType.DMA,
             pltpu.SemaphoreType.DMA((3,)),
             pltpu.SemaphoreType.DMA((3,)),
@@ -142,7 +140,7 @@
 
 def grid_kernel(
     got_hbm, out_hbm, top_ref, bottom_ref, edge_ref,
-    got_ref, out_ref, x32, acc, acc2, table_v, table_s, rowpair, colpair, edge32, sem, sem_in, sem_out,
+    got_ref, out_ref, x32, acc, acc2, table_v, table_s, rowpair, colpair, inverse, edge32, sem, sem_in, sem_out,
 ):
     parts = 4
     fetches = []
@@ -167,7 +165,7 @@
     for p in range(parts):
         fetches[p].wait()
         lax.fori_loop(p * SEND // 192 // parts, (p + 1) * SEND // 192 // parts, widen, 0)
-    cells = jnp.concatenate([x32[s * BLK + CAP : s * BLK + CAP + 1, :] for s in range(DEV)], axis=0)
+    cells = x32[pl.ds(CAP, DEV, stride=BLK), :]
     swapped = pltpu.roll(cells, CAP, axis=1)
     lane = lax.broadcasted_iota(jnp.int32, (DEV, 128), 1)
     first = lane < CAP
@@ -187,8 +185,10 @@
     flags = jnp.dot(repeated, groups, preferred_element_type=F32)
     flags = (flags + pltpu.roll(flags, DEV // 2, axis=0)).astype(jnp.int32)
     table_v[...] = jnp.where(first, index, flags).T
-    to_scalar = pltpu.make_async_copy(table_v, table_s, sem)
-    to_scalar.start()
+    to_scalar = []
+    for n, rows in enumerate((pl.ds(CAP, 8), pl.ds(0, CAP))):
+        to_scalar.append(pltpu.make_async_copy(table_v.at[rows], table_s.at[rows], sem.at[n]))
+        to_scalar[n].start()
 
     half = DEV // 2
     firsth = lax.broadcasted_iota(jnp.int32, (half, 128), 1) < CAP
@@ -211,13 +211,14 @@
         )
 
     tallies = lax.fori_loop(0, half // batch, tally, jnp.zeros((TW, 128), F32))
-    inverse = 1.0 / jnp.maximum(tallies, 1.0)
-
-    to_scalar.wait()
-
-    def source(s, c):
-        pairs = ((acc, s), (acc2, s + half))
-        for p in range(CAP // PART):
+    inverse[...] = 1.0 / jnp.maximum(tallies, 1.0)
+
+    to_scalar[0].wait()
+    for p in range(CAP // PART):
+        to_scalar[1 + p].wait()
+
+        def source(s, c):
+            pairs = ((acc, s), (acc2, s + half))
             clash = table_s.at[CAP + p][s]
 
             @pl.when(clash == 0)
@@ -240,31 +241,33 @@
                         at = pl.ds(table_s.at[k][t], 1)
                         a[at, :] = a[at, :] + x32[pl.ds(t * BLK + k, 1), :]
 
-        return c
-
-    lax.fori_loop(0, half, source, 0)
-    stores = []
-    for i in range(TH):
-        scale = jnp.broadcast_to(inverse[:, i : i + 1], (TW, CH))
-        rows = slice(TRASH + i * TW, TRASH + (i + 1) * TW)
-        mean = (acc[rows, :] + acc2[rows, :]) * scale
-        out_ref[i * TW : (i + 1) * TW, :] = mean.astype(BF16)
-        if i == 0:
-            top_ref[...] = mean.astype(BF16)
-        if i >= TH - 2:
-            bottom_ref[(i - TH + 2) * TW : (i - TH + 3) * TW, :] = mean.astype(BF16)
-        edge32[0, i : i + 1, :] = mean[0:1]
-        edge32[1, i : i + 1, :] = mean[239:240]
-        edge32[2, i : i + 1, :] = mean[255:256]
-        if (i + 1) % (TH // parts) == 0:
-            p = i // (TH // parts)
-            rows = pl.ds(p * (TH // parts) * TW, (TH // parts) * TW)
-            store = pltpu.make_async_copy(out_ref.at[rows], out_hbm.at[rows], sem_out.at[p])
-            store.start()
-            stores.append(store)
+            return c
+
+        lax.fori_loop(0, half, source, 0)
+
+    span = TH // parts
+
+    def normalise(p, c):
+        scales = inverse[...]
+        for k in range(span):
+            i = p * span + k
+            rows = pl.ds(pl.multiple_of(TRASH + i * TW, TW), TW)
+            mean = (acc[rows, :] + acc2[rows, :]) * jnp.broadcast_to(scales[:, k : k + 1], (TW, CH))
+            out_ref[pl.ds(pl.multiple_of(i * TW, TW), TW), :] = mean.astype(BF16)
+            for e, at in enumerate((0, 239, 255)):
+                edge32[e, pl.ds(i, 1), :] = mean[at : at + 1]
+        inverse[...] = pltpu.roll(scales, 128 - span, axis=1)
+        rows = pl.ds(pl.multiple_of(p * span * TW, TW), span * TW)
+        pltpu.make_async_copy(out_ref.at[rows], out_hbm.at[rows], sem_out.at[p]).start()
+        return c
+
+    lax.fori_loop(0, parts, normalise, 0)
+    top_ref[...] = out_ref[:TW, :]
+    bottom_ref[...] = out_ref[(TH - 2) * TW :, :]
     edge_ref[...] = edge32[...].astype(BF16)
-    for store in stores:
-        store.wait()
+    for p in range(parts):
+        rows = pl.ds(p * span * TW, span * TW)
+        pltpu.make_async_copy(out_ref.at[rows], out_hbm.at[rows], sem_out.at[p]).wait()
 
 
 def to_grid(got):
@@ -281,11 +284,12 @@
             pltpu.VMEM((TRASH + TH * TW, CH), F32),
             pltpu.VMEM((TRASH + TH * TW, CH), F32),
             pltpu.VMEM((DEV, 128), jnp.int32),
-            pltpu.SMEM((DEV, 128), jnp.int32),
+            pltpu.SMEM((CAP + 8, 128), jnp.int32),
             pltpu.VMEM((DEV // 2, 128), F32),
             pltpu.VMEM((DEV // 2, 128), F32),
+            pltpu.VMEM((TW, 128), F32),
             pltpu.VMEM((3, TH, CH), F32),
-            pltpu.SemaphoreType.DMA,
+            pltpu.SemaphoreType.DMA((2,)),
             pltpu.SemaphoreType.DMA((4,)),
             pltpu.SemaphoreType.DMA((4,)),
         ],
@@ -295,19 +299,24 @@
 
 
 def conv_kernel(
-    band_ref, cell_hbm, north_hbm, south_hbm, own_hbm, west_hbm, east_hbm, w1_hbm, w2_hbm, out_ref,
-    field, even, odd, own_ref, west_ref, east_ref, wcol, ecol, hcol, w1_ref, w2_ref, o32, sem,
+    band_ref, cell_hbm, north_hbm, south_hbm, own_hbm, west_hbm, east_hbm, w1_hbm, w2_hbm, out_hbm,
+    field, even, odd, own_ref, west_ref, east_ref, wcol, ecol, hcol, w1_ref, w2_ref, o32, out_ref, sem, sem_out,
 ):
-    pairs = (
+    steps = (TH + 1) // FIRST
+    pairs = [
         (west_hbm, west_ref),
         (east_hbm, east_ref),
         (own_hbm, own_ref),
+        (w1_hbm, w1_ref),
         (north_hbm, field.at[pl.ds(0, 2), pl.ds(1, 16)]),
         (south_hbm, field.at[2 + TH, pl.ds(1, 16)]),
-        (cell_hbm, field.at[pl.ds(2, TH), pl.ds(1, 16)]),
-        (w1_hbm, w1_ref),
         (w2_hbm, w2_ref),
-    )
+    ]
+    for i in range(steps):
+        size = min(TH, (i + 1) * FIRST) - i * FIRST
+        pairs.append(
+            (cell_hbm.at[pl.ds(i * FIRST, size)], field.at[pl.ds(2 + i * FIRST, size), pl.ds(1, 16)])
+        )
     fetches = [pltpu.make_async_copy(src, dst, sem.at[i]) for i, (src, dst) in enumerate(pairs)]
     for fetch in fetches:
         fetch.start()
@@ -324,15 +333,16 @@
         field[r, 17] = jnp.where(sub == 15, ecol[pl.ds(r, 1), :], after).astype(BF16)
         return c
 
-    lax.fori_loop(0, TH + 3, wrap, 0, unroll=5)
-    fetches[6].wait()
-
     taps = [west_ref[0].astype(F32), west_ref[1].astype(F32), own_ref[...].astype(F32)]
     lhs = jnp.concatenate([taps[b][a : a + 40] for a in range(3) for b in range(3)], axis=1)
     hcol[...] = gelu(jnp.dot(lhs.astype(BF16), w1_ref[...], preferred_element_type=F32))
+    lax.fori_loop(0, 2, wrap, 0)
     sub2 = lax.broadcasted_iota(jnp.int32, (16, HID), 0)
 
     def first(step, c):
+        for i in range(steps):
+            pl.when(step == i)(fetches[7 + i].wait)
+        lax.fori_loop(2 + FIRST * step, 2 + FIRST * (step + 1), wrap, 0)
         lhs = jnp.concatenate(
             [
                 field[pl.ds(FIRST * step + a, FIRST), b : b + 16].reshape(FIRST * TW, CH)
@@ -358,7 +368,7 @@
         even[0] = jnp.zeros((9, 16, HID), BF16)
         odd[0] = jnp.zeros((8, 16, HID), BF16)
 
-    fetches[7].wait()
+    fetches[6].wait()
 
     def second(step, c):
         lhs = jnp.concatenate(
@@ -387,9 +397,14 @@
                         r * 128 + t * 16 : r * 128 + (t + 1) * 16, h * 128 : (h + 1) * 128
                     ]
             out_ref[SECOND * step + r] = jnp.concatenate([o32[r, 0], o32[r, 1]], axis=1).astype(BF16)
+        rows = pl.ds(SECOND * step, SECOND)
+        pltpu.make_async_copy(out_ref.at[rows], out_hbm.at[rows], sem_out.at[step]).start()
         return c
 
     lax.fori_loop(0, TH // 2 // SECOND, second, 0)
+    for i in range(TH // 2 // SECOND):
+        rows = pl.ds(SECOND * i, SECOND)
+        pltpu.make_async_copy(out_ref.at[rows], out_hbm.at[rows], sem_out.at[i]).wait()
 
 
 def convolve(band, cells, north, south, own, west, east, w1, w2):
@@ -397,7 +412,7 @@
         conv_kernel,
         out_shape=jax.ShapeDtypeStruct((TH // 2, TW // 2, HID), BF16),
         in_specs=[pl.BlockSpec(memory_space=pltpu.SMEM)] + [pl.BlockSpec(memory_space=pl.ANY)] * 8,
-        out_specs=pl.BlockSpec(memory_space=pltpu.VMEM),
+        out_specs=pl.BlockSpec(memory_space=pl.ANY),
         scratch_shapes=[
             pltpu.VMEM((TH + 3, 18, 16, CH), BF16),
             pltpu.VMEM((TH + 1, 9, 16, HID), BF16),
@@ -411,7 +426,9 @@
             pltpu.VMEM((9 * CH, HID), BF16),
             pltpu.VMEM((9 * HID, HID), BF16),
             pltpu.VMEM((SECOND, 2, TW // 2, 128), F32),
-            pltpu.SemaphoreType.DMA((8,)),
+            pltpu.VMEM((TH // 2, TW // 2, HID), BF16),
+            pltpu.SemaphoreType.DMA((7 + (TH + 1) // FIRST,)),
+            pltpu.SemaphoreType.DMA((TH // 2 // SECOND,)),
         ],
         compiler_params=pltpu.CompilerParams(vmem_limit_bytes=52 * 1024 * 1024),
         name="convolve",

time: 94.1 us -> 92.8 us (0.986)
  Pallas kernels: 35.8 us -> 34.8 us
where the time goes in v5:
time: 92.8 us; the launch traced here: 92.4 us
  waiting for transfers between devices  34.9 us (38%)
  Pallas kernels  34.8 us (37%)
  starting transfers between devices  21.8 us (23%)
    all_to_all x1, waiting for transfers between devices, body(): lax.all_to_all(send.reshape(DEV, BLK // 2, 2, CH), ('lat', 'lon'), split_...  30.1 us
    pallas_call x1, Pallas kernels, to_grid(): pl.pallas_call(grid_kernel, out_shape=[jax.ShapeDtypeStruct(s, BF16) for...  14.5 us
    pallas_call x1, Pallas kernels, convolve(): pl.pallas_call(conv_kernel, out_shape=jax.ShapeDtypeStruct((TH // 2, TW /...  13 us
    all_to_all x1, starting transfers between devices, body(): lax.all_to_all(send.reshape(DEV, BLK // 2, 2, CH), ('lat', 'lon'), split_...  11.9 us
    pallas_call x1, Pallas kernels, pack(): pl.pallas_call(pack_kernel, out_shape=jax.ShapeDtypeStruct((SEND, CH), BF...  7.27 us
    ppermute x1, starting transfers between devices, body(): east = lax.ppermute(own, 'lon', [((i + 1) % lon, i) for i in range(lon)])  3.95 us
    ppermute x1, waiting for transfers between devices, body(): south = lax.ppermute(top, 'lat', [(i + 1, i) for i in range(lat - 1)])  3.64 us
    ppermute x1, starting transfers between devices, body(): north = lax.ppermute(bottom, 'lat', [(i, i + 1) for i in range(lat - 1)])  3.11 us
  transfers between devices with their start and end apart: 5, of which 4 were waited for; matrix products, arithmetic and copies ran while one was open for 0% of the time, Pallas kernels for 0%

profile of v5, /device:TPU:1, one launch (start us, length us, event | category | flops | bytes accessed | tf_op | source)
XLA Modules:
  0.0 92.4 jit_solution(5751478628533916285)
XLA Ops:
  0.7 7.3 %pack.1 = bf16[8448,128]{1,0:T(8,128)(2,1)} custom-call(s32[1]{0:T(128)S(6)} %copy.17.count_ref, s32[32,128]{1,0:T(8,128)} %bitcast.35, s32[32,128]{1,0:T(8,128)} %bitcast.36, bf16[4096,128]{1,0:T(8,128)(2,1)} %val_hbm.1), custom_call_target="tpu_custom_call" | custom-call | tf_op jit(solution)/shard_map/pack/pallas_call | solution.py:118
  7.9 11.9 %all-to-all-start = ((bf16[128,33,2,128]{3,2,1,0:T(2,128)(2,1)}), bf16[128,33,2,128]{3,2,1,0:T(2,128)(2,1)}, u32[]{:S(2)}, u32[]{:S(2)}) async-start(bf16[128,33,2,128]{3,2,1,0:T(2,128)(2,1)} %bitcast.33), calls=%async_computation | async-start | bytes 4325376 | tf_op jit(solution)/shard_map/all_to_all | solution.py:445
  19.8 0.0 copy-start
  19.9 0.0 copy-start.1
  19.9 0.1 pad.13.clone
  20.0 30.1 %all-to-all-done = bf16[128,33,2,128]{3,2,1,0:T(2,128)(2,1)} async-done(((bf16[128,33,2,128]{3,2,1,0:T(2,128)(2,1)}), bf16[128,33,2,128]{3,2,1,0:T(2,128)(2,1)}, u32[]{:S(2)}, u32[]{:S(2)}) %all-to-all-start) | async-done | bytes 2162720 | tf_op jit(solution)/shard_map/all_to_all | solution.py:445
  50.0 14.5 %to_grid.1 = (bf16[8192,128]{1,0:T(8,128)(2,1)}, bf16[256,128]{1,0:T(8,128)(2,1)S(1)}, bf16[512,128]{1,0:T(8,128)(2,1)S(1)}, bf16[3,32,128]{2,1,0:T(8,128)(2,1)S(1)}) custom-call(bf16[8448,128]{1,0:T(8,128)(2,1)} %bitcast.4.got_hbm), custom_call_target="tpu_custom_call" | custom-call | tf_op jit(solution)/shard_map/to_grid/pallas_call | solution.py:275
  64.5 3.1 %collective-permute-start = (bf16[512,128]{1,0:T(8,128)(2,1)S(1)}, bf16[512,128]{1,0:T(8,128)(2,1)S(1)}, u32[]{:S(2)}, u32[]{:S(2)}) collective-permute-start(bf16[512,128]{1,0:T(8,128)(2,1)S(1)} %get-tuple-element.10), channel_id=1, source_target_pairs={{0,16},{16,32},{32,48},{48,64},{64,80},{80,96},{96,112},{1,17},{17... | collective-permute-start | bytes 393224 | tf_op jit(solution)/shard_map/ppermute | solution.py:449
  67.7 1.9 %collective-permute-start.1 = (bf16[256,128]{1,0:T(8,128)(2,1)S(1)}, bf16[256,128]{1,0:T(8,128)(2,1)S(1)}, u32[]{:S(2)}, u32[]{:S(2)}) collective-permute-start(bf16[256,128]{1,0:T(8,128)(2,1)S(1)} %get-tuple-element.11), channel_id=1, source_target_pairs={{16,0},{32,16},{48,32},{64,48},{80,64},{96,80},{112,96},{17,1},{33... | collective-permute-start | bytes 196616 | tf_op jit(solution)/shard_map/ppermute | solution.py:450
  69.6 3.6 %collective-permute-done.1 = bf16[256,128]{1,0:T(8,128)(2,1)S(1)} collective-permute-done((bf16[256,128]{1,0:T(8,128)(2,1)S(1)}, bf16[256,128]{1,0:T(8,128)(2,1)S(1)}, u32[]{:S(2)}, u32[]{:S(2)}) %collective-permute-start.1) | collective-permute-done | bytes 65568 | tf_op jit(solution)/shard_map/ppermute | solution.py:450
  73.3 0.0 collective-permute-done
  73.3 0.1 maximum_bitcast_fusion
  73.4 0.9 collective-permute-start.2
  74.3 3.9 %collective-permute-start.3 = (bf16[48,128]{1,0:T(8,128)(2,1)S(1)}, bf16[48,128]{1,0:T(8,128)(2,1)S(1)}, u32[]{:S(2)}, u32[]{:S(2)}) collective-permute-start(bf16[48,128]{1,0:T(8,128)(2,1)S(1)} %get-tuple-element.24.own_hbm), channel_id=1, source_target_pairs={{1,0},{2,1},{3,2},{4,3},{5,4},{6,5},{7,6},{8,7},{9,8},{10,9},{11,1... | collective-permute-start | bytes 36872 | tf_op jit(solution)/shard_map/ppermute | solution.py:462
  78.2 0.8 collective-permute-done.3.east_hbm
  79.1 0.4 collective-permute-done.2.west_hbm
  79.5 0.0 copy-done
  79.5 0.0 copy-done.1
  79.5 13.0 %convolve.1 = bf16[16,128,256]{2,1,0:T(8,128)(2,1)} custom-call(s32[1]{0:T(128)} %bitcast.band_ref, bf16[32,16,16,128]{3,2,1,0:T(8,128)(2,1)} %bitcast.34, bf16[2,16,16,128]{3,2,1,0:T(8,128)(2,1)S(1)} %bitcast.31, bf16[16,16,128]{2,1,0:T(8,128)(2,1)S(1)} %bitcast.32, bf16[48,128]{1,0:T(8,128)(2,1)S(1)} %get-tuple-element.24.own_hbm, ...), custom_call_target="tpu_custom_call" | custom-call | tf_op jit(solution)/shard_map/convolve/pallas_call | solution.py:411
  (7 shorter events, 0.0 us)
Async XLA Ops:
  7.9 42.1 %all-to-all-start = ((bf16[128,33,2,128]{3,2,1,0:T(2,128)(2,1)}), bf16[128,33,2,128]{3,2,1,0:T(2,128)(2,1)}, u32[]{:S(2)}, u32[]{:S(2)}) async-start(bf16[128,33,2,128]{3,2,1,0:T(2,128)(2,1)} %bitcast.33), calls=%async_computation | async-start | bytes 4325376 | tf_op jit(solution)/shard_map/all_to_all | solution.py:445
  19.8 59.6 %copy-start = (bf16[3,3,256,256]{3,2,1,0:T(8,128)(2,1)S(1)}, bf16[3,3,256,256]{3,2,1,0:T(8,128)(2,1)}, u32[]{:S(2)}) copy-start(bf16[3,3,256,256]{3,2,1,0:T(8,128)(2,1)} %param.11) | copy-start | bytes 3538948
  19.9 59.6 %copy-start.1 = (bf16[3,3,128,256]{3,2,1,0:T(8,128)(2,1)S(1)}, bf16[3,3,128,256]{3,2,1,0:T(8,128)(2,1)}, u32[]{:S(2)}) copy-start(bf16[3,3,128,256]{3,2,1,0:T(8,128)(2,1)} %param.10) | copy-start | bytes 1769476
  64.5 8.7 %collective-permute-start = (bf16[512,128]{1,0:T(8,128)(2,1)S(1)}, bf16[512,128]{1,0:T(8,128)(2,1)S(1)}, u32[]{:S(2)}, u32[]{:S(2)}) collective-permute-start(bf16[512,128]{1,0:T(8,128)(2,1)S(1)} %get-tuple-element.10), channel_id=1, source_target_pairs={{0,16},{16,32},{32,48},{48,64},{64,80},{80,96},{96,112},{1,17},{17... | collective-permute-start | bytes 393224 | tf_op jit(solution)/shard_map/ppermute | solution.py:449
  67.7 5.6 %collective-permute-start.1 = (bf16[256,128]{1,0:T(8,128)(2,1)S(1)}, bf16[256,128]{1,0:T(8,128)(2,1)S(1)}, u32[]{:S(2)}, u32[]{:S(2)}) collective-permute-start(bf16[256,128]{1,0:T(8,128)(2,1)S(1)} %get-tuple-element.11), channel_id=1, source_target_pairs={{16,0},{32,16},{48,32},{64,48},{80,64},{96,80},{112,96},{17,1},{33... | collective-permute-start | bytes 196616 | tf_op jit(solution)/shard_map/ppermute | solution.py:450
  73.4 6.1 %collective-permute-start.2 = (bf16[2,48,128]{2,1,0:T(8,128)(2,1)S(1)}, bf16[2,48,128]{2,1,0:T(8,128)(2,1)S(1)}, u32[]{:S(2)}, u32[]{:S(2)}) collective-permute-start(bf16[2,48,128]{2,1,0:T(8,128)(2,1)S(1)} %pad_maximum_fusion), channel_id=1, source_target_pairs={{0,1},{1,2},{2,3},{3,4},{4,5},{5,6},{6,7},{7,8},{8,9},{9,10},{10,1... | collective-permute-start | bytes 73736 | tf_op jit(solution)/shard_map/ppermute | solution.py:461
  74.3 4.8 %collective-permute-start.3 = (bf16[48,128]{1,0:T(8,128)(2,1)S(1)}, bf16[48,128]{1,0:T(8,128)(2,1)S(1)}, u32[]{:S(2)}, u32[]{:S(2)}) collective-permute-start(bf16[48,128]{1,0:T(8,128)(2,1)S(1)} %get-tuple-element.24.own_hbm), channel_id=1, source_target_pairs={{1,0},{2,1},{3,2},{4,3},{5,4},{6,5},{7,6},{8,7},{9,8},{10,9},{11,1... | collective-permute-start | bytes 36872 | tf_op jit(solution)/shard_map/ppermute | solution.py:462

commit v6 on v5

--- a/solution.py
+++ b/solution.py
@@ -18,7 +18,6 @@
 SEND = DEV * BLK
 TRASH = 256
 GROUP = 8
-PART = 64
 FIRST = 11
 SECOND = 8
 COLS = 48
@@ -178,15 +177,14 @@
         same = (index == pltpu.roll(index, d, axis=1)) & (lane % GROUP >= d)
         repeated = repeated | same
     repeated = jnp.where(first & repeated, 1.0, 0.0).astype(BF16)
-    groups = (
-        lax.broadcasted_iota(jnp.int32, (128, 128), 0) // PART
-        == (lax.broadcasted_iota(jnp.int32, (128, 128), 1) - CAP)
-    ).astype(F32).astype(BF16)
+    slot = lax.broadcasted_iota(jnp.int32, (128, 128), 0)
+    kind = lax.broadcasted_iota(jnp.int32, (128, 128), 1) - CAP
+    groups = ((kind == 0) | (slot // GROUP == kind - 8)).astype(F32).astype(BF16)
     flags = jnp.dot(repeated, groups, preferred_element_type=F32)
     flags = (flags + pltpu.roll(flags, DEV // 2, axis=0)).astype(jnp.int32)
     table_v[...] = jnp.where(first, index, flags).T
     to_scalar = []
-    for n, rows in enumerate((pl.ds(CAP, 8), pl.ds(0, CAP))):
+    for n, rows in enumerate((pl.ds(CAP, 16), pl.ds(0, CAP))):
         to_scalar.append(pltpu.make_async_copy(table_v.at[rows], table_s.at[rows], sem.at[n]))
         to_scalar[n].start()
 
@@ -214,36 +212,45 @@
     inverse[...] = 1.0 / jnp.maximum(tallies, 1.0)
 
     to_scalar[0].wait()
-    for p in range(CAP // PART):
-        to_scalar[1 + p].wait()
-
-        def source(s, c):
-            pairs = ((acc, s), (acc2, s + half))
-            clash = table_s.at[CAP + p][s]
-
-            @pl.when(clash == 0)
-            def _():
-                for g in range(p * PART // GROUP, (p + 1) * PART // GROUP):
-                    slots = range(g * GROUP, (g + 1) * GROUP)
-                    index = [[pl.ds(table_s.at[k][t], 1) for k in slots] for _, t in pairs]
-                    sums = [
-                        [a[at, :] + x32[pl.ds(t * BLK + k, 1), :] for at, k in zip(ix, slots)]
-                        for (a, t), ix in zip(pairs, index)
-                    ]
-                    for (a, _), ix, new in zip(pairs, index, sums):
-                        for at, value in zip(ix, new):
-                            a[at, :] = value
-
-            @pl.when(clash != 0)
-            def _():
-                for k in range(p * PART, (p + 1) * PART):
-                    for a, t in pairs:
-                        at = pl.ds(table_s.at[k][t], 1)
-                        a[at, :] = a[at, :] + x32[pl.ds(t * BLK + k, 1), :]
-
-            return c
-
-        lax.fori_loop(0, half, source, 0)
+    to_scalar[1].wait()
+
+    def source(s, c):
+        pairs = ((acc, s), (acc2, s + half))
+
+        def add_group(g):
+            slots = range(g * GROUP, (g + 1) * GROUP)
+            index = [[pl.ds(table_s.at[k][t], 1) for k in slots] for _, t in pairs]
+            sums = [
+                [a[at, :] + x32[pl.ds(t * BLK + k, 1), :] for at, k in zip(ix, slots)]
+                for (a, t), ix in zip(pairs, index)
+            ]
+            for (a, _), ix, new in zip(pairs, index, sums):
+                for at, value in zip(ix, new):
+                    a[at, :] = value
+
+        def add_singly(g):
+            for k in range(g * GROUP, (g + 1) * GROUP):
+                for a, t in pairs:
+                    at = pl.ds(table_s.at[k][t], 1)
+                    a[at, :] = a[at, :] + x32[pl.ds(t * BLK + k, 1), :]
+
+        clash = table_s.at[CAP][s]
+
+        @pl.when(clash == 0)
+        def _():
+            for g in range(CAP // GROUP):
+                add_group(g)
+
+        @pl.when(clash != 0)
+        def _():
+            for g in range(CAP // GROUP):
+                here = table_s.at[CAP + 8 + g][s]
+                pl.when(here == 0)(lambda: add_group(g))
+                pl.when(here != 0)(lambda: add_singly(g))
+
+        return c
+
+    lax.fori_loop(0, half, source, 0)
 
     span = TH // parts
 
@@ -284,7 +291,7 @@
             pltpu.VMEM((TRASH + TH * TW, CH), F32),
             pltpu.VMEM((TRASH + TH * TW, CH), F32),
             pltpu.VMEM((DEV, 128), jnp.int32),
-            pltpu.SMEM((CAP + 8, 128), jnp.int32),
+            pltpu.SMEM((CAP + 16, 128), jnp.int32),
             pltpu.VMEM((DEV // 2, 128), F32),
             pltpu.VMEM((DEV // 2, 128), F32),
             pltpu.VMEM((TW, 128), F32),

time: 92.8 us -> 92.9 us (level)
  no operation moved by 1% of the time
where the time goes in v6:
time: 92.9 us; the launch traced here: 92.6 us
  waiting for transfers between devices  34.9 us (38%)
  Pallas kernels  34.5 us (37%)
  starting transfers between devices  22.2 us (24%)
    all_to_all x1, waiting for transfers between devices, body(): lax.all_to_all(send.reshape(DEV, BLK // 2, 2, CH), ('lat', 'lon'), split_...  30.1 us
    pallas_call x1, Pallas kernels, to_grid(): pl.pallas_call(grid_kernel, out_shape=[jax.ShapeDtypeStruct(s, BF16) for...  14.3 us
    pallas_call x1, Pallas kernels, convolve(): pl.pallas_call(conv_kernel, out_shape=jax.ShapeDtypeStruct((TH // 2, TW /...  13 us
    all_to_all x1, starting transfers between devices, body(): lax.all_to_all(send.reshape(DEV, BLK // 2, 2, CH), ('lat', 'lon'), split_...  11.9 us
    pallas_call x1, Pallas kernels, pack(): pl.pallas_call(pack_kernel, out_shape=jax.ShapeDtypeStruct((SEND, CH), BF...  7.27 us
    ppermute x1, starting transfers between devices, body(): east = lax.ppermute(own, 'lon', [((i + 1) % lon, i) for i in range(lon)])  4.22 us
    ppermute x1, waiting for transfers between devices, body(): south = lax.ppermute(top, 'lat', [(i + 1, i) for i in range(lat - 1)])  3.64 us
    ppermute x1, starting transfers between devices, body(): north = lax.ppermute(bottom, 'lat', [(i, i + 1) for i in range(lat - 1)])  3.47 us
  transfers between devices with their start and end apart: 5, of which 4 were waited for; matrix products, arithmetic and copies ran while one was open for 0% of the time, Pallas kernels for 0%

profile of v6, /device:TPU:1, one launch (start us, length us, event | category | flops | bytes accessed | tf_op | source)
XLA Modules:
  0.0 92.6 jit_solution(14979470675456157887)
XLA Ops:
  0.7 7.3 %pack.1 = bf16[8448,128]{1,0:T(8,128)(2,1)} custom-call(s32[1]{0:T(128)S(6)} %copy.17.count_ref, s32[32,128]{1,0:T(8,128)} %bitcast.35, s32[32,128]{1,0:T(8,128)} %bitcast.36, bf16[4096,128]{1,0:T(8,128)(2,1)} %val_hbm.1), custom_call_target="tpu_custom_call" | custom-call | tf_op jit(solution)/shard_map/pack/pallas_call | solution.py:117
  7.9 11.9 %all-to-all-start = ((bf16[128,33,2,128]{3,2,1,0:T(2,128)(2,1)}), bf16[128,33,2,128]{3,2,1,0:T(2,128)(2,1)}, u32[]{:S(2)}, u32[]{:S(2)}) async-start(bf16[128,33,2,128]{3,2,1,0:T(2,128)(2,1)} %bitcast.33), calls=%async_computation | async-start | bytes 4325376 | tf_op jit(solution)/shard_map/all_to_all | solution.py:452
  19.8 0.0 copy-start
  19.9 0.0 copy-start.1
  19.9 0.1 pad.13.clone
  20.0 30.1 %all-to-all-done = bf16[128,33,2,128]{3,2,1,0:T(2,128)(2,1)} async-done(((bf16[128,33,2,128]{3,2,1,0:T(2,128)(2,1)}), bf16[128,33,2,128]{3,2,1,0:T(2,128)(2,1)}, u32[]{:S(2)}, u32[]{:S(2)}) %all-to-all-start) | async-done | bytes 2162720 | tf_op jit(solution)/shard_map/all_to_all | solution.py:452
  50.0 14.3 %to_grid.1 = (bf16[8192,128]{1,0:T(8,128)(2,1)}, bf16[256,128]{1,0:T(8,128)(2,1)S(1)}, bf16[512,128]{1,0:T(8,128)(2,1)S(1)}, bf16[3,32,128]{2,1,0:T(8,128)(2,1)S(1)}) custom-call(bf16[8448,128]{1,0:T(8,128)(2,1)} %bitcast.4.got_hbm), custom_call_target="tpu_custom_call" | custom-call | tf_op jit(solution)/shard_map/to_grid/pallas_call | solution.py:282
  64.3 3.5 %collective-permute-start = (bf16[512,128]{1,0:T(8,128)(2,1)S(1)}, bf16[512,128]{1,0:T(8,128)(2,1)S(1)}, u32[]{:S(2)}, u32[]{:S(2)}) collective-permute-start(bf16[512,128]{1,0:T(8,128)(2,1)S(1)} %get-tuple-element.10), channel_id=1, source_target_pairs={{0,16},{16,32},{32,48},{48,64},{64,80},{80,96},{96,112},{1,17},{17... | collective-permute-start | bytes 393224 | tf_op jit(solution)/shard_map/ppermute | solution.py:456
  67.8 1.9 %collective-permute-start.1 = (bf16[256,128]{1,0:T(8,128)(2,1)S(1)}, bf16[256,128]{1,0:T(8,128)(2,1)S(1)}, u32[]{:S(2)}, u32[]{:S(2)}) collective-permute-start(bf16[256,128]{1,0:T(8,128)(2,1)S(1)} %get-tuple-element.11), channel_id=1, source_target_pairs={{16,0},{32,16},{48,32},{64,48},{80,64},{96,80},{112,96},{17,1},{33... | collective-permute-start | bytes 196616 | tf_op jit(solution)/shard_map/ppermute | solution.py:457
  69.7 3.6 %collective-permute-done.1 = bf16[256,128]{1,0:T(8,128)(2,1)S(1)} collective-permute-done((bf16[256,128]{1,0:T(8,128)(2,1)S(1)}, bf16[256,128]{1,0:T(8,128)(2,1)S(1)}, u32[]{:S(2)}, u32[]{:S(2)}) %collective-permute-start.1) | collective-permute-done | bytes 65568 | tf_op jit(solution)/shard_map/ppermute | solution.py:457
  73.4 0.0 collective-permute-done
  73.4 0.1 maximum_bitcast_fusion
  73.5 0.6 collective-permute-start.2
  74.1 4.2 %collective-permute-start.3 = (bf16[48,128]{1,0:T(8,128)(2,1)S(1)}, bf16[48,128]{1,0:T(8,128)(2,1)S(1)}, u32[]{:S(2)}, u32[]{:S(2)}) collective-permute-start(bf16[48,128]{1,0:T(8,128)(2,1)S(1)} %get-tuple-element.24.own_hbm), channel_id=1, source_target_pairs={{1,0},{2,1},{3,2},{4,3},{5,4},{6,5},{7,6},{8,7},{9,8},{10,9},{11,1... | collective-permute-start | bytes 36872 | tf_op jit(solution)/shard_map/ppermute | solution.py:469
  78.4 0.8 collective-permute-done.3.east_hbm
  79.2 0.4 collective-permute-done.2.west_hbm
  79.6 0.0 copy-done
  79.6 0.0 copy-done.1
  79.6 13.0 %convolve.1 = bf16[16,128,256]{2,1,0:T(8,128)(2,1)} custom-call(s32[1]{0:T(128)} %bitcast.band_ref, bf16[32,16,16,128]{3,2,1,0:T(8,128)(2,1)} %bitcast.34, bf16[2,16,16,128]{3,2,1,0:T(8,128)(2,1)S(1)} %bitcast.31, bf16[16,16,128]{2,1,0:T(8,128)(2,1)S(1)} %bitcast.32, bf16[48,128]{1,0:T(8,128)(2,1)S(1)} %get-tuple-element.24.own_hbm, ...), custom_call_target="tpu_custom_call" | custom-call | tf_op jit(solution)/shard_map/convolve/pallas_call | solution.py:418
  (7 shorter events, 0.0 us)
Async XLA Ops:
  7.9 42.1 %all-to-all-start = ((bf16[128,33,2,128]{3,2,1,0:T(2,128)(2,1)}), bf16[128,33,2,128]{3,2,1,0:T(2,128)(2,1)}, u32[]{:S(2)}, u32[]{:S(2)}) async-start(bf16[128,33,2,128]{3,2,1,0:T(2,128)(2,1)} %bitcast.33), calls=%async_computation | async-start | bytes 4325376 | tf_op jit(solution)/shard_map/all_to_all | solution.py:452
  19.8 59.7 %copy-start = (bf16[3,3,256,256]{3,2,1,0:T(8,128)(2,1)S(1)}, bf16[3,3,256,256]{3,2,1,0:T(8,128)(2,1)}, u32[]{:S(2)}) copy-start(bf16[3,3,256,256]{3,2,1,0:T(8,128)(2,1)} %param.11) | copy-start | bytes 3538948
  19.9 59.7 %copy-start.1 = (bf16[3,3,128,256]{3,2,1,0:T(8,128)(2,1)S(1)}, bf16[3,3,128,256]{3,2,1,0:T(8,128)(2,1)}, u32[]{:S(2)}) copy-start(bf16[3,3,128,256]{3,2,1,0:T(8,128)(2,1)} %param.10) | copy-start | bytes 1769476
  64.3 9.1 %collective-permute-start = (bf16[512,128]{1,0:T(8,128)(2,1)S(1)}, bf16[512,128]{1,0:T(8,128)(2,1)S(1)}, u32[]{:S(2)}, u32[]{:S(2)}) collective-permute-start(bf16[512,128]{1,0:T(8,128)(2,1)S(1)} %get-tuple-element.10), channel_id=1, source_target_pairs={{0,16},{16,32},{32,48},{48,64},{64,80},{80,96},{96,112},{1,17},{17... | collective-permute-start | bytes 393224 | tf_op jit(solution)/shard_map/ppermute | solution.py:456
  67.8 5.6 %collective-permute-start.1 = (bf16[256,128]{1,0:T(8,128)(2,1)S(1)}, bf16[256,128]{1,0:T(8,128)(2,1)S(1)}, u32[]{:S(2)}, u32[]{:S(2)}) collective-permute-start(bf16[256,128]{1,0:T(8,128)(2,1)S(1)} %get-tuple-element.11), channel_id=1, source_target_pairs={{16,0},{32,16},{48,32},{64,48},{80,64},{96,80},{112,96},{17,1},{33... | collective-permute-start | bytes 196616 | tf_op jit(solution)/shard_map/ppermute | solution.py:457
  73.5 6.1 %collective-permute-start.2 = (bf16[2,48,128]{2,1,0:T(8,128)(2,1)S(1)}, bf16[2,48,128]{2,1,0:T(8,128)(2,1)S(1)}, u32[]{:S(2)}, u32[]{:S(2)}) collective-permute-start(bf16[2,48,128]{2,1,0:T(8,128)(2,1)S(1)} %pad_maximum_fusion), channel_id=1, source_target_pairs={{0,1},{1,2},{2,3},{3,4},{4,5},{5,6},{6,7},{7,8},{8,9},{9,10},{10,1... | collective-permute-start | bytes 73736 | tf_op jit(solution)/shard_map/ppermute | solution.py:468
  74.1 5.1 %collective-permute-start.3 = (bf16[48,128]{1,0:T(8,128)(2,1)S(1)}, bf16[48,128]{1,0:T(8,128)(2,1)S(1)}, u32[]{:S(2)}, u32[]{:S(2)}) collective-permute-start(bf16[48,128]{1,0:T(8,128)(2,1)S(1)} %get-tuple-element.24.own_hbm), channel_id=1, source_target_pairs={{1,0},{2,1},{3,2},{4,3},{5,4},{6,5},{7,6},{8,7},{9,8},{10,9},{11,1... | collective-permute-start | bytes 36872 | tf_op jit(solution)/shard_map/ppermute | solution.py:469

commit v7 on v6

--- a/solution.py
+++ b/solution.py
@@ -192,7 +192,7 @@
     firsth = lax.broadcasted_iota(jnp.int32, (half, 128), 1) < CAP
     rowpair[...] = jnp.where(firsth, cells[:half], swapped[half:])
     colpair[...] = jnp.where(firsth, swapped[:half], cells[half:])
-    batch = 8
+    batch = 16
     col_ids = lax.broadcasted_iota(jnp.int32, (TW, 128), 0).astype(F32)
     row_ids = (lax.broadcasted_iota(jnp.int32, (128, 128), 0) + 1).astype(F32)
 

time: 92.9 us -> 92.3 us (level)
  no operation moved by 1% of the time
where the time goes in v7:
time: 92.3 us; the launch traced here: 92.1 us
  waiting for transfers between devices  34.9 us (38%)
  Pallas kernels  34.3 us (37%)
  starting transfers between devices  21.9 us (24%)
    all_to_all x1, waiting for transfers between devices, body(): lax.all_to_all(send.reshape(DEV, BLK // 2, 2, CH), ('lat', 'lon'), split_...  30.1 us
    pallas_call x1, Pallas kernels, to_grid(): pl.pallas_call(grid_kernel, out_shape=[jax.ShapeDtypeStruct(s, BF16) for...  14.1 us
    pallas_call x1, Pallas kernels, convolve(): pl.pallas_call(conv_kernel, out_shape=jax.ShapeDtypeStruct((TH // 2, TW /...  13 us
    all_to_all x1, starting transfers between devices, body(): lax.all_to_all(send.reshape(DEV, BLK // 2, 2, CH), ('lat', 'lon'), split_...  11.9 us
    pallas_call x1, Pallas kernels, pack(): pl.pallas_call(pack_kernel, out_shape=jax.ShapeDtypeStruct((SEND, CH), BF...  7.27 us
    ppermute x1, starting transfers between devices, body(): east = lax.ppermute(own, 'lon', [((i + 1) % lon, i) for i in range(lon)])  4.34 us
    ppermute x1, waiting for transfers between devices, body(): south = lax.ppermute(top, 'lat', [(i + 1, i) for i in range(lat - 1)])  3.64 us
    ppermute x1, starting transfers between devices, body(): north = lax.ppermute(bottom, 'lat', [(i, i + 1) for i in range(lat - 1)])  3.24 us
  transfers between devices with their start and end apart: 5, of which 4 were waited for; matrix products, arithmetic and copies ran while one was open for 0% of the time, Pallas kernels for 0%

profile of v7, /device:TPU:1, one launch (start us, length us, event | category | flops | bytes accessed | tf_op | source)
XLA Modules:
  0.0 92.1 jit_solution(8990586014396876653)
XLA Ops:
  0.7 7.3 %pack.1 = bf16[8448,128]{1,0:T(8,128)(2,1)} custom-call(s32[1]{0:T(128)S(6)} %copy.17.count_ref, s32[32,128]{1,0:T(8,128)} %bitcast.35, s32[32,128]{1,0:T(8,128)} %bitcast.36, bf16[4096,128]{1,0:T(8,128)(2,1)} %val_hbm.1), custom_call_target="tpu_custom_call" | custom-call | tf_op jit(solution)/shard_map/pack/pallas_call | solution.py:117
  7.9 11.9 %all-to-all-start = ((bf16[128,33,2,128]{3,2,1,0:T(2,128)(2,1)}), bf16[128,33,2,128]{3,2,1,0:T(2,128)(2,1)}, u32[]{:S(2)}, u32[]{:S(2)}) async-start(bf16[128,33,2,128]{3,2,1,0:T(2,128)(2,1)} %bitcast.33), calls=%async_computation | async-start | bytes 4325376 | tf_op jit(solution)/shard_map/all_to_all | solution.py:452
  19.8 0.0 copy-start
  19.9 0.0 copy-start.1
  19.9 0.1 pad.13.clone
  20.0 30.1 %all-to-all-done = bf16[128,33,2,128]{3,2,1,0:T(2,128)(2,1)} async-done(((bf16[128,33,2,128]{3,2,1,0:T(2,128)(2,1)}), bf16[128,33,2,128]{3,2,1,0:T(2,128)(2,1)}, u32[]{:S(2)}, u32[]{:S(2)}) %all-to-all-start) | async-done | bytes 2162720 | tf_op jit(solution)/shard_map/all_to_all | solution.py:452
  50.0 14.1 %to_grid.1 = (bf16[8192,128]{1,0:T(8,128)(2,1)}, bf16[256,128]{1,0:T(8,128)(2,1)S(1)}, bf16[512,128]{1,0:T(8,128)(2,1)S(1)}, bf16[3,32,128]{2,1,0:T(8,128)(2,1)S(1)}) custom-call(bf16[8448,128]{1,0:T(8,128)(2,1)} %bitcast.4.got_hbm), custom_call_target="tpu_custom_call" | custom-call | tf_op jit(solution)/shard_map/to_grid/pallas_call | solution.py:282
  64.1 3.2 %collective-permute-start = (bf16[512,128]{1,0:T(8,128)(2,1)S(1)}, bf16[512,128]{1,0:T(8,128)(2,1)S(1)}, u32[]{:S(2)}, u32[]{:S(2)}) collective-permute-start(bf16[512,128]{1,0:T(8,128)(2,1)S(1)} %get-tuple-element.10), channel_id=1, source_target_pairs={{0,16},{16,32},{32,48},{48,64},{64,80},{80,96},{96,112},{1,17},{17... | collective-permute-start | bytes 393224 | tf_op jit(solution)/shard_map/ppermute | solution.py:456
  67.4 1.9 %collective-permute-start.1 = (bf16[256,128]{1,0:T(8,128)(2,1)S(1)}, bf16[256,128]{1,0:T(8,128)(2,1)S(1)}, u32[]{:S(2)}, u32[]{:S(2)}) collective-permute-start(bf16[256,128]{1,0:T(8,128)(2,1)S(1)} %get-tuple-element.11), channel_id=1, source_target_pairs={{16,0},{32,16},{48,32},{64,48},{80,64},{96,80},{112,96},{17,1},{33... | collective-permute-start | bytes 196616 | tf_op jit(solution)/shard_map/ppermute | solution.py:457
  69.3 3.6 %collective-permute-done.1 = bf16[256,128]{1,0:T(8,128)(2,1)S(1)} collective-permute-done((bf16[256,128]{1,0:T(8,128)(2,1)S(1)}, bf16[256,128]{1,0:T(8,128)(2,1)S(1)}, u32[]{:S(2)}, u32[]{:S(2)}) %collective-permute-start.1) | collective-permute-done | bytes 65568 | tf_op jit(solution)/shard_map/ppermute | solution.py:457
  73.0 0.0 collective-permute-done
  73.0 0.1 maximum_bitcast_fusion
  73.1 0.5 collective-permute-start.2
  73.6 4.3 %collective-permute-start.3 = (bf16[48,128]{1,0:T(8,128)(2,1)S(1)}, bf16[48,128]{1,0:T(8,128)(2,1)S(1)}, u32[]{:S(2)}, u32[]{:S(2)}) collective-permute-start(bf16[48,128]{1,0:T(8,128)(2,1)S(1)} %get-tuple-element.24.own_hbm), channel_id=1, source_target_pairs={{1,0},{2,1},{3,2},{4,3},{5,4},{6,5},{7,6},{8,7},{9,8},{10,9},{11,1... | collective-permute-start | bytes 36872 | tf_op jit(solution)/shard_map/ppermute | solution.py:469
  77.9 0.8 collective-permute-done.3.east_hbm
  78.8 0.4 collective-permute-done.2.west_hbm
  79.2 0.0 copy-done
  79.2 0.0 copy-done.1
  79.2 13.0 %convolve.1 = bf16[16,128,256]{2,1,0:T(8,128)(2,1)} custom-call(s32[1]{0:T(128)} %bitcast.band_ref, bf16[32,16,16,128]{3,2,1,0:T(8,128)(2,1)} %bitcast.34, bf16[2,16,16,128]{3,2,1,0:T(8,128)(2,1)S(1)} %bitcast.31, bf16[16,16,128]{2,1,0:T(8,128)(2,1)S(1)} %bitcast.32, bf16[48,128]{1,0:T(8,128)(2,1)S(1)} %get-tuple-element.24.own_hbm, ...), custom_call_target="tpu_custom_call" | custom-call | tf_op jit(solution)/shard_map/convolve/pallas_call | solution.py:418
  (7 shorter events, 0.0 us)
Async XLA Ops:
  7.9 42.1 %all-to-all-start = ((bf16[128,33,2,128]{3,2,1,0:T(2,128)(2,1)}), bf16[128,33,2,128]{3,2,1,0:T(2,128)(2,1)}, u32[]{:S(2)}, u32[]{:S(2)}) async-start(bf16[128,33,2,128]{3,2,1,0:T(2,128)(2,1)} %bitcast.33), calls=%async_computation | async-start | bytes 4325376 | tf_op jit(solution)/shard_map/all_to_all | solution.py:452
  19.8 59.3 %copy-start = (bf16[3,3,256,256]{3,2,1,0:T(8,128)(2,1)S(1)}, bf16[3,3,256,256]{3,2,1,0:T(8,128)(2,1)}, u32[]{:S(2)}) copy-start(bf16[3,3,256,256]{3,2,1,0:T(8,128)(2,1)} %param.11) | copy-start | bytes 3538948
  19.9 59.3 %copy-start.1 = (bf16[3,3,128,256]{3,2,1,0:T(8,128)(2,1)S(1)}, bf16[3,3,128,256]{3,2,1,0:T(8,128)(2,1)}, u32[]{:S(2)}) copy-start(bf16[3,3,128,256]{3,2,1,0:T(8,128)(2,1)} %param.10) | copy-start | bytes 1769476
  64.1 8.8 %collective-permute-start = (bf16[512,128]{1,0:T(8,128)(2,1)S(1)}, bf16[512,128]{1,0:T(8,128)(2,1)S(1)}, u32[]{:S(2)}, u32[]{:S(2)}) collective-permute-start(bf16[512,128]{1,0:T(8,128)(2,1)S(1)} %get-tuple-element.10), channel_id=1, source_target_pairs={{0,16},{16,32},{32,48},{48,64},{64,80},{80,96},{96,112},{1,17},{17... | collective-permute-start | bytes 393224 | tf_op jit(solution)/shard_map/ppermute | solution.py:456
  67.4 5.6 %collective-permute-start.1 = (bf16[256,128]{1,0:T(8,128)(2,1)S(1)}, bf16[256,128]{1,0:T(8,128)(2,1)S(1)}, u32[]{:S(2)}, u32[]{:S(2)}) collective-permute-start(bf16[256,128]{1,0:T(8,128)(2,1)S(1)} %get-tuple-element.11), channel_id=1, source_target_pairs={{16,0},{32,16},{48,32},{64,48},{80,64},{96,80},{112,96},{17,1},{33... | collective-permute-start | bytes 196616 | tf_op jit(solution)/shard_map/ppermute | solution.py:457
  73.1 6.1 %collective-permute-start.2 = (bf16[2,48,128]{2,1,0:T(8,128)(2,1)S(1)}, bf16[2,48,128]{2,1,0:T(8,128)(2,1)S(1)}, u32[]{:S(2)}, u32[]{:S(2)}) collective-permute-start(bf16[2,48,128]{2,1,0:T(8,128)(2,1)S(1)} %pad_maximum_fusion), channel_id=1, source_target_pairs={{0,1},{1,2},{2,3},{3,4},{4,5},{5,6},{6,7},{7,8},{8,9},{9,10},{10,1... | collective-permute-start | bytes 73736 | tf_op jit(solution)/shard_map/ppermute | solution.py:468
  73.6 5.2 %collective-permute-start.3 = (bf16[48,128]{1,0:T(8,128)(2,1)S(1)}, bf16[48,128]{1,0:T(8,128)(2,1)S(1)}, u32[]{:S(2)}, u32[]{:S(2)}) collective-permute-start(bf16[48,128]{1,0:T(8,128)(2,1)S(1)} %get-tuple-element.24.own_hbm), channel_id=1, source_target_pairs={{1,0},{2,1},{3,2},{4,3},{5,4},{6,5},{7,6},{8,7},{9,8},{10,9},{11,1... | collective-permute-start | bytes 36872 | tf_op jit(solution)/shard_map/ppermute | solution.py:469

commit v8 on v7

--- a/solution.py
+++ b/solution.py
@@ -192,7 +192,7 @@
     firsth = lax.broadcasted_iota(jnp.int32, (half, 128), 1) < CAP
     rowpair[...] = jnp.where(firsth, cells[:half], swapped[half:])
     colpair[...] = jnp.where(firsth, swapped[:half], cells[half:])
-    batch = 16
+    batch = 32
     col_ids = lax.broadcasted_iota(jnp.int32, (TW, 128), 0).astype(F32)
     row_ids = (lax.broadcasted_iota(jnp.int32, (128, 128), 0) + 1).astype(F32)
 

time: 92.3 us -> 92.1 us (level)
  no operation moved by 1% of the time
where the time goes in v8:
time: 92.1 us; the launch traced here: 91.6 us
  waiting for transfers between devices  34.9 us (38%)
  Pallas kernels  33.5 us (36%)
  starting transfers between devices  22.1 us (24%)
    all_to_all x1, waiting for transfers between devices, body(): lax.all_to_all(send.reshape(DEV, BLK // 2, 2, CH), ('lat', 'lon'), split_...  30.1 us
    pallas_call x1, Pallas kernels, to_grid(): pl.pallas_call(grid_kernel, out_shape=[jax.ShapeDtypeStruct(s, BF16) for...  13.3 us
    pallas_call x1, Pallas kernels, convolve(): pl.pallas_call(conv_kernel, out_shape=jax.ShapeDtypeStruct((TH // 2, TW /...  13 us
    all_to_all x1, starting transfers between devices, body(): lax.all_to_all(send.reshape(DEV, BLK // 2, 2, CH), ('lat', 'lon'), split_...  11.9 us
    pallas_call x1, Pallas kernels, pack(): pl.pallas_call(pack_kernel, out_shape=jax.ShapeDtypeStruct((SEND, CH), BF...  7.27 us
    ppermute x1, starting transfers between devices, body(): east = lax.ppermute(own, 'lon', [((i + 1) % lon, i) for i in range(lon)])  4.22 us
    ppermute x1, waiting for transfers between devices, body(): south = lax.ppermute(top, 'lat', [(i + 1, i) for i in range(lat - 1)])  3.64 us
    ppermute x1, starting transfers between devices, body(): north = lax.ppermute(bottom, 'lat', [(i, i + 1) for i in range(lat - 1)])  3.47 us
  transfers between devices with their start and end apart: 5, of which 4 were waited for; matrix products, arithmetic and copies ran while one was open for 0% of the time, Pallas kernels for 0%

profile of v8, /device:TPU:1, one launch (start us, length us, event | category | flops | bytes accessed | tf_op | source)
XLA Modules:
  0.0 91.6 jit_solution(6498975812211107803)
XLA Ops:
  0.7 7.3 %pack.1 = bf16[8448,128]{1,0:T(8,128)(2,1)} custom-call(s32[1]{0:T(128)S(6)} %copy.17.count_ref, s32[32,128]{1,0:T(8,128)} %bitcast.35, s32[32,128]{1,0:T(8,128)} %bitcast.36, bf16[4096,128]{1,0:T(8,128)(2,1)} %val_hbm.1), custom_call_target="tpu_custom_call" | custom-call | tf_op jit(solution)/shard_map/pack/pallas_call | solution.py:117
  7.9 11.9 %all-to-all-start = ((bf16[128,33,2,128]{3,2,1,0:T(2,128)(2,1)}), bf16[128,33,2,128]{3,2,1,0:T(2,128)(2,1)}, u32[]{:S(2)}, u32[]{:S(2)}) async-start(bf16[128,33,2,128]{3,2,1,0:T(2,128)(2,1)} %bitcast.33), calls=%async_computation | async-start | bytes 4325376 | tf_op jit(solution)/shard_map/all_to_all | solution.py:452
  19.8 0.0 copy-start
  19.9 0.0 copy-start.1
  19.9 0.1 pad.13.clone
  20.0 30.1 %all-to-all-done = bf16[128,33,2,128]{3,2,1,0:T(2,128)(2,1)} async-done(((bf16[128,33,2,128]{3,2,1,0:T(2,128)(2,1)}), bf16[128,33,2,128]{3,2,1,0:T(2,128)(2,1)}, u32[]{:S(2)}, u32[]{:S(2)}) %all-to-all-start) | async-done | bytes 2162720 | tf_op jit(solution)/shard_map/all_to_all | solution.py:452
  50.0 13.3 %to_grid.1 = (bf16[8192,128]{1,0:T(8,128)(2,1)}, bf16[256,128]{1,0:T(8,128)(2,1)S(1)}, bf16[512,128]{1,0:T(8,128)(2,1)S(1)}, bf16[3,32,128]{2,1,0:T(8,128)(2,1)S(1)}) custom-call(bf16[8448,128]{1,0:T(8,128)(2,1)} %bitcast.4.got_hbm), custom_call_target="tpu_custom_call" | custom-call | tf_op jit(solution)/shard_map/to_grid/pallas_call | solution.py:282
  63.3 3.5 %collective-permute-start = (bf16[512,128]{1,0:T(8,128)(2,1)S(1)}, bf16[512,128]{1,0:T(8,128)(2,1)S(1)}, u32[]{:S(2)}, u32[]{:S(2)}) collective-permute-start(bf16[512,128]{1,0:T(8,128)(2,1)S(1)} %get-tuple-element.10), channel_id=1, source_target_pairs={{0,16},{16,32},{32,48},{48,64},{64,80},{80,96},{96,112},{1,17},{17... | collective-permute-start | bytes 393224 | tf_op jit(solution)/shard_map/ppermute | solution.py:456
  66.8 1.9 %collective-permute-start.1 = (bf16[256,128]{1,0:T(8,128)(2,1)S(1)}, bf16[256,128]{1,0:T(8,128)(2,1)S(1)}, u32[]{:S(2)}, u32[]{:S(2)}) collective-permute-start(bf16[256,128]{1,0:T(8,128)(2,1)S(1)} %get-tuple-element.11), channel_id=1, source_target_pairs={{16,0},{32,16},{48,32},{64,48},{80,64},{96,80},{112,96},{17,1},{33... | collective-permute-start | bytes 196616 | tf_op jit(solution)/shard_map/ppermute | solution.py:457
  68.7 3.6 %collective-permute-done.1 = bf16[256,128]{1,0:T(8,128)(2,1)S(1)} collective-permute-done((bf16[256,128]{1,0:T(8,128)(2,1)S(1)}, bf16[256,128]{1,0:T(8,128)(2,1)S(1)}, u32[]{:S(2)}, u32[]{:S(2)}) %collective-permute-start.1) | collective-permute-done | bytes 65568 | tf_op jit(solution)/shard_map/ppermute | solution.py:457
  72.4 0.0 collective-permute-done
  72.4 0.1 maximum_bitcast_fusion
  72.5 0.6 collective-permute-start.2
  73.1 4.2 %collective-permute-start.3 = (bf16[48,128]{1,0:T(8,128)(2,1)S(1)}, bf16[48,128]{1,0:T(8,128)(2,1)S(1)}, u32[]{:S(2)}, u32[]{:S(2)}) collective-permute-start(bf16[48,128]{1,0:T(8,128)(2,1)S(1)} %get-tuple-element.24.own_hbm), channel_id=1, source_target_pairs={{1,0},{2,1},{3,2},{4,3},{5,4},{6,5},{7,6},{8,7},{9,8},{10,9},{11,1... | collective-permute-start | bytes 36872 | tf_op jit(solution)/shard_map/ppermute | solution.py:469
  77.3 0.8 collective-permute-done.3.east_hbm
  78.2 0.4 collective-permute-done.2.west_hbm
  78.6 0.0 copy-done
  78.6 0.0 copy-done.1
  78.6 13.0 %convolve.1 = bf16[16,128,256]{2,1,0:T(8,128)(2,1)} custom-call(s32[1]{0:T(128)} %bitcast.band_ref, bf16[32,16,16,128]{3,2,1,0:T(8,128)(2,1)} %bitcast.34, bf16[2,16,16,128]{3,2,1,0:T(8,128)(2,1)S(1)} %bitcast.31, bf16[16,16,128]{2,1,0:T(8,128)(2,1)S(1)} %bitcast.32, bf16[48,128]{1,0:T(8,128)(2,1)S(1)} %get-tuple-element.24.own_hbm, ...), custom_call_target="tpu_custom_call" | custom-call | tf_op jit(solution)/shard_map/convolve/pallas_call | solution.py:418
  (7 shorter events, 0.0 us)
Async XLA Ops:
  7.9 42.1 %all-to-all-start = ((bf16[128,33,2,128]{3,2,1,0:T(2,128)(2,1)}), bf16[128,33,2,128]{3,2,1,0:T(2,128)(2,1)}, u32[]{:S(2)}, u32[]{:S(2)}) async-start(bf16[128,33,2,128]{3,2,1,0:T(2,128)(2,1)} %bitcast.33), calls=%async_computation | async-start | bytes 4325376 | tf_op jit(solution)/shard_map/all_to_all | solution.py:452
  19.8 58.7 %copy-start = (bf16[3,3,256,256]{3,2,1,0:T(8,128)(2,1)S(1)}, bf16[3,3,256,256]{3,2,1,0:T(8,128)(2,1)}, u32[]{:S(2)}) copy-start(bf16[3,3,256,256]{3,2,1,0:T(8,128)(2,1)} %param.11) | copy-start | bytes 3538948
  19.9 58.7 %copy-start.1 = (bf16[3,3,128,256]{3,2,1,0:T(8,128)(2,1)S(1)}, bf16[3,3,128,256]{3,2,1,0:T(8,128)(2,1)}, u32[]{:S(2)}) copy-start(bf16[3,3,128,256]{3,2,1,0:T(8,128)(2,1)} %param.10) | copy-start | bytes 1769476
  63.3 9.1 %collective-permute-start = (bf16[512,128]{1,0:T(8,128)(2,1)S(1)}, bf16[512,128]{1,0:T(8,128)(2,1)S(1)}, u32[]{:S(2)}, u32[]{:S(2)}) collective-permute-start(bf16[512,128]{1,0:T(8,128)(2,1)S(1)} %get-tuple-element.10), channel_id=1, source_target_pairs={{0,16},{16,32},{32,48},{48,64},{64,80},{80,96},{96,112},{1,17},{17... | collective-permute-start | bytes 393224 | tf_op jit(solution)/shard_map/ppermute | solution.py:456
  66.8 5.6 %collective-permute-start.1 = (bf16[256,128]{1,0:T(8,128)(2,1)S(1)}, bf16[256,128]{1,0:T(8,128)(2,1)S(1)}, u32[]{:S(2)}, u32[]{:S(2)}) collective-permute-start(bf16[256,128]{1,0:T(8,128)(2,1)S(1)} %get-tuple-element.11), channel_id=1, source_target_pairs={{16,0},{32,16},{48,32},{64,48},{80,64},{96,80},{112,96},{17,1},{33... | collective-permute-start | bytes 196616 | tf_op jit(solution)/shard_map/ppermute | solution.py:457
  72.5 6.1 %collective-permute-start.2 = (bf16[2,48,128]{2,1,0:T(8,128)(2,1)S(1)}, bf16[2,48,128]{2,1,0:T(8,128)(2,1)S(1)}, u32[]{:S(2)}, u32[]{:S(2)}) collective-permute-start(bf16[2,48,128]{2,1,0:T(8,128)(2,1)S(1)} %pad_maximum_fusion), channel_id=1, source_target_pairs={{0,1},{1,2},{2,3},{3,4},{4,5},{5,6},{6,7},{7,8},{8,9},{9,10},{10,1... | collective-permute-start | bytes 73736 | tf_op jit(solution)/shard_map/ppermute | solution.py:468
  73.1 5.1 %collective-permute-start.3 = (bf16[48,128]{1,0:T(8,128)(2,1)S(1)}, bf16[48,128]{1,0:T(8,128)(2,1)S(1)}, u32[]{:S(2)}, u32[]{:S(2)}) collective-permute-start(bf16[48,128]{1,0:T(8,128)(2,1)S(1)} %get-tuple-element.24.own_hbm), channel_id=1, source_target_pairs={{1,0},{2,1},{3,2},{4,3},{5,4},{6,5},{7,6},{8,7},{9,8},{10,9},{11,1... | collective-permute-start | bytes 36872 | tf_op jit(solution)/shard_map/ppermute | solution.py:469
